TPU v7x, 32 devices: a whole 2x2x4 slice. The times are simulated.
32 devices in a mesh: fsdp: 8 (over y, x, core), sp: 4 (over z).
Axes of the slice: x: 2, y: 2, z: 4, core: 2. Of those that a mesh axis runs over, the one named last changes fastest.
Arguments:
- tokens: bfloat16 [12288, 1536], P(('fsdp', 'sp')), may hold values from -6 to 6
- cotangent: bfloat16 [12288, 1536], P(('fsdp', 'sp')), may hold values from -6 to 6
- seq_lengths: int32 [8], P('fsdp'), may hold values from 1024 to 1536, as said below
- block_order: int32 [8, 8], P('fsdp'), may hold values from 0 to 7, as said below
- w_query: bfloat16 [1536, 1536], P('fsdp'), may hold values from -0.15625 to 0.15625
- w_key: bfloat16 [1536, 256], P('fsdp'), may hold values from -0.15625 to 0.15625
- w_value: bfloat16 [1536, 256], P('fsdp'), may hold values from -0.15625 to 0.15625
- b_query: bfloat16 [1536], P('fsdp'), may hold values from -3 to 3
- b_key: bfloat16 [256], P('fsdp'), may hold values from -3 to 3
- b_value: bfloat16 [256], P('fsdp'), may hold values from -3 to 3
- w_output: bfloat16 [1536, 1536], P('fsdp'), may hold values from -1.25 to 1.25
- gain_attn: bfloat16 [1536], P('fsdp'), may hold values from 0.5 to 1.5
- gain_mlp: bfloat16 [1536], P('fsdp'), may hold values from 0.5 to 1.5
- w_gate: bfloat16 [1536, 8960], P('fsdp'), may hold values from -0.15625 to 0.15625
- w_up: bfloat16 [1536, 8960], P('fsdp'), may hold values from -0.15625 to 0.15625
- w_down: bfloat16 [8960, 1536], P('fsdp'), may hold values from -0.0625 to 0.0625
Outputs:
- layer_out: bfloat16 [12288, 1536], P(('fsdp', 'sp'))
- input_grad: float32 [12288, 1536], P(('fsdp', 'sp'))
- grad_w_query: float32 [1536, 1536], P('fsdp')
- grad_w_key: float32 [1536, 256], P('fsdp')
- grad_w_value: float32 [1536, 256], P('fsdp')
- grad_b_query: float32 [1536], P('fsdp')
- grad_b_key: float32 [256], P('fsdp')
- grad_b_value: float32 [256], P('fsdp')
- grad_w_output: float32 [1536, 1536], P('fsdp')
- grad_gain_attn: float32 [1536], P('fsdp')
- grad_gain_mlp: float32 [1536], P('fsdp')
- grad_w_gate: float32 [1536, 8960], P('fsdp')
- grad_w_up: float32 [1536, 8960], P('fsdp')
- grad_w_down: float32 [8960, 1536], P('fsdp')
- root_means: float32 [3], replicated
Inputs may be any that keep to these rules, and one draw needn't show every extreme that they name: Each group's sequence fills the first seq_lengths[f] places of its packed stream; the rest is padding. Some group is full and some group has exactly 1024. `block_order`: each row is a permutation of the group's 8 stream blocks; entries 2s and 2s + 1 are b and 7 - b for some b.
All inputs are finite; a program needn't handle non-finite values.
Results may differ from a plain program's by a relative error of at most 0.023.
Values may be sent and summed in bfloat16 or wider, within the bound.
No kernel may reach another device: no remote copies, remote signals or barrier semaphores. Data moves between devices by JAX's collectives and lax.ppermute only.
A program may use at most 576 MiB of HBM per device.

v0:
```python
import jax
import jax.numpy as jnp
from jax import lax
from jax.sharding import PartitionSpec as P

H = 12
KVH = 2
HD = 128


EPS = 1e-06
THETA = 1000000.0


def rotary_tables(positions):
    half_width = HD // 2
    inverse = THETA ** (-(jnp.arange(half_width, dtype=jnp.float32) * 2.0) / HD)
    angles = positions.astype(jnp.float32)[:, None] * inverse[None, :]
    angles = jnp.concatenate([angles, angles], axis=-1)
    return (jnp.cos(angles), jnp.sin(angles))


def rotate(values, cosine, sine):
    half_width = values.shape[-1] // 2
    turned = jnp.concatenate([-values[..., half_width:], values[..., :half_width]], axis=-1)
    return values * cosine[:, None, :] + turned * sine[:, None, :]


def unrotate(grads_in, cosine, sine):
    half_width = grads_in.shape[-1] // 2
    scaled = grads_in * sine[:, None, :]
    turned = jnp.concatenate([scaled[..., half_width:], -scaled[..., :half_width]], axis=-1)
    return grads_in * cosine[:, None, :] + turned


def stream_positions(order_row, first_row, row_count, block_size):
    row_ids = first_row + jnp.arange(row_count, dtype=jnp.int32)
    which_block = row_ids // block_size
    matches = jnp.arange(order_row.shape[0], dtype=jnp.int32)[None, :] == which_block[:, None]
    block_start = jnp.sum(jnp.where(matches, order_row[None, :], 0), axis=1)
    return block_start * block_size + row_ids % block_size


def norm_backward(normed_grad, unit_rows, gain_rows, scale_rows):
    gain_grad = jnp.sum(normed_grad * unit_rows, axis=0)
    scaled = normed_grad * gain_rows
    inner = jnp.mean(scaled * unit_rows, axis=-1, keepdims=True)
    return (gain_grad, scale_rows * (scaled - unit_rows * inner))


def contract_last(left, right):
    return lax.dot_general(
        left, right, (((1,), (1,)), ((), ())), preferred_element_type=jnp.float32
    )


def contract_first(left, right):
    return lax.dot_general(
        left, right, (((0,), (0,)), ((), ())), preferred_element_type=jnp.float32
    )


def attend_forward(queries, keys_values, positions):
    count_all = queries.shape[0]
    block_rows = min(512, count_all)
    keys_part = keys_values[:, :HD]
    values_part = keys_values[:, HD:]
    scaling = HD ** (-0.5)

    def one_block(number):
        start_row = number * block_rows
        block_q = lax.dynamic_slice_in_dim(queries, start_row, block_rows, 0)
        block_pos = lax.dynamic_slice_in_dim(positions, start_row, block_rows, 0)
        scores = (
            jnp.einsum("qhd,kd->hqk", block_q, keys_part, preferred_element_type=jnp.float32)
            * scaling
        )
        allowed = positions[None, None, :] <= block_pos[None, :, None]
        scores = jnp.where(allowed, scores, -1e30)
        row_peak = jnp.max(scores, axis=-1, keepdims=True)
        weights_exp = jnp.exp(scores - row_peak)
        row_total = jnp.sum(weights_exp, axis=-1, keepdims=True)
        probabilities = (weights_exp / row_total).astype(jnp.bfloat16)
        output = jnp.einsum(
            "hqk,kd->qhd", probabilities, values_part, preferred_element_type=jnp.float32
        )
        return (output, (row_peak + jnp.log(row_total))[..., 0])

    outputs, logsums = lax.map(one_block, jnp.arange(count_all // block_rows))
    return (outputs.reshape(count_all, -1), logsums)


def attend_backward(queries, keys_values, positions, logsums, out_grads):
    count_all = queries.shape[0]
    block_rows = min(512, count_all)
    keys_part = keys_values[:, :HD]
    values_part = keys_values[:, HD:]
    scaling = HD ** (-0.5)

    def one_block(carried, number):
        start_row = number * block_rows
        block_q = lax.dynamic_slice_in_dim(queries, start_row, block_rows, 0)
        block_pos = lax.dynamic_slice_in_dim(positions, start_row, block_rows, 0)
        block_grad = lax.dynamic_slice_in_dim(out_grads, start_row, block_rows, 0)
        block_sum = logsums[number]
        scores = (
            jnp.einsum("qhd,kd->hqk", block_q, keys_part, preferred_element_type=jnp.float32)
            * scaling
        )
        allowed = positions[None, None, :] <= block_pos[None, :, None]
        scores = jnp.where(allowed, scores, -1e30)
        probabilities = jnp.exp(scores - block_sum[..., None])
        prob_grad = jnp.einsum(
            "qhd,kd->hqk", block_grad, values_part, preferred_element_type=jnp.float32
        )
        weighted = jnp.sum(probabilities * prob_grad, axis=-1, keepdims=True)
        score_grad = (probabilities * (prob_grad - weighted)).astype(jnp.bfloat16)
        query_grad = (
            jnp.einsum("hqk,kd->qhd", score_grad, keys_part, preferred_element_type=jnp.float32)
            * scaling
        )
        key_grad = (
            carried[0]
            + jnp.einsum("hqk,qhd->kd", score_grad, block_q, preferred_element_type=jnp.float32)
            * scaling
        )
        value_grad = carried[1] + jnp.einsum(
            "hqk,qhd->kd",
            probabilities.astype(jnp.bfloat16),
            block_grad,
            preferred_element_type=jnp.float32,
        )
        return ((key_grad, value_grad), query_grad)

    zero_grads = jnp.zeros((count_all, HD), jnp.float32)
    (key_grad, value_grad), query_grads = lax.scan(
        one_block, (zero_grads, zero_grads), jnp.arange(count_all // block_rows)
    )
    return (query_grads.reshape(count_all, -1), jnp.concatenate([key_grad, value_grad], axis=-1))


def per_device(
    tokens,
    cotangent,
    seq_lengths,
    block_order,
    w_query,
    w_key,
    w_value,
    b_query,
    b_key,
    b_value,
    w_output,
    gain_attn,
    gain_mlp,
    w_gate,
    w_up,
    w_down,
):
    local_rows = tokens.shape[0]
    groups_sp = lax.axis_size("sp")
    device_sp = lax.axis_index("sp")
    fsdp_count = lax.axis_size("fsdp")
    fsdp_index = lax.axis_index("fsdp")
    group_rows = local_rows * groups_sp
    block_rows = local_rows // 2
    heads_local = H // groups_sp
    query_width = H * HD
    key_width = KVH * HD
    full_q, full_k, full_v, full_o, bias_q, bias_k, bias_v, norm_one, norm_two = (
        lax.all_gather(w_query, "fsdp", axis=0, tiled=True),
        lax.all_gather(w_key, "fsdp", axis=0, tiled=True),
        lax.all_gather(w_value, "fsdp", axis=0, tiled=True),
        lax.all_gather(w_output, "fsdp", axis=0, tiled=True),
        lax.all_gather(b_query, "fsdp", axis=0, tiled=True),
        lax.all_gather(b_key, "fsdp", axis=0, tiled=True),
        lax.all_gather(b_value, "fsdp", axis=0, tiled=True),
        lax.all_gather(gain_attn, "fsdp", axis=0, tiled=True),
        lax.all_gather(gain_mlp, "fsdp", axis=0, tiled=True),
    )
    full_gate, full_up, full_down = (
        lax.all_gather(w_gate, "fsdp", axis=0, tiled=True),
        lax.all_gather(w_up, "fsdp", axis=0, tiled=True),
        lax.all_gather(w_down, "fsdp", axis=0, tiled=True),
    )
    order_row = block_order[0]
    local_pos = stream_positions(order_row, device_sp * local_rows, local_rows, block_rows)
    group_pos = stream_positions(order_row, 0, group_rows, block_rows)
    valid_rows = (local_pos < seq_lengths[0]).astype(jnp.float32)[:, None]
    inputs = tokens.astype(jnp.float32)
    gain_one = norm_one.astype(jnp.float32)
    gain_two = norm_two.astype(jnp.float32)
    scale_one = lax.rsqrt(jnp.mean(inputs * inputs, axis=-1, keepdims=True) + EPS)
    unit_one = inputs * scale_one
    normed_one = (unit_one * gain_one).astype(jnp.bfloat16)
    query_lin = jnp.dot(normed_one, full_q, preferred_element_type=jnp.float32) + bias_q.astype(
        jnp.float32
    )
    key_lin = jnp.dot(normed_one, full_k, preferred_element_type=jnp.float32) + bias_k.astype(
        jnp.float32
    )
    value_lin = jnp.dot(normed_one, full_v, preferred_element_type=jnp.float32) + bias_v.astype(
        jnp.float32
    )
    cosine, sine = rotary_tables(local_pos)
    query_rot = rotate(query_lin.reshape(local_rows, H, HD), cosine, sine).astype(jnp.bfloat16)
    key_rot = rotate(key_lin.reshape(local_rows, KVH, HD), cosine, sine).astype(jnp.bfloat16)
    value_low = value_lin.reshape(local_rows, KVH, HD).astype(jnp.bfloat16)
    owners = [target * KVH // groups_sp for target in range(groups_sp)]
    pair_send = jnp.concatenate([key_rot[:, owners, :], value_low[:, owners, :]], axis=-1)
    query_send = query_rot.reshape(local_rows, groups_sp, heads_local * HD)
    query_heads, pair_heads = (
        lax.all_to_all(query_send, "sp", split_axis=1, concat_axis=0, tiled=True),
        lax.all_to_all(pair_send, "sp", split_axis=1, concat_axis=0, tiled=True),
    )
    query_heads = query_heads.reshape(group_rows, heads_local, HD)
    pair_heads = pair_heads.reshape(group_rows, 2 * HD)
    attended, logsums = attend_forward(query_heads, pair_heads, group_pos)
    mixed_heads = attended.astype(jnp.bfloat16).reshape(group_rows, 1, heads_local * HD)
    mixed = lax.all_to_all(mixed_heads, "sp", split_axis=0, concat_axis=1, tiled=True).reshape(
        local_rows, query_width
    )
    attn_branch = jnp.dot(mixed, full_o, preferred_element_type=jnp.float32)
    hidden_in = inputs + valid_rows * attn_branch
    scale_two = lax.rsqrt(jnp.mean(hidden_in * hidden_in, axis=-1, keepdims=True) + EPS)
    unit_two = hidden_in * scale_two
    normed_two = (unit_two * gain_two).astype(jnp.bfloat16)
    gate_lin = jnp.dot(normed_two, full_gate, preferred_element_type=jnp.float32)
    up_lin = jnp.dot(normed_two, full_up, preferred_element_type=jnp.float32)
    sigma = jax.nn.sigmoid(gate_lin)
    activated = gate_lin * sigma
    hidden = (activated * up_lin).astype(jnp.bfloat16)
    mlp_branch = jnp.dot(hidden, full_down, preferred_element_type=jnp.float32)
    result = hidden_in + valid_rows * mlp_branch
    upstream = cotangent.astype(jnp.float32)
    mlp_grad = (valid_rows * upstream).astype(jnp.bfloat16)
    hidden_grad = contract_last(mlp_grad, lax.all_gather(w_down, "fsdp", axis=0, tiled=True))
    gate_grad = (hidden_grad * up_lin * (sigma * (1.0 + gate_lin * (1.0 - sigma)))).astype(
        jnp.bfloat16
    )
    up_grad = (hidden_grad * activated).astype(jnp.bfloat16)
    pieces = lax.all_gather((w_gate, w_up), "fsdp", axis=0, tiled=True)
    normed_two_grad = contract_last(gate_grad, pieces[0]) + contract_last(up_grad, pieces[1])
    gain_two_grad, norm_two_back = norm_backward(normed_two_grad, unit_two, gain_two, scale_two)
    hidden_in_grad = upstream + norm_two_back
    attn_grad = (valid_rows * hidden_in_grad).astype(jnp.bfloat16)
    mixed_grad = contract_last(attn_grad, full_o).astype(jnp.bfloat16)
    grad_send = mixed_grad.reshape(local_rows, groups_sp, heads_local * HD)
    grad_heads = lax.all_to_all(grad_send, "sp", split_axis=1, concat_axis=0, tiled=True).reshape(
        group_rows, heads_local, HD
    )
    query_grad, pair_grad = attend_backward(query_heads, pair_heads, group_pos, logsums, grad_heads)
    query_back, pair_back = (
        lax.all_to_all(
            query_grad.reshape(group_rows, 1, heads_local * HD).astype(jnp.bfloat16),
            "sp",
            split_axis=0,
            concat_axis=1,
            tiled=True,
        ).astype(jnp.float32),
        lax.all_to_all(
            pair_grad.reshape(group_rows, 1, 2 * HD).astype(jnp.bfloat16),
            "sp",
            split_axis=0,
            concat_axis=1,
            tiled=True,
        ).astype(jnp.float32),
    )
    query_back = query_back.reshape(local_rows, H, HD)
    pair_total = jnp.sum(pair_back.reshape(local_rows, KVH, groups_sp // KVH, 2 * HD), axis=2)
    query_lin_grad = (
        unrotate(query_back, cosine, sine).reshape(local_rows, query_width).astype(jnp.bfloat16)
    )
    key_lin_grad = (
        unrotate(pair_total[..., :HD], cosine, sine)
        .reshape(local_rows, key_width)
        .astype(jnp.bfloat16)
    )
    value_lin_grad = pair_total[..., HD:].reshape(local_rows, key_width).astype(jnp.bfloat16)
    normed_one_grad = (
        contract_last(query_lin_grad, full_q)
        + contract_last(key_lin_grad, full_k)
        + contract_last(value_lin_grad, full_v)
    )
    gain_one_grad, norm_one_back = norm_backward(normed_one_grad, unit_one, gain_one, scale_one)
    input_grad = hidden_in_grad + norm_one_back
    projection_grads = jnp.concatenate([query_lin_grad, key_lin_grad, value_lin_grad], axis=1)
    attn_term = jnp.concatenate(
        [contract_first(normed_one, projection_grads), contract_first(mixed, attn_grad)], axis=1
    )
    attn_share = lax.psum_scatter(attn_term, ("fsdp", "sp"), scatter_dimension=0, tiled=True)
    gate_up_term = contract_first(normed_two, jnp.concatenate([gate_grad, up_grad], axis=1))
    gate_up_share = lax.psum_scatter(gate_up_term, ("fsdp", "sp"), scatter_dimension=0, tiled=True)
    down_term = contract_first(hidden, mlp_grad)
    down_share = lax.psum_scatter(down_term, ("fsdp", "sp"), scatter_dimension=0, tiled=True)
    attn_full, gate_up_full, down_full = (
        lax.all_gather(attn_share.astype(jnp.bfloat16), "sp", axis=0, tiled=True).astype(
            attn_share.dtype
        ),
        lax.all_gather(gate_up_share.astype(jnp.bfloat16), "sp", axis=0, tiled=True).astype(
            gate_up_share.dtype
        ),
        lax.all_gather(down_share.astype(jnp.bfloat16), "sp", axis=0, tiled=True).astype(
            down_share.dtype
        ),
    )
    stat_parts = jnp.stack(
        [
            jnp.sum(valid_rows * result * result),
            jnp.sum(valid_rows * attn_branch * attn_branch),
            jnp.sum(valid_rows * mlp_branch * mlp_branch),
            jnp.sum(valid_rows),
        ]
    )
    summed = lax.psum(
        (
            jnp.sum(query_lin_grad.astype(jnp.float32), axis=0),
            jnp.sum(key_lin_grad.astype(jnp.float32), axis=0),
            jnp.sum(value_lin_grad.astype(jnp.float32), axis=0),
            gain_one_grad,
            gain_two_grad,
            stat_parts,
        ),
        ("fsdp", "sp"),
    )

    def own_piece(vector):
        width_piece = vector.shape[0] // fsdp_count
        return lax.dynamic_slice_in_dim(vector, fsdp_index * width_piece, width_piece, 0)

    totals = summed[5]
    root_means = jnp.sqrt(totals[:3] / (totals[3] * normed_one.shape[1]))
    feed_width = gate_up_full.shape[1] // 2
    return (
        result.astype(jnp.bfloat16),
        input_grad,
        attn_full[:, :query_width],
        attn_full[:, query_width : query_width + key_width],
        attn_full[:, query_width + key_width : query_width + 2 * key_width],
        own_piece(summed[0]),
        own_piece(summed[1]),
        own_piece(summed[2]),
        attn_full[:, query_width + 2 * key_width :],
        own_piece(summed[3]),
        own_piece(summed[4]),
        gate_up_full[:, :feed_width],
        gate_up_full[:, feed_width:],
        down_full,
        root_means,
    )


def solution(mesh):
    in_specs = (
        P(("fsdp", "sp"), None),
        P(("fsdp", "sp"), None),
        P("fsdp"),
        P("fsdp", None),
        P("fsdp", None),
        P("fsdp", None),
        P("fsdp", None),
        P("fsdp"),
        P("fsdp"),
        P("fsdp"),
        P("fsdp", None),
        P("fsdp"),
        P("fsdp"),
        P("fsdp", None),
        P("fsdp", None),
        P("fsdp", None),
    )
    out_specs = (
        P(("fsdp", "sp"), None),
        P(("fsdp", "sp"), None),
        P("fsdp", None),
        P("fsdp", None),
        P("fsdp", None),
        P("fsdp"),
        P("fsdp"),
        P("fsdp"),
        P("fsdp", None),
        P("fsdp"),
        P("fsdp"),
        P("fsdp", None),
        P("fsdp", None),
        P("fsdp", None),
        P(),
    )
    return jax.shard_map(
        per_device, mesh=mesh, in_specs=in_specs, out_specs=out_specs, check_vma=False
    )
```

profile of v0, /device:TPU:2, one launch (start us, length us, event | category | flops | bytes accessed | tf_op | source)
XLA Modules:
  0.0 2683.8 jit_solution(1699894619708027220)
XLA Ops:
  13.8 21.6 all-reduce.7
  35.5 15.7 all_gather.51
  52.5 10.0 all_gather.53
  98.7 26.9 %all-to-all-done = bf16[384,4,384]{0,2,1:T(8,128)(2,1)S(1)} async-done(((bf16[384,4,384]{0,2,1:T(8,128)(2,1)}), bf16[384,4,384]{0,2,1:T(8,128)(2,1)S(1)}, u32[]{:S(2)}, u32[]{:S(2)}) %all-to-all-start) | async-done | bytes 1179680 | tf_op jit(solution)/shard_map/all_to_all | solution.py:213
  133.5 32.9 %while.27 = (s32[]{:T(128)}, bf16[3,512,3,128]{3,1,2,0:T(8,128)(2,1)}, f32[3,3,512]{2,1,0:T(4,128)}, s32[1536]{0:T(1024)S(1)}, s32[3]{0:T(128)S(1)}, /*index=5*/...) while((s32[]{:T(128)}, ...), condition=%wide.region_6.7_spmd, body=%wide.region_3.6_spmd.sunk | while | flops 1237056000 | bytes 33488056 | solution.py:89
  179.0 10.1 reduce.6
  196.8 26.9 %all-to-all-done.2 = bf16[4,2,73728]{2,1,0:T(2,128)(2,1)} async-done(((bf16[4,2,73728]{2,1,0:T(2,128)(2,1)}), bf16[4,2,73728]{2,1,0:T(2,128)(2,1)}, u32[]{:S(2)}, u32[]{:S(2)}) %all-to-all-start.2) | async-done | bytes 1179680 | tf_op jit(solution)/shard_map/all_to_all | solution.py:220
  236.6 21.2 fusion.109
  257.8 110.7 %all-gather.15.cloned.1.call-done = bf16[1536,8960]{1,0:T(8,128)(2,1)} async-done(((bf16[192,8960]{1,0:T(8,128)(2,1)}), bf16[1536,8960]{1,0:T(8,128)(2,1)}) %all-gather.15.cloned.1.call-update) | async-done | bytes 27525136 | tf_op jit(solution)/shard_map/all_gather | solution.py:183
  368.5 19.0 fusion.110
  387.5 118.1 %all-gather.17.cloned.1.call-done = bf16[8960,1536]{1,0:T(8,128)(2,1)} async-done(((bf16[1120,1536]{1,0:T(8,128)(2,1)}), bf16[8960,1536]{1,0:T(8,128)(2,1)}) %all-gather.17.cloned.1.call-update) | async-done | bytes 27525136 | tf_op jit(solution)/shard_map/all_gather | solution.py:184
  505.6 28.3 %multiply_convert_fusion = (bf16[384,8960]{1,0:T(8,128)(2,1)}, bf16[384,8960]{1,0:T(8,128)(2,1)}, bf16[384,8960]{1,0:T(8,128)(2,1)}) fusion(f32[384,8960]{1,0:T(8,128)} %fusion.109, f32[384,8960]{1,0:T(8,128)} %fusion.110, bf16[8960,1536]{1,0:T(8,128)(2,1)} %all-gather.17.cloned.1.call-done, bf16[384,1536]{1,0:T(8,128)(2,1)} %param.23, ...), kind=kOutput, calls=%fused_computation.56 | convolution fusion | flops 10623025152 | bytes 76875264 | tf_op jit(solution)/shard_map/dot_general | solution.py:52
  533.9 16.8 fusion.111
  550.8 18.0 convolution_add_fusion.2
  568.8 20.8 fusion.59
  604.2 28.9 %all-to-all-done.3 = bf16[384,4,384]{0,2,1:T(8,128)(2,1)S(1)} async-done(((bf16[384,4,384]{0,2,1:T(8,128)(2,1)}), bf16[384,4,384]{0,2,1:T(8,128)(2,1)S(1)}, u32[]{:S(2)}, u32[]{:S(2)}) %all-to-all-start.3) | async-done | bytes 1179680 | tf_op jit(solution)/shard_map/all_to_all | solution.py:249
  640.1 128.6 %while.28 = (s32[]{:T(128)}, f32[1536,128]{1,0:T(8,128)}, f32[1536,128]{1,0:T(8,128)S(1)}, bf16[3,512,3,128]{3,1,2,0:T(8,128)(2,1)}, s32[1536]{0:T(1024)S(1)}, /...) while((s32[]{:T(128)}, f32[1536,128]{1,0:T(8,128)}, ...), condition=%wide.region_11.12_spmd.clone, body=%wide.region_9.11_spmd.clone.sunk | while | flops 3043097088 | bytes 85373768 | solution.py:136
  659.3 9.4 fusion.174
  694.1 8.0 fusion.173
  702.1 9.4 fusion.174
  745.0 9.4 fusion.174
  785.2 10.1 reduce.7
  816.4 15.4 all-to-all-done.4
  855.6 31.8 %fusion.69 = f32[8960,1536]{1,0:T(8,128)} fusion(bf16[384,8960]{1,0:T(8,128)(2,1)} %get-tuple-element.325, bf16[384,1536]{1,0:T(8,128)(2,1)S(1)} %copy-done.26, f32[384]{0:T(512)S(1)} %copy-done.55), kind=kOutput, calls=%fused_computation.122 | convolution fusion | flops 10571415552 | bytes 63112704 | tf_op jit(solution)/shard_map/dot_general | solution.py:58
  888.8 47.7 %fusion.40 = f32[1536,17920]{1,0:T(8,128)} fusion(bf16[384,1536]{1,0:T(8,128)(2,1)S(1)} %copy-done.21, bf16[384,8960]{1,0:T(8,128)(2,1)} %get-tuple-element.323, bf16[384,8960]{1,0:T(8,128)(2,1)} %get-tuple-element.324), kind=kOutput, calls=%fused_computation.52 | convolution fusion | flops 21166817280 | bytes 125042688 | tf_op jit(solution)/shard_map/dot_general | solution.py:58
  936.6 140.1 %reduce-scatter.6.cloned.1.call-done = f32[48,3584]{1,0:T(8,128)} async-done(((f32[1536,3584]{1,0:T(8,128)}), f32[48,3584]{1,0:T(8,128)}) %reduce-scatter.6.cloned.1.call-update) | async-done | bytes 688144 | tf_op jit(solution)/shard_map/reduce_scatter | solution.py:291
  1078.6 466.2 %reduce-scatter.10.cloned.1.call-done = f32[280,1536]{1,0:T(8,128)} async-done(((f32[8960,1536]{1,0:T(8,128)}), f32[280,1536]{1,0:T(8,128)}) %reduce-scatter.10.cloned.1.call-update) | async-done | bytes 1720336
  1547.4 890.7 %reduce-scatter.8.cloned.1.call-done = f32[48,17920]{1,0:T(8,128)} async-done(((f32[1536,17920]{1,0:T(8,128)}), f32[48,17920]{1,0:T(8,128)}) %reduce-scatter.8.cloned.1.call-update) | async-done | bytes 3440656 | tf_op jit(solution)/shard_map/reduce_scatter | solution.py:293
  2462.1 43.7 %all-reduce.6 = (f32[1536]{0:T(1024)}, f32[256]{0:T(256)}, f32[256]{0:T(256)}, f32[1536]{0:T(1024)}, f32[1536]{0:T(1024)}, /*index=5*/f32[4]{0:T(128)}) all-reduce(f32[1536]{0:T(1024)} %reduce_sum.176, f32[256]{0:T(256)} %bitcast.249, f32[256]{0:T(256)} %bitcast.248, ...), channel_id=1, replica_groups=mesh['fsdp'=8,'sp'=4] {'fsdp','sp'}, use_global_device_ids=true, to_apply=%region_16.17 | all-reduce | flops 5124 | bytes 40992 | tf_op jit(solution)/shard_map/psum | solution.py:315
  2523.8 18.1 all-gather.23.cloned.1.call-done
  2547.7 120.0 %all-gather.21.cloned.1.call-done = bf16[192,17920]{1,0:T(8,128)(2,1)} async-done(((bf16[48,17920]{1,0:T(8,128)(2,1)}), bf16[192,17920]{1,0:T(8,128)(2,1)}) %all-gather.21.cloned.1.call-update) | async-done | bytes 6881296 | tf_op jit(solution)/shard_map/all_gather | solution.py:300
  2667.7 9.1 fusion.103
  (347 shorter events, 334.1 us)
Async XLA Ops:
  7.2 67.3 %all-gather.9.cloned.1.call-start = ((), (), s32[]{:S(2)}) async-start(), calls=%async_computation.9 | async-start | bytes 5308416 | tf_op jit(solution)/shard_map/all_gather | solution.py:171
  7.9 222.1 %all-gather.11.cloned.1.call-start = ((), (), s32[]{:S(2)}) async-start(), calls=%async_computation.10 | async-start | bytes 5308416 | tf_op jit(solution)/shard_map/all_gather | solution.py:174
  8.7 227.9 %all-gather.13.cloned.1.call-start = ((), (), s32[]{:S(2)}) async-start(), calls=%async_computation.11 | async-start | bytes 30965760 | tf_op jit(solution)/shard_map/all_gather | solution.py:182
  9.4 359.1 %all-gather.15.cloned.1.call-start = ((), (), s32[]{:S(2)}) async-start(), calls=%async_computation.12 | async-start | bytes 30965760 | tf_op jit(solution)/shard_map/all_gather | solution.py:183
  10.0 25.4 copy-start.49
  10.0 41.1 %copy-start.4 = (bf16[384,1536]{1,0:T(8,128)(2,1)S(1)}, bf16[384,1536]{1,0:T(8,128)(2,1)}, u32[]{:S(2)}) copy-start(bf16[384,1536]{1,0:T(8,128)(2,1)} %param.22) | copy-start | bytes 3538948
  10.1 495.5 %all-gather.17.cloned.1.call-start = ((), (), s32[]{:S(2)}) async-start(), calls=%async_computation.13 | async-start | bytes 30965760 | tf_op jit(solution)/shard_map/all_gather | solution.py:184
  35.5 39.0 %copy-start.46 = (f32[1536]{0:T(1024)}, f32[1536]{0:T(1024)S(1)}, u32[]{:S(2)}) copy-start(f32[1536]{0:T(1024)S(1)} %convert_element_type.219) | copy-start | bytes 18436
  51.5 23.0 copy-start.51
  68.0 25.6 all-to-all-start.1
  93.6 31.9 %all-to-all-start = ((bf16[384,4,384]{0,2,1:T(8,128)(2,1)}), bf16[384,4,384]{0,2,1:T(8,128)(2,1)S(1)}, u32[]{:S(2)}, u32[]{:S(2)}) async-start(bf16[384,4,384]{0,2,1:T(8,128)(2,1)} %fusion.61), calls=%async_computation | async-start | bytes 2359296 | tf_op jit(solution)/shard_map/all_to_all | solution.py:213
  166.4 12.1 copy-start.2
  166.4 12.1 copy-start.16
  166.5 12.1 copy-start.44
  190.8 32.8 %all-to-all-start.2 = ((bf16[4,2,73728]{2,1,0:T(2,128)(2,1)}), bf16[4,2,73728]{2,1,0:T(2,128)(2,1)}, u32[]{:S(2)}, u32[]{:S(2)}) async-start(bf16[4,2,73728]{2,1,0:T(2,128)(2,1)} %reshape.443), calls=%async_computation.2 | async-start | bytes 2359296 | tf_op jit(solution)/shard_map/all_to_all | solution.py:220
  196.8 395.1 %copy-start.54 = (f32[384]{0:T(512)}, f32[384]{0:T(512)S(1)}, u32[]{:S(2)}) copy-start(f32[384]{0:T(512)S(1)} %get-tuple-element.312) | copy-start | bytes 4612
  236.6 131.9 %copy-start.20 = (bf16[384,1536]{1,0:T(8,128)(2,1)}, bf16[384,1536]{1,0:T(8,128)(2,1)S(1)}, u32[]{:S(2)}) copy-start(bf16[384,1536]{1,0:T(8,128)(2,1)S(1)} %multiply_convert_fusion.4) | copy-start | bytes 3538948
  550.7 18.0 copy-start.35
  568.8 20.8 copy-start.25
  599.2 33.9 %all-to-all-start.3 = ((bf16[384,4,384]{0,2,1:T(8,128)(2,1)}), bf16[384,4,384]{0,2,1:T(8,128)(2,1)S(1)}, u32[]{:S(2)}, u32[]{:S(2)}) async-start(bf16[384,4,384]{0,2,1:T(8,128)(2,1)} %bitcast.28), calls=%async_computation.3 | async-start | bytes 2359296 | tf_op jit(solution)/shard_map/all_to_all | solution.py:249
  772.5 26.5 all-to-all-start.5
  799.0 32.8 %all-to-all-start.4 = ((bf16[4,2,73728]{2,1,0:T(2,128)(2,1)}), bf16[4,2,73728]{2,1,0:T(2,128)(2,1)}, u32[]{:S(2)}, u32[]{:S(2)}) async-start(bf16[4,2,73728]{2,1,0:T(2,128)(2,1)} %reshape.445), calls=%async_computation.4 | async-start | bytes 2359296 | tf_op jit(solution)/shard_map/all_to_all | solution.py:254
  804.1 272.6 %reduce-scatter.6.cloned.1.call-start = ((), (), s32[]{:S(2)}) async-start(), calls=%async_computation.14 | async-start | bytes 22708224 | tf_op jit(solution)/shard_map/reduce_scatter | solution.py:291
  816.2 26.0 copy-start.38
  816.3 25.8 copy-start.36
  854.4 690.4 %reduce-scatter.10.cloned.1.call-start = ((), (), s32[]{:S(2)}) async-start(), calls=%async_computation.19 | async-start | bytes 56770560
  887.4 1550.7 %reduce-scatter.8.cloned.1.call-start = ((), (), s32[]{:S(2)}) async-start(), calls=%async_computation.16 | async-start | bytes 113541120 | tf_op jit(solution)/shard_map/reduce_scatter | solution.py:293
  936.5 1582.6 %all-gather.19.cloned.1.call-start = ((), (), s32[]{:S(2)}) async-start(), calls=%async_computation.15 | async-start | bytes 1720320 | tf_op jit(solution)/shard_map/all_gather | solution.py:297
  1078.5 1463.3 %all-gather.23.cloned.1.call-start = ((), (), s32[]{:S(2)}) async-start(), calls=%async_computation.18 | async-start | bytes 4300800 | tf_op jit(solution)/shard_map/all_gather | solution.py:303
  1547.3 894.1 %copy-start.10 = (f32[384,12,128]{0,2,1:T(8,128)S(1)}, f32[384,12,128]{0,2,1:T(8,128)}, u32[]{:S(2)}) copy-start(f32[384,12,128]{0,2,1:T(8,128)} %copy-done.9) | copy-start | bytes 7077892
  1547.3 1120.4 %all-gather.21.cloned.1.call-start = ((), (), s32[]{:S(2)}) async-start(), calls=%async_computation.17 | async-start | bytes 8601600 | tf_op jit(solution)/shard_map/all_gather | solution.py:300
  2459.1 56.3 %copy-start.14 = (f32[384,1536]{1,0:T(8,128)S(1)}, f32[384,1536]{1,0:T(8,128)}, u32[]{:S(2)}) copy-start(f32[384,1536]{1,0:T(8,128)} %copy-done.12) | copy-start | bytes 7077892
  (56 other events, 217.9 us)
Sparse Core Ops, SparseCore 0:
  9.9 43.3 all-gather.8
  55.2 38.9 all-gather.10
  96.1 135.2 all-gather.12
  233.2 135.2 all-gather.14
  370.2 135.2 all-gather.16
  854.5 222.0 reduce-scatter.5
  1083.0 461.7 reduce-scatter.9
  1552.4 885.6 reduce-scatter.7
  2439.7 32.9 all-gather.18
  2474.1 67.6 all-gather.22
  2544.0 123.6 all-gather.20
where the time goes:
time: 2700 us; the launch traced here: 2680 us
  waiting for transfers between devices  1970 us (73%)
  matrix products  341 us (13%)
  local copies, waits for them, and re-layouts  115 us (4%)
  other arithmetic  109 us (4%)
  blocking collectives  91 us (3%)
  starting transfers between devices  28.1 us (1%)
    reduce_scatter x1, waiting for transfers between devices, per_device(): lax.psum_scatter(gate_up_term, ('fsdp', 'sp'), scatter_dimension=0, tiled...  891 us
    unnamed x12, waiting for transfers between devices  469 us
    reduce_scatter x1, waiting for transfers between devices, per_device(): lax.psum_scatter(attn_term, ('fsdp', 'sp'), scatter_dimension=0, tiled=True)  140 us
    all_gather x1, waiting for transfers between devices, per_device(): lax.all_gather(gate_up_share.astype(jnp.bfloat16), 'sp', axis=0, tiled=True)  120 us
    all_gather x1, waiting for transfers between devices, per_device(): lax.all_gather(w_down, 'fsdp', axis=0, tiled=True)  118 us
    all_gather x1, waiting for transfers between devices, per_device(): lax.all_gather(w_up, 'fsdp', axis=0, tiled=True)  111 us
    dot_general x4, matrix products, contract_first(): lax.dot_general(left, right, (((0,), (0,)), ((), ())), preferred_element_...  88.4 us
    dot_general x7, matrix products, contract_last(): lax.dot_general(left, right, (((1,), (1,)), ((), ())), preferred_element_...  76 us
  transfers between devices with their start and end apart: 17, of which 12 were waited for; matrix products, arithmetic and copies ran while one was open for 11% of the time, Pallas kernels for 0%

commit v1 on v0

v1 whole, which is shorter than its diff:
```python
import functools

import jax
import jax.numpy as jnp
from jax import lax
from jax.experimental import pallas as pl
from jax.experimental.pallas import tpu as pltpu
from jax.sharding import PartitionSpec as P

H = 12
KVH = 2
HD = 128
HEADS_STEP = 2


EPS = 1e-06
THETA = 1000000.0
BF = jnp.bfloat16
F32 = jnp.float32


def rotary_tables(positions):
    half_width = HD // 2
    inverse = THETA ** (-(jnp.arange(half_width, dtype=F32) * 2.0) / HD)
    angles = positions.astype(F32)[:, None] * inverse[None, :]
    cosine, sine = jnp.cos(angles), jnp.sin(angles)
    return (
        jnp.concatenate([cosine, cosine], axis=-1),
        jnp.concatenate([-sine, sine], axis=-1),
    )


def swap_halves(values):
    half_width = HD // 2
    return jnp.concatenate([values[..., half_width:], values[..., :half_width]], axis=-1)


def stream_positions(order_row, first_row, row_count, block_size):
    row_ids = first_row + jnp.arange(row_count, dtype=jnp.int32)
    which_block = row_ids // block_size
    matches = jnp.arange(order_row.shape[0], dtype=jnp.int32)[None, :] == which_block[:, None]
    block_start = jnp.sum(jnp.where(matches, order_row[None, :], 0), axis=1)
    return block_start * block_size + row_ids % block_size


def norm_backward(normed_grad, unit_rows, gain_rows, scale_rows):
    gain_grad = jnp.sum(normed_grad * unit_rows, axis=0)
    scaled = normed_grad * gain_rows
    inner = jnp.mean(scaled * unit_rows, axis=-1, keepdims=True)
    return (gain_grad, scale_rows * (scaled - unit_rows * inner))


def contract_last(left, right):
    return lax.dot_general(left, right, (((1,), (1,)), ((), ())), preferred_element_type=F32)


def contract_first(left, right):
    return lax.dot_general(left, right, (((0,), (0,)), ((), ())), preferred_element_type=F32)


def product(left, right):
    return jnp.dot(left, right, preferred_element_type=F32)


def head_scores(query, keys, allowed):
    scores = contract_last(query, keys) * (HD ** (-0.5))
    scores = jnp.where(allowed, scores, -1e30)
    weights_exp = jnp.exp(scores - jnp.max(scores, axis=-1, keepdims=True))
    return weights_exp, 1.0 / jnp.sum(weights_exp, axis=-1, keepdims=True)


def attend_forward_kernel(
    query_lin, keys, values, cosine, signed_sine, query_pos, key_pos, query_rot, mixed
):
    allowed = key_pos[...] <= query_pos[...]
    for head in range(HEADS_STEP):
        columns = slice(head * HD, (head + 1) * HD)
        linear = query_lin[:, columns]
        rotated = linear * cosine[...] + pltpu.roll(linear, HD // 2, 1) * signed_sine[...]
        rotated = rotated.astype(BF)
        query_rot[:, columns] = rotated
        weights_exp, inverse_sum = head_scores(rotated, keys[...], allowed)
        probabilities = (weights_exp * inverse_sum).astype(BF)
        mixed[:, columns] = product(probabilities, values[...]).astype(BF)


def attend_forward(query_lin, keys_values, cosine, signed_sine, query_pos, key_pos):
    rows, width = query_lin.shape
    count_all = keys_values.shape[0]
    per_kv = H // KVH // HEADS_STEP
    wide = HEADS_STEP * HD
    table = pl.BlockSpec((rows, HD), lambda step: (0, 0))
    by_head = pl.BlockSpec((rows, wide), lambda step: (0, step))
    return pl.pallas_call(
        attend_forward_kernel,
        grid=(H // HEADS_STEP,),
        in_specs=[
            by_head,
            pl.BlockSpec((count_all, HD), lambda step: (0, step // per_kv)),
            pl.BlockSpec((count_all, HD), lambda step: (0, KVH + step // per_kv)),
            table,
            table,
            pl.BlockSpec((rows, 1), lambda step: (0, 0)),
            pl.BlockSpec((1, count_all), lambda step: (0, 0)),
        ],
        out_specs=[by_head, by_head],
        out_shape=[jax.ShapeDtypeStruct((rows, width), BF)] * 2,
        compiler_params=pltpu.CompilerParams(vmem_limit_bytes=48 * 1024 * 1024),
        cost_estimate=pl.CostEstimate(
            flops=4 * rows * count_all * width,
            bytes_accessed=8 * rows * width + 2 * keys_values.size,
            transcendentals=H * rows * count_all,
        ),
    )(query_lin, keys_values, keys_values, cosine, signed_sine, query_pos, key_pos)


def attend_backward_kernel(
    query_rot,
    out_grad,
    keys,
    values,
    cosine,
    signed_sine,
    query_pos,
    key_pos,
    query_grad,
    key_grad,
    value_grad,
    key_sum,
    value_sum,
    *,
    per_kv,
):
    step = pl.program_id(0)
    allowed = key_pos[...] <= query_pos[...]
    scaling = HD ** (-0.5)

    @pl.when(step % per_kv == 0)
    def _():
        key_sum[...] = jnp.zeros_like(key_sum)
        value_sum[...] = jnp.zeros_like(value_sum)

    for head in range(HEADS_STEP):
        columns = slice(head * HD, (head + 1) * HD)
        query = query_rot[:, columns]
        grad = out_grad[:, columns]
        weights_exp, inverse_sum = head_scores(query, keys[...], allowed)
        probabilities = weights_exp * inverse_sum
        prob_grad = contract_last(grad, values[...])
        weighted = jnp.sum(probabilities * prob_grad, axis=-1, keepdims=True)
        score_grad = (probabilities * (prob_grad - weighted)).astype(BF)
        turned = product(score_grad, keys[...]) * scaling
        turned = turned * cosine[...] - pltpu.roll(turned, HD // 2, 1) * signed_sine[...]
        query_grad[:, columns] = turned.astype(BF)
        key_sum[...] += contract_first(score_grad, query) * scaling
        value_sum[...] += contract_first(probabilities.astype(BF), grad)

    @pl.when(step % per_kv == per_kv - 1)
    def _():
        key_grad[...] = key_sum[...].astype(BF)
        value_grad[...] = value_sum[...].astype(BF)


def attend_backward(query_rot, out_grad, keys_values, cosine, signed_sine, query_pos, key_pos):
    rows, width = query_rot.shape
    count_all = keys_values.shape[0]
    per_kv = H // KVH // HEADS_STEP
    wide = HEADS_STEP * HD
    table = pl.BlockSpec((rows, HD), lambda step: (0, 0))
    by_head = pl.BlockSpec((rows, wide), lambda step: (0, step))
    by_kv = pl.BlockSpec((count_all, HD), lambda step: (0, step // per_kv))
    return pl.pallas_call(
        functools.partial(attend_backward_kernel, per_kv=per_kv),
        grid=(H // HEADS_STEP,),
        in_specs=[
            by_head,
            by_head,
            by_kv,
            pl.BlockSpec((count_all, HD), lambda step: (0, KVH + step // per_kv)),
            table,
            table,
            pl.BlockSpec((rows, 1), lambda step: (0, 0)),
            pl.BlockSpec((1, count_all), lambda step: (0, 0)),
        ],
        out_specs=[by_head, by_kv, by_kv],
        out_shape=[
            jax.ShapeDtypeStruct((rows, width), BF),
            jax.ShapeDtypeStruct((count_all, KVH * HD), BF),
            jax.ShapeDtypeStruct((count_all, KVH * HD), BF),
        ],
        scratch_shapes=[pltpu.VMEM((count_all, HD), F32)] * 2,
        compiler_params=pltpu.CompilerParams(vmem_limit_bytes=48 * 1024 * 1024),
        cost_estimate=pl.CostEstimate(
            flops=10 * rows * count_all * width,
            bytes_accessed=8 * rows * width + 4 * keys_values.size,
            transcendentals=H * rows * count_all,
        ),
    )(query_rot, out_grad, keys_values, keys_values, cosine, signed_sine, query_pos, key_pos)


def swap_fsdp(values, mask):
    count = lax.axis_size("fsdp")
    return lax.ppermute(values, "fsdp", [(i, i ^ mask) for i in range(count)])


def gather_tokens(rows):
    if lax.axis_size("fsdp") != 8:
        return lax.all_gather(rows, "fsdp", axis=0, tiled=True)
    half = rows.shape[0] // 2
    from_x = swap_fsdp(rows, 2)
    from_y = swap_fsdp(rows, 4)
    far_first = swap_fsdp(from_y[:half], 2)
    far_last = swap_fsdp(from_x[half:], 4)
    own_core = jnp.concatenate([rows, from_x, from_y, far_first, far_last], axis=0)
    return jnp.concatenate([own_core, swap_fsdp(own_core, 1)], axis=0)


def scatter_tokens(partial):
    count = lax.axis_size("fsdp")
    if count != 8:
        return lax.psum_scatter(partial, "fsdp", scatter_dimension=0, tiled=True).astype(F32)
    rows = partial.shape[0] // count
    half = rows // 2
    other = swap_fsdp(partial[4 * rows :], 1)
    summed = (partial[: 4 * rows].astype(F32) + other.astype(F32)).astype(BF)
    own, to_x, to_y, far = (summed[k * rows : (k + 1) * rows] for k in range(4))
    by_x = swap_fsdp(far[:half], 2)
    by_y = swap_fsdp(far[half:], 4)
    to_y = jnp.concatenate([(to_y[:half].astype(F32) + by_x.astype(F32)).astype(BF), to_y[half:]], axis=0)
    to_x = jnp.concatenate([to_x[:half], (to_x[half:].astype(F32) + by_y.astype(F32)).astype(BF)], axis=0)
    return own.astype(F32) + swap_fsdp(to_x, 2).astype(F32) + swap_fsdp(to_y, 4).astype(F32)


def sp_reduce_scatter(take_part):
    count = lax.axis_size("sp")
    place = lax.axis_index("sp")
    up, down = None, None
    for step in range(1, count):
        part_up = take_part(jnp.clip(count - step + place, 0, count - 1))
        part_down = take_part(jnp.clip(step - count + place, 0, count - 1))
        if up is not None:
            part_up = (part_up.astype(F32) + up.astype(F32)).astype(BF)
            part_down = (part_down.astype(F32) + down.astype(F32)).astype(BF)
        up = lax.ppermute(part_up, "sp", [(i, i + 1) for i in range(step)])
        down = lax.ppermute(part_down, "sp", [(count - 1 - i, count - 2 - i) for i in range(step)])
    own = take_part(place)
    return (own.astype(F32) + up.astype(F32) + down.astype(F32)).astype(BF)


def sp_all_gather(own):
    count = lax.axis_size("sp")
    place = lax.axis_index("sp")
    up, down = own, own
    found = [own] * count
    for step in range(1, count):
        up = lax.ppermute(up, "sp", [(i, i + 1) for i in range(step - 1, count - 1)])
        down = lax.ppermute(down, "sp", [(count - 1 - i, count - 2 - i) for i in range(step - 1, count - 1)])
        for index in range(count):
            found[index] = jnp.where(place - index == step, up, found[index])
            found[index] = jnp.where(index - place == step, down, found[index])
    return found


def per_device(
    tokens,
    cotangent,
    seq_lengths,
    block_order,
    w_query,
    w_key,
    w_value,
    b_query,
    b_key,
    b_value,
    w_output,
    gain_attn,
    gain_mlp,
    w_gate,
    w_up,
    w_down,
):
    local_rows, width = tokens.shape
    sp_count = lax.axis_size("sp")
    sp_index = lax.axis_index("sp")
    fsdp_count = lax.axis_size("fsdp")
    fsdp_index = lax.axis_index("fsdp")
    group_rows = local_rows * sp_count
    block_rows = local_rows // 2
    query_width = H * HD
    key_width = KVH * HD
    hidden_all = w_gate.shape[1]
    hidden_width = hidden_all // fsdp_count
    shard_rows = w_gate.shape[0]

    w_kv = lax.all_gather(jnp.concatenate([w_key, w_value], axis=1), "fsdp", axis=0, tiled=True)
    vectors = lax.all_gather(
        jnp.concatenate([b_query, b_key, b_value, gain_attn, gain_mlp])[None, :], "fsdp", axis=0, tiled=True
    ).astype(F32)
    widths = [b_query.shape[0], b_key.shape[0], b_value.shape[0], gain_attn.shape[0], gain_mlp.shape[0]]
    edges = [sum(widths[:n]) for n in range(len(widths) + 1)]
    bias_q, bias_k, bias_v, gain_one, gain_two = (
        vectors[:, edges[n] : edges[n + 1]].reshape(-1) for n in range(len(widths))
    )
    w_q = lax.all_gather(w_query, "fsdp", axis=0, tiled=True)
    w_o = lax.all_gather(w_output, "fsdp", axis=0, tiled=True)

    gate_up = jnp.stack(
        [
            w_gate.reshape(shard_rows, fsdp_count, hidden_width),
            w_up.reshape(shard_rows, fsdp_count, hidden_width),
        ],
        axis=0,
    ).transpose(2, 0, 1, 3)
    gate_up = lax.all_to_all(gate_up, "fsdp", split_axis=0, concat_axis=0, tiled=True)
    my_gate = gate_up[:, 0].reshape(width, hidden_width)
    my_up = gate_up[:, 1].reshape(width, hidden_width)

    order_row = block_order[0]
    local_pos = stream_positions(order_row, sp_index * local_rows, local_rows, block_rows)
    group_pos = stream_positions(order_row, 0, group_rows, block_rows)
    query_pos, key_pos = local_pos[:, None], group_pos[None, :]
    valid_rows = (local_pos < seq_lengths[0]).astype(F32)[:, None]
    upstream = cotangent.astype(F32)
    mlp_grad = gather_tokens((valid_rows * upstream).astype(BF))

    inputs = tokens.astype(F32)
    scale_one = lax.rsqrt(jnp.mean(inputs * inputs, axis=-1, keepdims=True) + EPS)
    unit_one = inputs * scale_one
    normed_one = (unit_one * gain_one).astype(BF)
    cosine, signed_sine = rotary_tables(local_pos)
    kv_lin = product(normed_one, w_kv)
    key_lin = (kv_lin[:, :key_width] + bias_k).reshape(local_rows, KVH, HD)
    key_rot = key_lin * cosine[:, None, :] + swap_halves(key_lin) * signed_sine[:, None, :]
    keys_values = jnp.concatenate(
        [key_rot.reshape(local_rows, key_width).astype(BF), (kv_lin[:, key_width:] + bias_v).astype(BF)], axis=1
    )
    keys_values = lax.all_gather(keys_values, "sp", axis=0, tiled=True)
    query_lin = product(normed_one, w_q) + bias_q
    query_rot, mixed = attend_forward(query_lin, keys_values, cosine, signed_sine, query_pos, key_pos)
    attn_branch = product(mixed, w_o)
    hidden_in = inputs + valid_rows * attn_branch
    scale_two = lax.rsqrt(jnp.mean(hidden_in * hidden_in, axis=-1, keepdims=True) + EPS)
    unit_two = hidden_in * scale_two
    normed_two = gather_tokens((unit_two * gain_two).astype(BF))

    gate_lin = product(normed_two, my_gate)
    up_lin = product(normed_two, my_up)
    hidden_grad = contract_last(mlp_grad, w_down)
    sigma = jax.nn.sigmoid(gate_lin)
    activated = gate_lin * sigma
    hidden = (activated * up_lin).astype(BF)
    gate_grad = (hidden_grad * up_lin * (sigma * (1.0 + gate_lin * (1.0 - sigma)))).astype(BF)
    up_grad = (hidden_grad * activated).astype(BF)
    normed_two_grad = scatter_tokens((contract_last(gate_grad, my_gate) + contract_last(up_grad, my_up)).astype(BF))
    mlp_branch = scatter_tokens(product(hidden, w_down).astype(BF))

    sp_rows = shard_rows // sp_count

    def down_part(index):
        part = hidden_width // sp_count
        return lax.dynamic_slice_in_dim(down_term, index * part, part, 0)

    def split_rows(term):
        blocks = term.reshape(fsdp_count, sp_count, sp_rows, hidden_width)
        return lambda index: lax.dynamic_index_in_dim(blocks, index, 1, keepdims=False)

    def gather_rows(own):
        own = lax.all_to_all(own, "fsdp", split_axis=0, concat_axis=0, tiled=True)
        parts = [part.transpose(1, 0, 2).reshape(sp_rows, hidden_all) for part in sp_all_gather(own)]
        return jnp.concatenate(parts, axis=0).astype(F32)

    down_term = contract_first(hidden, mlp_grad).astype(BF)
    grad_down = jnp.concatenate(sp_all_gather(sp_reduce_scatter(down_part)), axis=0).astype(F32)
    gate_term = contract_first(normed_two, gate_grad).astype(BF)
    grad_gate = gather_rows(sp_reduce_scatter(split_rows(gate_term)))
    up_term = contract_first(normed_two, up_grad).astype(BF)
    grad_up = gather_rows(sp_reduce_scatter(split_rows(up_term)))

    result = hidden_in + valid_rows * mlp_branch
    gain_two_grad, norm_two_back = norm_backward(normed_two_grad, unit_two, gain_two, scale_two)
    hidden_in_grad = upstream + norm_two_back
    attn_grad = (valid_rows * hidden_in_grad).astype(BF)
    mixed_grad = contract_last(attn_grad, w_o).astype(BF)
    query_lin_grad, key_part, value_part = attend_backward(
        query_rot, mixed_grad, keys_values, cosine, signed_sine, query_pos, key_pos
    )
    pair_total = lax.psum_scatter(
        jnp.concatenate([key_part, value_part], axis=1), "sp", scatter_dimension=0, tiled=True
    ).astype(F32)
    key_rot_grad = pair_total[:, :key_width].reshape(local_rows, KVH, HD)
    key_lin_grad = key_rot_grad * cosine[:, None, :] - swap_halves(key_rot_grad) * signed_sine[:, None, :]
    kv_lin_grad = jnp.concatenate(
        [key_lin_grad.reshape(local_rows, key_width).astype(BF), pair_total[:, key_width:].astype(BF)], axis=1
    )
    normed_one_grad = contract_last(query_lin_grad, w_q) + contract_last(kv_lin_grad, w_kv)
    gain_one_grad, norm_one_back = norm_backward(normed_one_grad, unit_one, gain_one, scale_one)
    input_grad = hidden_in_grad + norm_one_back

    output_term = contract_first(mixed, attn_grad).astype(BF)
    output_share = lax.psum_scatter(output_term, "fsdp", scatter_dimension=0, tiled=True)
    projection_term = contract_first(normed_one, jnp.concatenate([query_lin_grad, kv_lin_grad], axis=1)).astype(BF)
    projection_share = lax.psum_scatter(projection_term, "fsdp", scatter_dimension=0, tiled=True)
    attn_share = jnp.concatenate([projection_share, output_share], axis=1)

    def attn_part(index):
        return lax.dynamic_slice_in_dim(attn_share, index * sp_rows, sp_rows, 0)

    attn_full = jnp.concatenate(sp_all_gather(sp_reduce_scatter(attn_part)), axis=0).astype(F32)

    stat_parts = jnp.stack(
        [
            jnp.sum(valid_rows * result * result),
            jnp.sum(valid_rows * attn_branch * attn_branch),
            jnp.sum(valid_rows * mlp_branch * mlp_branch),
            jnp.sum(valid_rows),
        ]
    )
    summed = lax.psum(
        (
            jnp.sum(query_lin_grad.astype(F32), axis=0),
            jnp.sum(kv_lin_grad.astype(F32), axis=0),
            gain_one_grad,
            gain_two_grad,
            stat_parts,
        ),
        ("fsdp", "sp"),
    )

    def own_piece(vector):
        width_piece = vector.shape[0] // fsdp_count
        return lax.dynamic_slice_in_dim(vector, fsdp_index * width_piece, width_piece, 0)

    totals = summed[4]
    root_means = jnp.sqrt(totals[:3] / (totals[3] * width))
    return (
        result.astype(BF),
        input_grad,
        attn_full[:, :query_width],
        attn_full[:, query_width : query_width + key_width],
        attn_full[:, query_width + key_width : query_width + 2 * key_width],
        own_piece(summed[0]),
        own_piece(summed[1][:key_width]),
        own_piece(summed[1][key_width:]),
        attn_full[:, query_width + 2 * key_width :],
        own_piece(summed[2]),
        own_piece(summed[3]),
        grad_gate,
        grad_up,
        grad_down,
        root_means,
    )


def solution(mesh):
    both, first = P(("fsdp", "sp"), None), P("fsdp", None)
    one = P("fsdp")
    in_specs = (both, both, one, first, first, first, first, one, one, one, first, one, one, first, first, first)
    out_specs = (both, both, first, first, first, one, one, one, first, one, one, first, first, first, P())
    return jax.shard_map(per_device, mesh=mesh, in_specs=in_specs, out_specs=out_specs, check_vma=False)
```

time: 2700 us -> 1070 us (0.40)
  waiting for transfers between devices: 1970 us -> 330 us
  starting transfers between devices: 28.1 us -> 176 us
  matrix products: 341 us -> 195 us
  Pallas kernels: 0 us -> 52.1 us
  blocking collectives: 91 us -> 55.3 us
    reduce_scatter x2 -> x3, waiting for transfers between devices: 1030 us -> 25.9 us  [the longest x1 25.9 us: per_device(): lax.psum_scatter(jnp.concatenate([key_part, value_part], axis=1), 'sp', s...]
    unnamed x12 -> x7, waiting for transfers between devices: 469 us -> 1.3 us
    all_gather x8 -> x4, waiting for transfers between devices: 367 us -> 59.8 us  [the longest x1 43.3 us: per_device(): w_o = lax.all_gather(w_output, 'fsdp', axis=0, tiled=True)]
    ppermute x0 -> x68, waiting for transfers between devices: none -> 239 us  [the longest x20 92.3 us: swap_fsdp(): return lax.ppermute(values, 'fsdp', [(i, i ^ mask) for i in range(count)])]
    ppermute x0 -> x68, starting transfers between devices: none -> 161 us  [the longest x12 60.2 us: sp_all_gather(): lax.ppermute(up, 'sp', [(i, i + 1) for i in range(step - 1, count - 1)])]
    dot_general x28 -> x6, matrix products: 177 us -> 61.4 us  [product(): return jnp.dot(left, right, preferred_element_type=F32)]
    all_to_all x6 -> x3, waiting for transfers between devices: 104 us -> 3.15 us  [the longest x2 3.15 us: gather_rows(): own = lax.all_to_all(own, 'fsdp', split_axis=0, concat_axis=0, tiled=True)]
    pallas_call x0 -> x2, Pallas kernels: none -> 52.1 us  [the longest x1 32.7 us: attend_backward(): pl.pallas_call(functools.partial(attend_backward_kernel, per_kv=per_kv),...]
  transfers between devices with their start and end apart: 17 -> 78, of which waited for: 12 -> 31; matrix products, arithmetic and copies ran while one was open for 11% -> 27% of each run, Pallas kernels for 0% -> 2%
where the time goes in v1:
time: 1070 us; the launch traced here: 1060 us
  waiting for transfers between devices  330 us (31%)
  matrix products  195 us (18%)
  starting transfers between devices  176 us (16%)
  local copies, waits for them, and re-layouts  132 us (12%)
  other arithmetic  106 us (10%)
  blocking collectives  55.3 us (5%)
  Pallas kernels  52.1 us (5%)
  between operations  17.2 us (2%)
    ppermute x20, waiting for transfers between devices, swap_fsdp(): return lax.ppermute(values, 'fsdp', [(i, i ^ mask) for i in range(count)])  92.3 us
    dot_general x6, matrix products, contract_last(): lax.dot_general(left, right, (((1,), (1,)), ((), ())), preferred_element_...  76.2 us
    ppermute x12, waiting for transfers between devices, sp_all_gather(): lax.ppermute(down, 'sp', [(count - 1 - i, count - 2 - i) for i in range(s...  72.3 us
    ppermute x12, waiting for transfers between devices, sp_reduce_scatter(): up = lax.ppermute(part_up, 'sp', [(i, i + 1) for i in range(step)])  68.3 us
    dot_general x6, matrix products, product(): return jnp.dot(left, right, preferred_element_type=F32)  61.4 us
    ppermute x12, starting transfers between devices, sp_all_gather(): lax.ppermute(up, 'sp', [(i, i + 1) for i in range(step - 1, count - 1)])  60.2 us
    dot_general x5, matrix products, contract_first(): lax.dot_general(left, right, (((0,), (0,)), ((), ())), preferred_element_...  57 us
    ppermute x12, starting transfers between devices, sp_reduce_scatter(): up = lax.ppermute(part_up, 'sp', [(i, i + 1) for i in range(step)])  52.7 us
  transfers between devices with their start and end apart: 78, of which 31 were waited for; matrix products, arithmetic and copies ran while one was open for 27% of the time, Pallas kernels for 2%

profile of v1, /device:TPU:2, one launch (start us, length us, event | category | flops | bytes accessed | tf_op | source)
XLA Modules:
  0.0 1062.6 jit_solution(6477753033590728934)
XLA Ops:
  13.3 9.0 all-gather.1
  25.6 11.8 %all-gather.9.cloned.1.call-done = bf16[1536,512]{1,0:T(8,128)(2,1)} async-done(((bf16[192,512]{1,0:T(8,128)(2,1)}), bf16[1536,512]{1,0:T(8,128)(2,1)}) %all-gather.9.cloned.1.call-update) | async-done | bytes 1572880 | tf_op jit(solution)/shard_map/all_gather | solution.py:295
  89.1 24.7 %collective-permute-done.11 = bf16[384,1536]{1,0:T(8,128)(2,1)} collective-permute-done((bf16[384,1536]{1,0:T(8,128)(2,1)}, bf16[384,1536]{1,0:T(8,128)(2,1)}, u32[]{:S(2)}, u32[]{:S(2)}) %collective-permute-start.11) | collective-permute-done | bytes 1179680 | tf_op jit(solution)/shard_map/ppermute | solution.py:203
  134.2 19.4 %shard_map.271 = (bf16[384,1536]{1,0:T(8,128)(2,1)S(1)}, bf16[384,1536]{1,0:T(8,128)(2,1)S(1)}) custom-call(f32[384,1536]{1,0:T(8,128)} %convolution_add_fusion.1.query_lin, bf16[1536,512]{1,0:T(8,128)(2,1)S(1)} %copy-done.12, bf16[1536,512]{1,0:T(8,128)(2,1)S(1)} %copy-done.12, f32[384,128]{1,0:T(8,128)S(1)} %copy-done.8, f32[384,128]{1,0:T(8,128)S(1)} %copy-done.2, ...), custom_call_target="tpu_custom_call" | custom-call | flops 3623878656 | bytes 6291456 | tf_op jit(solution)/shard_map/pallas_call | solution.py:94
  155.7 43.3 %all-gather.13.cloned.1.call-done = bf16[1536,1536]{1,0:T(8,128)(2,1)} async-done(((bf16[192,1536]{1,0:T(8,128)(2,1)}), bf16[1536,1536]{1,0:T(8,128)(2,1)}) %all-gather.13.cloned.1.call-update) | async-done | bytes 4718608 | tf_op jit(solution)/shard_map/all_gather | solution.py:305
  224.2 16.1 %collective-permute-done.1 = bf16[384,1536]{1,0:T(8,128)(2,1)S(1)} collective-permute-done((bf16[384,1536]{1,0:T(8,128)(2,1)S(1)}, bf16[384,1536]{1,0:T(8,128)(2,1)S(1)}, u32[]{:S(2)}, u32[]{:S(2)}) %collective-permute-start.1) | collective-permute-done | bytes 1179680 | tf_op jit(solution)/shard_map/ppermute | solution.py:203
  244.5 10.2 collective-permute-done.2
  271.4 16.7 %fusion.69 = f32[3072,1120]{0,1:T(8,128)} fusion(bf16[3072,1536]{1,0:T(8,128)(2,1)} %constant_dynamic-update-slice_fusion.5, bf16[1536,1120]{1,0:T(8,128)(2,1)S(1)} %bitcast.145), kind=kOutput, calls=%fused_computation.226 | convolution fusion | flops 10569646080 | bytes 26640384 | tf_op jit(solution)/shard_map/dot_general | solution.py:62
  288.1 16.3 %fusion.70 = f32[3072,1120]{0,1:T(8,128)} fusion(bf16[3072,1536]{1,0:T(8,128)(2,1)} %constant_dynamic-update-slice_fusion.5, bf16[1536,1120]{1,0:T(8,128)(2,1)S(1)} %bitcast.143), kind=kOutput, calls=%fused_computation.227 | convolution fusion | flops 10569646080 | bytes 26640384 | tf_op jit(solution)/shard_map/dot_general | solution.py:62
  304.4 26.1 %multiply_convert_fusion = (bf16[3072,1120]{0,1:T(8,128)(2,1)}, bf16[3072,1120]{0,1:T(8,128)(2,1)}, bf16[3072,1120]{0,1:T(8,128)(2,1)}) fusion(f32[3072,1120]{0,1:T(8,128)} %fusion.69, f32[3072,1120]{0,1:T(8,128)} %fusion.70, bf16[3072,1536]{1,0:T(8,128)(2,1)} %constant_dynamic-update-slice_fusion.16, bf16[1120,1536]{1,0:T(8,128)(2,1)S(1)} %copy-done), kind=kOutput, calls=%fused_computation.1 | convolution fusion | flops 10621255680 | bytes 61046784 | tf_op jit(solution)/shard_map/dot_general | solution.py:54
  330.5 17.3 %fusion.71 = f32[3072,1536]{1,0:T(8,128)} fusion(bf16[3072,1120]{0,1:T(8,128)(2,1)} %get-tuple-element.48, bf16[1536,1120]{1,0:T(8,128)(2,1)S(1)} %bitcast.146), kind=kOutput, calls=%fused_computation.228 | convolution fusion | flops 10569646080 | bytes 29196288 | tf_op jit(solution)/shard_map/dot_general | solution.py:54
  347.7 20.8 %add_convert_fusion = bf16[3072,1536]{1,0:T(8,128)(2,1)} fusion(f32[3072,1536]{1,0:T(8,128)} %fusion.71, bf16[3072,1120]{0,1:T(8,128)(2,1)} %get-tuple-element.47, bf16[1536,1120]{1,0:T(8,128)(2,1)} %bitcast.144), kind=kOutput, calls=%fused_computation | convolution fusion | flops 10579083264 | bytes 38633472 | tf_op jit(solution)/shard_map/dot_general | solution.py:54
  374.3 13.1 %convolution_convert_fusion = bf16[3072,1536]{1,0:T(8,128)(2,1)S(1)} fusion(bf16[3072,1120]{0,1:T(8,128)(2,1)S(1)} %copy-done.61, bf16[1120,1536]{1,0:T(8,128)(2,1)S(1)} %copy-done), kind=kOutput, calls=%fused_computation.6 | convolution fusion | flops 10574364672 | bytes 19759104 | tf_op jit(solution)/shard_map/dot_general | solution.py:62
  432.5 14.2 %convolution_convert_fusion.1 = bf16[1536,1120]{0,1:T(8,128)(2,1)} fusion(bf16[3072,1120]{0,1:T(8,128)(2,1)S(1)} %bitcast.156, bf16[3072,1536]{1,0:T(8,128)(2,1)} %constant_dynamic-update-slice_fusion.5), kind=kOutput, calls=%fused_computation.9 | convolution fusion | flops 10571366400 | bytes 19759104 | tf_op jit(solution)/shard_map/dot_general | solution.py:58
  453.1 24.0 %collective-permute-done.7 = bf16[384,1536]{1,0:T(8,128)(2,1)} collective-permute-done((bf16[384,1536]{1,0:T(8,128)(2,1)}, bf16[384,1536]{1,0:T(8,128)(2,1)}, u32[]{:S(2)}, u32[]{:S(2)}) %collective-permute-start.7) | collective-permute-done | bytes 1179680 | tf_op jit(solution)/shard_map/ppermute | solution.py:203
  492.0 32.7 %shard_map.272 = (bf16[384,1536]{1,0:T(8,128)(2,1)S(1)}, bf16[1536,256]{1,0:T(8,128)(2,1)S(1)}, bf16[1536,256]{1,0:T(8,128)(2,1)S(1)}) custom-call(bf16[384,1536]{1,0:T(8,128)(2,1)S(1)} %copy-done.16, bf16[384,1536]{1,0:T(8,128)(2,1)S(1)} %convolution_convert_fusion.6.out_grad, bf16[1536,512]{1,0:T(8,128)(2,1)} %all-gather.11.cloned.1.call-done.keys.values, ...), custom_call_target="tpu_custom_call" | custom-call | flops 9059696640 | bytes 7864320 | tf_op jit(solution)/shard_map/pallas_call | solution.py:172
  535.9 15.2 %convolution_convert_fusion.2 = bf16[1536,1120]{0,1:T(8,128)(2,1)S(1)} fusion(bf16[3072,1120]{0,1:T(8,128)(2,1)} %get-tuple-element.48, bf16[3072,1536]{1,0:T(8,128)(2,1)} %constant_dynamic-update-slice_fusion.5), kind=kOutput, calls=%fused_computation.10 | convolution fusion | flops 10571366400 | bytes 19759104 | tf_op jit(solution)/shard_map/dot_general | solution.py:58
  559.9 25.9 %reduce-scatter.4.cloned.1.call-done = bf16[384,512]{1,0:T(8,128)(2,1)} async-done(((bf16[1536,512]{1,0:T(8,128)(2,1)}), bf16[384,512]{1,0:T(8,128)(2,1)}) %reduce-scatter.4.cloned.1.call-update) | async-done | bytes 393232 | tf_op jit(solution)/shard_map/reduce_scatter | solution.py:387
  596.2 15.3 %convolution_convert_fusion.3 = bf16[1120,1536]{1,0:T(8,128)(2,1)S(1)} fusion(bf16[3072,1120]{0,1:T(8,128)(2,1)} %get-tuple-element.49, bf16[3072,1536]{1,0:T(8,128)(2,1)} %constant_dynamic-update-slice_fusion.16), kind=kOutput, calls=%fused_computation.11 | convolution fusion | flops 10571366400 | bytes 19759104 | tf_op jit(solution)/shard_map/dot_general | solution.py:58
  622.5 11.3 %collective-permute-done.56 = bf16[280,1536]{1,0:T(8,128)(2,1)S(1)} collective-permute-done((bf16[280,1536]{1,0:T(8,128)(2,1)S(1)}, bf16[280,1536]{1,0:T(8,128)(2,1)S(1)}, u32[]{:S(2)}, u32[]{:S(2)}) %collective-permute-start.56) | collective-permute-done | bytes 860192 | tf_op jit(solution)/shard_map/ppermute | solution.py:244
  639.8 13.0 %collective-permute-done.33 = bf16[8,48,1120]{2,1,0:T(8,128)(2,1)S(1)} collective-permute-done((bf16[8,48,1120]{2,1,0:T(8,128)(2,1)S(1)}, bf16[8,48,1120]{2,1,0:T(8,128)(2,1)S(1)}, u32[]{:S(2)}, u32[]{:S(2)}) %collective-permute-start.33) | collective-permute-done | bytes 860192 | tf_op jit(solution)/shard_map/ppermute | solution.py:244
  654.9 16.8 %collective-permute-done.45 = bf16[8,48,1120]{2,1,0:T(8,128)(2,1)S(1)} collective-permute-done((bf16[8,48,1120]{2,1,0:T(8,128)(2,1)S(1)}, bf16[8,48,1120]{2,1,0:T(8,128)(2,1)S(1)}, u32[]{:S(2)}, u32[]{:S(2)}) %collective-permute-start.45) | collective-permute-done | bytes 860192 | tf_op jit(solution)/shard_map/ppermute | solution.py:244
  678.0 12.2 %collective-permute-done.57 = bf16[280,1536]{1,0:T(8,128)(2,1)S(1)} collective-permute-done((bf16[280,1536]{1,0:T(8,128)(2,1)S(1)}, bf16[280,1536]{1,0:T(8,128)(2,1)S(1)}, u32[]{:S(2)}, u32[]{:S(2)}) %collective-permute-start.57) | collective-permute-done | bytes 860192 | tf_op jit(solution)/shard_map/ppermute | solution.py:244
  700.1 9.1 collective-permute-done.46
  751.6 16.2 %collective-permute-start.65 = (bf16[280,1536]{1,0:T(8,128)(2,1)}, bf16[280,1536]{1,0:T(8,128)(2,1)}, u32[]{:S(2)}, u32[]{:S(2)}) collective-permute-start(bf16[280,1536]{1,0:T(8,128)(2,1)} %add_convert_fusion.3), channel_id=1, source_target_pairs={{0,1},{1,2},{2,3},{4,5},{5,6},{6,7},{8,9},{9,10},{10,11},{12,13},{... | collective-permute-start | bytes 2580488 | tf_op jit(solution)/shard_map/ppermute | solution.py:256
  785.3 21.0 %collective-permute-start.41 = (bf16[8,48,1120]{2,1,0:T(8,128)(2,1)S(1)}, bf16[8,48,1120]{2,1,0:T(8,128)(2,1)}, u32[]{:S(2)}, u32[]{:S(2)}) collective-permute-start(bf16[8,48,1120]{2,1,0:T(8,128)(2,1)S(1)} %all-to-all-done.1), channel_id=1, source_target_pairs={{0,1},{1,2},{2,3},{4,5},{5,6},{6,7},{8,9},{9,10},{10,11},{12,13},{... | collective-permute-start | bytes 2580488 | tf_op jit(solution)/shard_map/ppermute | solution.py:256
  810.5 12.7 %collective-permute-done.38 = bf16[8,48,1120]{2,1,0:T(8,128)(2,1)} collective-permute-done((bf16[8,48,1120]{2,1,0:T(8,128)(2,1)S(1)}, bf16[8,48,1120]{2,1,0:T(8,128)(2,1)}, u32[]{:S(2)}, u32[]{:S(2)}) %collective-permute-start.38) | collective-permute-done | bytes 860192 | tf_op jit(solution)/shard_map/ppermute | solution.py:257
  826.1 15.6 %collective-permute-done.63 = bf16[280,1536]{1,0:T(8,128)(2,1)} collective-permute-done((bf16[280,1536]{1,0:T(8,128)(2,1)}, bf16[280,1536]{1,0:T(8,128)(2,1)}, u32[]{:S(2)}, u32[]{:S(2)}) %collective-permute-start.63) | collective-permute-done | bytes 860192 | tf_op jit(solution)/shard_map/ppermute | solution.py:257
  844.5 16.0 %collective-permute-done.52 = bf16[8,48,1120]{2,1,0:T(8,128)(2,1)S(1)} collective-permute-done((bf16[8,48,1120]{2,1,0:T(8,128)(2,1)}, bf16[8,48,1120]{2,1,0:T(8,128)(2,1)S(1)}, u32[]{:S(2)}, u32[]{:S(2)}) %collective-permute-start.52) | collective-permute-done | bytes 860192 | tf_op jit(solution)/shard_map/ppermute | solution.py:257
  887.2 10.8 %collective-permute-done.64 = bf16[280,1536]{1,0:T(8,128)(2,1)} collective-permute-done((bf16[280,1536]{1,0:T(8,128)(2,1)}, bf16[280,1536]{1,0:T(8,128)(2,1)}, u32[]{:S(2)}, u32[]{:S(2)}) %collective-permute-start.64) | collective-permute-done | bytes 860192 | tf_op jit(solution)/shard_map/ppermute | solution.py:257
  945.1 17.3 %collective-permute-start.22 = (bf16[48,3584]{1,0:T(8,128)(2,1)}, bf16[48,3584]{1,0:T(8,128)(2,1)S(1)}, u32[]{:S(2)}, u32[]{:S(2)}) collective-permute-start(bf16[48,3584]{1,0:T(8,128)(2,1)} %get-tuple-element.97), channel_id=1, source_target_pairs={{0,1},{1,2},{2,3},{4,5},{5,6},{6,7},{8,9},{9,10},{10,11},{12,13},{... | collective-permute-start | bytes 1032200 | tf_op jit(solution)/shard_map/ppermute | solution.py:244
  993.5 46.3 %all-reduce = (f32[1536]{0:T(1024)S(1)}, f32[512]{0:T(512)S(1)}, f32[1536]{0:T(1024)S(1)}, f32[1536]{0:T(1024)S(1)}, f32[4]{0:T(128)S(1)}) all-reduce(f32[1536]{0:T(1024)S(1)} %convert_reduce_fusion, f32[512]{0:T(512)S(1)} %convert_reduce_fusion.1, f32[1536]{0:T(1024)S(1)} %get-tuple-element.29, ...), channel_id=1, replica_groups=mesh['fsdp'=8,'sp'=4] {'fsdp','sp'}, use_global_device_ids=true, to_apply=%region_10.11 | all-reduce | flops 5124 | bytes 40992 | tf_op jit(solution)/shard_map/psum | solution.py:418
  (425 shorter events, 454.9 us)
Async XLA Ops:
  9.0 110.1 %all-gather.7.cloned.1.call-start = ((), (), s32[]{:S(2)}) async-start(), calls=%async_computation.6 | async-start | bytes 5308416 | tf_op jit(solution)/shard_map/all_gather | solution.py:304
  9.8 120.2 %all-gather.11.cloned.1.call-start = ((), (), s32[]{:S(2)}) async-start(), calls=%async_computation.8 | async-start | bytes 1966080 | tf_op jit(solution)/shard_map/all_gather | solution.py:337
  47.8 151.3 %all-gather.13.cloned.1.call-start = ((), (), s32[]{:S(2)}) async-start(), calls=%async_computation.9 | async-start | bytes 5308416 | tf_op jit(solution)/shard_map/all_gather | solution.py:305
  52.6 63.2 %collective-permute-start.10 = (bf16[384,1536]{1,0:T(8,128)(2,1)}, bf16[384,1536]{1,0:T(8,128)(2,1)}, u32[]{:S(2)}, u32[]{:S(2)}) collective-permute-start(bf16[384,1536]{1,0:T(8,128)(2,1)} %get-tuple-element.42), channel_id=1, source_target_pairs={{0,8},{4,12},{8,0},{12,4},{16,24},{20,28},{24,16},{28,20},{1,9},{5... | collective-permute-start | bytes 3538952 | tf_op jit(solution)/shard_map/ppermute | solution.py:203
  53.1 60.8 %collective-permute-start.11 = (bf16[384,1536]{1,0:T(8,128)(2,1)}, bf16[384,1536]{1,0:T(8,128)(2,1)}, u32[]{:S(2)}, u32[]{:S(2)}) collective-permute-start(bf16[384,1536]{1,0:T(8,128)(2,1)} %get-tuple-element.42), channel_id=1, source_target_pairs={{0,16},{4,20},{8,24},{12,28},{16,0},{20,4},{24,8},{28,12},{1,17},{... | collective-permute-start | bytes 3538952 | tf_op jit(solution)/shard_map/ppermute | solution.py:203
  80.0 177.0 %all-to-all-start = ((bf16[8,2,192,1120]{3,2,1,0:T(8,128)(2,1)}), bf16[8,2,192,1120]{3,2,1,0:T(8,128)(2,1)}, u32[]{:S(2)}, u32[]{:S(2)}) async-start(bf16[8,2,192,1120]{3,2,1,0:T(8,128)(2,1)} %copy.126), calls=%async_computation | async-start | bytes 14155776 | tf_op jit(solution)/shard_map/all_to_all | solution.py:314
  85.5 500.3 %reduce-scatter.4.cloned.1.call-start = ((), (), s32[]{:S(2)}) async-start(), calls=%async_computation.10 | async-start | bytes 1966080 | tf_op jit(solution)/shard_map/reduce_scatter | solution.py:387
  115.8 102.9 %collective-permute-start.12 = (bf16[192,1536]{1,0:T(8,128)(2,1)}, bf16[192,1536]{1,0:T(8,128)(2,1)}, u32[]{:S(2)}, u32[]{:S(2)}) collective-permute-start(bf16[192,1536]{1,0:T(8,128)(2,1)} %slice.225), channel_id=1, source_target_pairs={{0,8},{4,12},{8,0},{12,4},{16,24},{20,28},{24,16},{28,20},{1,9},{5... | collective-permute-start | bytes 1769480 | tf_op jit(solution)/shard_map/ppermute | solution.py:203
  117.7 103.2 %collective-permute-start.13 = (bf16[192,1536]{1,0:T(8,128)(2,1)}, bf16[192,1536]{1,0:T(8,128)(2,1)}, u32[]{:S(2)}, u32[]{:S(2)}) collective-permute-start(bf16[192,1536]{1,0:T(8,128)(2,1)} %slice.226), channel_id=1, source_target_pairs={{0,16},{4,20},{8,24},{12,28},{16,0},{20,4},{24,8},{28,12},{1,17},{... | collective-permute-start | bytes 1769480 | tf_op jit(solution)/shard_map/ppermute | solution.py:203
  429.1 48.0 %collective-permute-start.7 = (bf16[384,1536]{1,0:T(8,128)(2,1)}, bf16[384,1536]{1,0:T(8,128)(2,1)}, u32[]{:S(2)}, u32[]{:S(2)}) collective-permute-start(bf16[384,1536]{1,0:T(8,128)(2,1)} %pad_maximum_fusion.1), channel_id=1, source_target_pairs={{0,8},{4,12},{8,0},{12,4},{16,24},{20,28},{24,16},{28,20},{1,9},{5... | collective-permute-start | bytes 3538952 | tf_op jit(solution)/shard_map/ppermute | solution.py:203
  431.0 46.2 %collective-permute-start.9 = (bf16[384,1536]{1,0:T(8,128)(2,1)}, bf16[384,1536]{1,0:T(8,128)(2,1)}, u32[]{:S(2)}, u32[]{:S(2)}) collective-permute-start(bf16[384,1536]{1,0:T(8,128)(2,1)} %pad_maximum_fusion.2), channel_id=1, source_target_pairs={{0,16},{4,20},{8,24},{12,28},{16,0},{20,4},{24,8},{28,12},{1,17},{... | collective-permute-start | bytes 3538952 | tf_op jit(solution)/shard_map/ppermute | solution.py:203
  527.0 380.2 %reduce-scatter.6.cloned.1.call-start = ((), (), s32[]{:S(2)}) async-start(), calls=%async_computation.11 | async-start | bytes 7077888 | tf_op jit(solution)/shard_map/reduce_scatter | solution.py:402
  529.9 87.4 %collective-permute-start.44 = (bf16[8,48,1120]{2,1,0:T(8,128)(2,1)}, bf16[8,48,1120]{2,1,0:T(8,128)(2,1)}, u32[]{:S(2)}, u32[]{:S(2)}) collective-permute-start(bf16[8,48,1120]{2,1,0:T(8,128)(2,1)} %get-tuple-element.81), channel_id=1, source_target_pairs={{0,1},{4,5},{8,9},{12,13},{16,17},{20,21},{24,25},{28,29}} | collective-permute-start | bytes 2580488 | tf_op jit(solution)/shard_map/ppermute | solution.py:244
  534.2 84.5 %collective-permute-start.47 = (bf16[8,48,1120]{2,1,0:T(8,128)(2,1)}, bf16[8,48,1120]{2,1,0:T(8,128)(2,1)}, u32[]{:S(2)}, u32[]{:S(2)}) collective-permute-start(bf16[8,48,1120]{2,1,0:T(8,128)(2,1)} %get-tuple-element.82), channel_id=1, source_target_pairs={{3,2},{7,6},{11,10},{15,14},{19,18},{23,22},{27,26},{31,30}} | collective-permute-start | bytes 2580488 | tf_op jit(solution)/shard_map/ppermute | solution.py:245
  557.5 57.6 %collective-permute-start.32 = (bf16[8,48,1120]{2,1,0:T(8,128)(2,1)}, bf16[8,48,1120]{2,1,0:T(8,128)(2,1)}, u32[]{:S(2)}, u32[]{:S(2)}) collective-permute-start(bf16[8,48,1120]{2,1,0:T(8,128)(2,1)} %get-tuple-element.85), channel_id=1, source_target_pairs={{0,1},{4,5},{8,9},{12,13},{16,17},{20,21},{24,25},{28,29}} | collective-permute-start | bytes 2580488 | tf_op jit(solution)/shard_map/ppermute | solution.py:244
  614.4 63.6 %collective-permute-start.59 = (bf16[280,1536]{1,0:T(8,128)(2,1)S(1)}, bf16[280,1536]{1,0:T(8,128)(2,1)S(1)}, u32[]{:S(2)}, u32[]{:S(2)}) collective-permute-start(bf16[280,1536]{1,0:T(8,128)(2,1)S(1)} %get-tuple-element.90), channel_id=1, source_target_pairs={{3,2},{7,6},{11,10},{15,14},{19,18},{23,22},{27,26},{31,30}} | collective-permute-start | bytes 2580488 | tf_op jit(solution)/shard_map/ppermute | solution.py:245
  620.6 51.2 %collective-permute-start.45 = (bf16[8,48,1120]{2,1,0:T(8,128)(2,1)S(1)}, bf16[8,48,1120]{2,1,0:T(8,128)(2,1)S(1)}, u32[]{:S(2)}, u32[]{:S(2)}) collective-permute-start(bf16[8,48,1120]{2,1,0:T(8,128)(2,1)S(1)} %get-tuple-element.79), channel_id=1, source_target_pairs={{0,1},{1,2},{4,5},{5,6},{8,9},{9,10},{12,13},{13,14},{16,17},{17,1... | collective-permute-start | bytes 2580488 | tf_op jit(solution)/shard_map/ppermute | solution.py:244
  634.8 55.4 %collective-permute-start.57 = (bf16[280,1536]{1,0:T(8,128)(2,1)S(1)}, bf16[280,1536]{1,0:T(8,128)(2,1)S(1)}, u32[]{:S(2)}, u32[]{:S(2)}) collective-permute-start(bf16[280,1536]{1,0:T(8,128)(2,1)S(1)} %add_convert_fusion.7), channel_id=1, source_target_pairs={{0,1},{1,2},{4,5},{5,6},{8,9},{9,10},{12,13},{13,14},{16,17},{17,1... | collective-permute-start | bytes 2580488 | tf_op jit(solution)/shard_map/ppermute | solution.py:244
  654.2 44.3 %collective-permute-start.36 = (bf16[8,48,1120]{2,1,0:T(8,128)(2,1)S(1)}, bf16[8,48,1120]{2,1,0:T(8,128)(2,1)S(1)}, u32[]{:S(2)}, u32[]{:S(2)}) collective-permute-start(bf16[8,48,1120]{2,1,0:T(8,128)(2,1)S(1)} %get-tuple-element.84), channel_id=1, source_target_pairs={{3,2},{2,1},{7,6},{6,5},{11,10},{10,9},{15,14},{14,13},{19,18},{18... | collective-permute-start | bytes 2580488 | tf_op jit(solution)/shard_map/ppermute | solution.py:245
  726.9 40.9 %collective-permute-start.50 = (bf16[8,48,1120]{2,1,0:T(8,128)(2,1)}, bf16[8,48,1120]{2,1,0:T(8,128)(2,1)}, u32[]{:S(2)}, u32[]{:S(2)}) collective-permute-start(bf16[8,48,1120]{2,1,0:T(8,128)(2,1)} %all-to-all-done.2), channel_id=1, source_target_pairs={{3,2},{2,1},{1,0},{7,6},{6,5},{5,4},{11,10},{10,9},{9,8},{15,14},{... | collective-permute-start | bytes 2580488 | tf_op jit(solution)/shard_map/ppermute | solution.py:257
  728.2 40.9 %collective-permute-start.53 = (bf16[8,48,1120]{2,1,0:T(8,128)(2,1)}, bf16[8,48,1120]{2,1,0:T(8,128)(2,1)}, u32[]{:S(2)}, u32[]{:S(2)}) collective-permute-start(bf16[8,48,1120]{2,1,0:T(8,128)(2,1)} %all-to-all-done.2), channel_id=1, source_target_pairs={{0,1},{1,2},{2,3},{4,5},{5,6},{6,7},{8,9},{9,10},{10,11},{12,13},{... | collective-permute-start | bytes 2580488 | tf_op jit(solution)/shard_map/ppermute | solution.py:256
  742.0 167.4 %reduce-scatter.8.cloned.1.call-start = ((), (), s32[]{:S(2)}) async-start(), calls=%async_computation.12 | async-start | bytes 5308416 | tf_op jit(solution)/shard_map/reduce_scatter | solution.py:400
  751.6 54.7 %collective-permute-start.65 = (bf16[280,1536]{1,0:T(8,128)(2,1)}, bf16[280,1536]{1,0:T(8,128)(2,1)}, u32[]{:S(2)}, u32[]{:S(2)}) collective-permute-start(bf16[280,1536]{1,0:T(8,128)(2,1)} %add_convert_fusion.3), channel_id=1, source_target_pairs={{0,1},{1,2},{2,3},{4,5},{5,6},{6,7},{8,9},{9,10},{10,11},{12,13},{... | collective-permute-start | bytes 2580488 | tf_op jit(solution)/shard_map/ppermute | solution.py:256
  769.1 40.1 %collective-permute-start.54 = (bf16[8,48,1120]{2,1,0:T(8,128)(2,1)}, bf16[8,48,1120]{2,1,0:T(8,128)(2,1)}, u32[]{:S(2)}, u32[]{:S(2)}) collective-permute-start(bf16[8,48,1120]{2,1,0:T(8,128)(2,1)} %collective-permute-done.53), channel_id=1, source_target_pairs={{1,2},{2,3},{5,6},{6,7},{9,10},{10,11},{13,14},{14,15},{17,18},{18... | collective-permute-start | bytes 2580488 | tf_op jit(solution)/shard_map/ppermute | solution.py:256
  770.7 52.5 %collective-permute-start.38 = (bf16[8,48,1120]{2,1,0:T(8,128)(2,1)S(1)}, bf16[8,48,1120]{2,1,0:T(8,128)(2,1)}, u32[]{:S(2)}, u32[]{:S(2)}) collective-permute-start(bf16[8,48,1120]{2,1,0:T(8,128)(2,1)S(1)} %all-to-all-done.1), channel_id=1, source_target_pairs={{3,2},{2,1},{1,0},{7,6},{6,5},{5,4},{11,10},{10,9},{9,8},{15,14},{... | collective-permute-start | bytes 2580488 | tf_op jit(solution)/shard_map/ppermute | solution.py:257
  809.2 51.3 %collective-permute-start.52 = (bf16[8,48,1120]{2,1,0:T(8,128)(2,1)}, bf16[8,48,1120]{2,1,0:T(8,128)(2,1)S(1)}, u32[]{:S(2)}, u32[]{:S(2)}) collective-permute-start(bf16[8,48,1120]{2,1,0:T(8,128)(2,1)} %collective-permute-done.51), channel_id=1, source_target_pairs={{1,0},{5,4},{9,8},{13,12},{17,16},{21,20},{25,24},{29,28}} | collective-permute-start | bytes 2580488 | tf_op jit(solution)/shard_map/ppermute | solution.py:257
  824.8 55.0 %collective-permute-start.39 = (bf16[8,48,1120]{2,1,0:T(8,128)(2,1)}, bf16[8,48,1120]{2,1,0:T(8,128)(2,1)}, u32[]{:S(2)}, u32[]{:S(2)}) collective-permute-start(bf16[8,48,1120]{2,1,0:T(8,128)(2,1)} %collective-permute-done.38), channel_id=1, source_target_pairs={{2,1},{1,0},{6,5},{5,4},{10,9},{9,8},{14,13},{13,12},{18,17},{17,1... | collective-permute-start | bytes 2580488 | tf_op jit(solution)/shard_map/ppermute | solution.py:257
  843.2 54.8 %collective-permute-start.64 = (bf16[280,1536]{1,0:T(8,128)(2,1)}, bf16[280,1536]{1,0:T(8,128)(2,1)}, u32[]{:S(2)}, u32[]{:S(2)}) collective-permute-start(bf16[280,1536]{1,0:T(8,128)(2,1)} %collective-permute-done.63), channel_id=1, source_target_pairs={{1,0},{5,4},{9,8},{13,12},{17,16},{21,20},{25,24},{29,28}} | collective-permute-start | bytes 2580488 | tf_op jit(solution)/shard_map/ppermute | solution.py:257
  879.8 45.1 %collective-permute-start.40 = (bf16[8,48,1120]{2,1,0:T(8,128)(2,1)}, bf16[8,48,1120]{2,1,0:T(8,128)(2,1)S(1)}, u32[]{:S(2)}, u32[]{:S(2)}) collective-permute-start(bf16[8,48,1120]{2,1,0:T(8,128)(2,1)} %collective-permute-done.39), channel_id=1, source_target_pairs={{1,0},{5,4},{9,8},{13,12},{17,16},{21,20},{25,24},{29,28}} | collective-permute-start | bytes 2580488 | tf_op jit(solution)/shard_map/ppermute | solution.py:257
  881.1 44.7 %collective-permute-start.43 = (bf16[8,48,1120]{2,1,0:T(8,128)(2,1)}, bf16[8,48,1120]{2,1,0:T(8,128)(2,1)}, u32[]{:S(2)}, u32[]{:S(2)}) collective-permute-start(bf16[8,48,1120]{2,1,0:T(8,128)(2,1)} %collective-permute-done.42), channel_id=1, source_target_pairs={{2,3},{6,7},{10,11},{14,15},{18,19},{22,23},{26,27},{30,31}} | collective-permute-start | bytes 2580488 | tf_op jit(solution)/shard_map/ppermute | solution.py:256
  989.4 52.2 %collective-permute-start.27 = (bf16[48,3584]{1,0:T(8,128)(2,1)S(1)}, bf16[48,3584]{1,0:T(8,128)(2,1)S(1)}, u32[]{:S(2)}, u32[]{:S(2)}) collective-permute-start(bf16[48,3584]{1,0:T(8,128)(2,1)S(1)} %collective-permute-done.26), channel_id=1, source_target_pairs={{2,1},{1,0},{6,5},{5,4},{10,9},{9,8},{14,13},{13,12},{18,17},{17,1... | collective-permute-start | bytes 1032200 | tf_op jit(solution)/shard_map/ppermute | solution.py:257
  990.7 52.2 %collective-permute-start.30 = (bf16[48,3584]{1,0:T(8,128)(2,1)S(1)}, bf16[48,3584]{1,0:T(8,128)(2,1)S(1)}, u32[]{:S(2)}, u32[]{:S(2)}) collective-permute-start(bf16[48,3584]{1,0:T(8,128)(2,1)S(1)} %collective-permute-done.29), channel_id=1, source_target_pairs={{1,2},{2,3},{5,6},{6,7},{9,10},{10,11},{13,14},{14,15},{17,18},{18... | collective-permute-start | bytes 1032200 | tf_op jit(solution)/shard_map/ppermute | solution.py:256
  (110 other events, 2625.6 us)
Sparse Core Ops, SparseCore 0:
  10.5 26.9 all-gather.8
  39.3 51.9 all-gather.6
  92.9 37.0 all-gather.10
  131.8 67.2 all-gather.12
  527.2 58.6 reduce-scatter.3
  596.3 63.4 reduce-scatter.5
  778.4 78.0 reduce-scatter.7

commit v2 on v1

v2 whole, which is shorter than its diff:
```python
import functools

import jax
import jax.numpy as jnp
from jax import lax
from jax.experimental import pallas as pl
from jax.experimental.pallas import tpu as pltpu
from jax.sharding import PartitionSpec as P

H = 12
KVH = 2
HD = 128
HEADS_STEP = 2
LANES = 128


EPS = 1e-06
THETA = 1000000.0
BF = jnp.bfloat16
F32 = jnp.float32


def rotary_tables(positions):
    half_width = HD // 2
    inverse = THETA ** (-(jnp.arange(half_width, dtype=F32) * 2.0) / HD)
    angles = positions.astype(F32)[:, None] * inverse[None, :]
    cosine, sine = jnp.cos(angles), jnp.sin(angles)
    return (
        jnp.concatenate([cosine, cosine], axis=-1),
        jnp.concatenate([-sine, sine], axis=-1),
    )


def swap_halves(values):
    half_width = HD // 2
    return jnp.concatenate([values[..., half_width:], values[..., :half_width]], axis=-1)


def stream_positions(order_row, first_row, row_count, block_size):
    row_ids = first_row + jnp.arange(row_count, dtype=jnp.int32)
    which_block = row_ids // block_size
    matches = jnp.arange(order_row.shape[0], dtype=jnp.int32)[None, :] == which_block[:, None]
    block_start = jnp.sum(jnp.where(matches, order_row[None, :], 0), axis=1)
    return block_start * block_size + row_ids % block_size


def norm_backward(normed_grad, unit_rows, gain_rows, scale_rows):
    gain_grad = jnp.sum(normed_grad * unit_rows, axis=0)
    scaled = normed_grad * gain_rows
    inner = jnp.mean(scaled * unit_rows, axis=-1, keepdims=True)
    return (gain_grad, scale_rows * (scaled - unit_rows * inner))


def contract_last(left, right):
    return lax.dot_general(left, right, (((1,), (1,)), ((), ())), preferred_element_type=F32)


def contract_first(left, right):
    return lax.dot_general(left, right, (((0,), (0,)), ((), ())), preferred_element_type=F32)


def product(left, right):
    return jnp.dot(left, right, preferred_element_type=F32)


def head_scores(query, keys, allowed):
    scores = contract_last(query, keys) * (HD ** (-0.5))
    scores = jnp.where(allowed, scores, -1e30)
    weights_exp = jnp.exp(scores - jnp.max(scores, axis=-1, keepdims=True))
    return weights_exp, 1.0 / jnp.sum(weights_exp, axis=-1, keepdims=True)


def attend_forward_kernel(
    query_lin, keys, values, cosine, signed_sine, query_pos, key_pos, query_rot, mixed
):
    allowed = key_pos[...] <= query_pos[...]
    for head in range(HEADS_STEP):
        columns = slice(head * HD, (head + 1) * HD)
        linear = query_lin[:, columns]
        rotated = linear * cosine[...] + pltpu.roll(linear, HD // 2, 1) * signed_sine[...]
        rotated = rotated.astype(BF)
        query_rot[:, columns] = rotated
        weights_exp, inverse_sum = head_scores(rotated, keys[...], allowed)
        probabilities = (weights_exp * inverse_sum).astype(BF)
        mixed[:, columns] = product(probabilities, values[...]).astype(BF)


def attend_forward(query_lin, keys_values, cosine, signed_sine, query_pos, key_pos):
    rows, width = query_lin.shape
    count_all = keys_values.shape[0]
    per_kv = H // KVH // HEADS_STEP
    wide = HEADS_STEP * HD
    table = pl.BlockSpec((rows, HD), lambda step: (0, 0))
    by_head = pl.BlockSpec((rows, wide), lambda step: (0, step))
    return pl.pallas_call(
        attend_forward_kernel,
        grid=(H // HEADS_STEP,),
        in_specs=[
            by_head,
            pl.BlockSpec((count_all, HD), lambda step: (0, step // per_kv)),
            pl.BlockSpec((count_all, HD), lambda step: (0, KVH + step // per_kv)),
            table,
            table,
            pl.BlockSpec((rows, 1), lambda step: (0, 0)),
            pl.BlockSpec((1, count_all), lambda step: (0, 0)),
        ],
        out_specs=[by_head, by_head],
        out_shape=[jax.ShapeDtypeStruct((rows, width), BF)] * 2,
        compiler_params=pltpu.CompilerParams(vmem_limit_bytes=48 * 1024 * 1024),
        cost_estimate=pl.CostEstimate(
            flops=4 * rows * count_all * width,
            bytes_accessed=8 * rows * width + 2 * keys_values.size,
            transcendentals=H * rows * count_all,
        ),
    )(query_lin, keys_values, keys_values, cosine, signed_sine, query_pos, key_pos)


def attend_backward_kernel(
    query_rot, out_grad, keys, values, cosine, signed_sine, query_pos, key_pos, query_grad, pair_grad, key_sum, value_sum
):
    step = pl.program_id(0)
    allowed = key_pos[...] <= query_pos[...]
    scaling = HD ** (-0.5)

    @pl.when(step == 0)
    def _():
        key_sum[...] = jnp.zeros_like(key_sum)
        value_sum[...] = jnp.zeros_like(value_sum)

    for head in range(HEADS_STEP):
        columns = slice(head * HD, (head + 1) * HD)
        query = query_rot[:, columns]
        grad = out_grad[:, columns]
        weights_exp, inverse_sum = head_scores(query, keys[...], allowed)
        probabilities = weights_exp * inverse_sum
        prob_grad = contract_last(grad, values[...])
        weighted = jnp.sum(probabilities * prob_grad, axis=-1, keepdims=True)
        score_grad = (probabilities * (prob_grad - weighted)).astype(BF)
        turned = product(score_grad, keys[...]) * scaling
        turned = turned * cosine[...] - pltpu.roll(turned, HD // 2, 1) * signed_sine[...]
        query_grad[:, columns] = turned.astype(BF)
        key_sum[...] += contract_first(score_grad, query) * scaling
        value_sum[...] += contract_first(probabilities.astype(BF), grad)

    @pl.when(step == pl.num_programs(0) - 1)
    def _():
        pair_grad[:, :HD] = key_sum[...].astype(BF)
        pair_grad[:, HD:] = value_sum[...].astype(BF)


def attend_backward(earlier, number, query_rot, out_grad, keys_values, cosine, signed_sine, query_pos, key_pos):
    rows = query_rot.shape[0]
    count_all = keys_values.shape[0]
    per_kv = H // KVH // HEADS_STEP
    wide = HEADS_STEP * HD
    table = pl.BlockSpec((rows, HD), lambda step: (0, 0))
    by_head = pl.BlockSpec((rows, wide), lambda step: (0, number * per_kv + step))
    in_specs = [
        by_head,
        by_head,
        pl.BlockSpec((count_all, HD), lambda step: (0, number)),
        pl.BlockSpec((count_all, HD), lambda step: (0, KVH + number)),
        table,
        table,
        pl.BlockSpec((rows, 1), lambda step: (0, 0)),
        pl.BlockSpec((1, count_all), lambda step: (0, 0)),
    ]
    out_specs = [
        pl.BlockSpec((rows, wide), lambda step: (0, step)),
        pl.BlockSpec((count_all, 2 * HD), lambda step: (0, 0)),
    ]
    out_shape = [
        jax.ShapeDtypeStruct((rows, per_kv * wide), BF),
        jax.ShapeDtypeStruct((count_all, 2 * HD), BF),
    ]
    operands = (query_rot, out_grad, keys_values, keys_values, cosine, signed_sine, query_pos, key_pos)
    scratch = [pltpu.VMEM((count_all, HD), F32)] * 2
    call = ordered_call(
        attend_backward_kernel, operands, in_specs, out_specs, out_shape, earlier, (per_kv,), scratch=scratch, vmem=48
    )
    return call(*operands, *earlier)


def chunk_widths(hidden_width):
    first = max(LANES, hidden_width // (2 * LANES) * LANES)
    return [first, hidden_width - first]


def round_up(value, step):
    return (value + step - 1) // step * step


def cut_kernel(gate, up, *outputs, hidden_width, widths):
    count = gate.shape[1] // hidden_width
    for owner in range(count):
        column = owner * hidden_width
        for out, wide in zip(outputs, widths):
            padded = round_up(wide, LANES)
            first = column // LANES * LANES
            shift = column - first
            span = round_up(shift + wide, LANES)
            for half, source in enumerate((gate, up)):
                part = source[:, first : first + span].astype(F32)
                if shift:
                    part = pltpu.roll(part, span - shift, 1)
                if span < padded:
                    part = jnp.concatenate([part, jnp.zeros((part.shape[0], padded - span), F32)], axis=1)
                part = part[:, :padded]
                if wide < padded:
                    lane = lax.broadcasted_iota(jnp.int32, part.shape, 1)
                    part = jnp.where(lane < wide, part, 0.0)
                out[owner, :, half * padded : (half + 1) * padded] = part.astype(BF)
            column += wide


def cut_gate_up(w_gate, w_up, hidden_width, widths):
    rows, total = w_gate.shape
    count = total // hidden_width
    return pl.pallas_call(
        functools.partial(cut_kernel, hidden_width=hidden_width, widths=widths),
        out_shape=[jax.ShapeDtypeStruct((count, rows, 2 * round_up(wide, LANES)), BF) for wide in widths],
        compiler_params=pltpu.CompilerParams(vmem_limit_bytes=48 * 1024 * 1024),
        cost_estimate=pl.CostEstimate(flops=4 * w_gate.size, bytes_accessed=8 * w_gate.size, transcendentals=0),
    )(w_gate, w_up)


def swap_fsdp(values, mask):
    count = lax.axis_size("fsdp")
    return lax.ppermute(values, "fsdp", [(i, i ^ mask) for i in range(count)])


def after(value, *others):
    return lax.optimization_barrier((value,) + others)[0]


def place_kernel(index, *refs, sizes):
    count = len(sizes)
    pieces, out, semaphores = refs[:count], refs[count], refs[count + 1]
    copies = []
    for number, (mask, first, size) in enumerate(sizes):
        start = jnp.bitwise_xor(index[0], mask) * (out.shape[0] // 8) + first
        target = out.at[pl.ds(pl.multiple_of(start, 16), size)]
        copies.append(pltpu.make_async_copy(pieces[number], target, semaphores.at[number]))
        copies[-1].start()
    for copy in copies:
        copy.wait()


def place_parts(parts, index):
    rows = sum(part.shape[0] for _, _, part in parts)
    columns, dtype = parts[0][2].shape[1], parts[0][2].dtype
    sizes = [(mask, first, part.shape[0]) for mask, first, part in parts]
    anywhere = pl.BlockSpec(memory_space=pl.ANY)
    return pl.pallas_call(
        functools.partial(place_kernel, sizes=sizes),
        in_specs=[pl.BlockSpec(memory_space=pltpu.SMEM)] + [anywhere] * len(parts),
        out_specs=pl.BlockSpec(memory_space=pltpu.VMEM),
        out_shape=jax.ShapeDtypeStruct((rows, columns), dtype),
        scratch_shapes=[pltpu.SemaphoreType.DMA((len(parts),))],
        compiler_params=pltpu.CompilerParams(vmem_limit_bytes=32 * 1024 * 1024),
        cost_estimate=pl.CostEstimate(flops=0, bytes_accessed=4 * rows * columns, transcendentals=0),
    )(index, *(part for _, _, part in parts))


def gather_rows(rows, index, *earlier):
    if lax.axis_size("fsdp") != 8:
        return lax.all_gather(rows, "fsdp", axis=0, tiled=True), (rows,), (rows,)
    size = rows.shape[0]
    half = size // 2
    rows = after(rows, *earlier)
    from_x = swap_fsdp(rows, 2)
    from_y = swap_fsdp(rows, 4)
    far_first = swap_fsdp(from_y[:half], 2)
    far_last = swap_fsdp(from_x[half:], 4)
    parts = []
    for mask, first, part in ((0, 0, rows), (2, 0, from_x), (4, 0, from_y), (6, 0, far_first), (6, half, far_last)):
        parts.append((mask, first, part))
        parts.append((mask ^ 1, first, swap_fsdp(part, 1)))
    return place_parts(parts, index), (from_x, from_y), (far_first, far_last)


def gather_small(rows, index):
    if lax.axis_size("fsdp") != 8:
        return lax.all_gather(rows, "fsdp", axis=0, tiled=True), (rows,)
    found = [(mask, rows if mask == 0 else swap_fsdp(rows, mask)) for mask in (0, 2, 4, 6)]
    parts = [(mask, 0, part) for mask, part in found]
    parts += [(mask ^ 1, 0, swap_fsdp(part, 1)) for mask, part in found]
    return place_parts(parts, index), tuple(part for _, part in found)


COVER = 10**12


def ordered_call(kernel, operands, in_specs, out_specs, out_shape, earlier, grid=(), scalars=0, scratch=(), vmem=16):
    count = scalars + len(operands)

    def body(*refs):
        kernel(*refs[:count], *refs[count + len(earlier) :])

    return pl.pallas_call(
        body,
        grid_spec=pltpu.PrefetchScalarGridSpec(
            num_scalar_prefetch=scalars,
            grid=grid,
            in_specs=list(in_specs) + [pl.BlockSpec(memory_space=pl.ANY)] * len(earlier),
            out_specs=out_specs,
            scratch_shapes=scratch,
        ),
        out_shape=out_shape,
        compiler_params=pltpu.CompilerParams(vmem_limit_bytes=vmem * 1024 * 1024),
        cost_estimate=pl.CostEstimate(flops=COVER, bytes_accessed=1024, transcendentals=0),
    )


def spacer_kernel(out):
    out[...] = jnp.zeros_like(out)


def spacer(earlier):
    out_shape = jax.ShapeDtypeStruct((8, LANES), F32)
    return ordered_call(spacer_kernel, (), [], pl.BlockSpec(memory_space=pltpu.VMEM), out_shape, earlier)(*earlier)


class Line:
    def __init__(self, ready):
        self.ready = ready
        self.marks = []
        self.last = ()

    def kernel(self, call, *arrived):
        found = call(self.last + arrived)
        self.last = (jax.tree.leaves(found)[0],)
        return found

    def step(self, work, *arrived):
        ready = self.ready
        arrived = self.last + arrived

        def marked():
            return work(), [array[(0,) * (array.ndim - 1)][:1] for array in arrived]

        shapes = jax.eval_shape(marked)

        def skip():
            return jnp.logical_not(ready), jax.tree.map(lambda leaf: jnp.zeros(leaf.shape, leaf.dtype), shapes)

        self.ready, (found, marks) = lax.cond(ready, lambda: (ready, marked()), skip)
        self.marks += marks
        self.last = (jax.tree.leaves(found)[0],)
        self.kernel(spacer)
        return found


def add_kernel(left, right, out):
    out[...] = (left[...].astype(F32) + right[...].astype(F32)).astype(BF)


def add_low(earlier, left, right):
    shape = left.shape
    columns = shape[-1]
    left, right = left.reshape(-1, columns), right.reshape(-1, columns)
    total = left.shape[0]
    rows = next(size for size in (768, 512, 384, 256, 192, 128, 64, 32, 16, total) if total % size == 0)
    block = pl.BlockSpec((rows, columns), lambda step: (step, 0))
    out_shape = jax.ShapeDtypeStruct(left.shape, BF)
    call = ordered_call(add_kernel, (left, right), [block] * 2, block, out_shape, earlier, (total // rows,), vmem=32)
    return call(left, right, *earlier).reshape(shape)


def split_kernel(same, other, own, to_x, to_y, far_first, far_last):
    rows = own.shape[0]
    half = rows // 2
    for first, out in ((0, own), (rows, to_x), (2 * rows, to_y), (3 * rows, far_first), (3 * rows + half, far_last)):
        size = out.shape[0]
        left, right = same[first : first + size], other[first : first + size]
        out[...] = (left.astype(F32) + right.astype(F32)).astype(BF)


def far_masks(other):
    return (1, 3, 5, 7) if other else (0, 2, 4, 6)


def pick_shards(partial, other):
    if partial.shape[0] != 8:
        return partial.reshape(-1, partial.shape[2])
    index = lax.axis_index("fsdp")
    parts = [lax.dynamic_index_in_dim(partial, index ^ mask, 0, keepdims=False) for mask in far_masks(other)]
    return jnp.concatenate(parts, axis=0)


def from_core(other):
    return swap_fsdp(other, 1) if lax.axis_size("fsdp") == 8 else other


def split_sum(earlier, same, moved):
    if lax.axis_size("fsdp") != 8:
        return [lax.psum_scatter(same, "fsdp", scatter_dimension=0, tiled=True)]
    rows, columns = same.shape[0] // 4, same.shape[1]
    sizes = (rows, rows, rows, rows // 2, rows // 2)
    whole = pl.BlockSpec(memory_space=pltpu.VMEM)
    out_shape = [jax.ShapeDtypeStruct((size, columns), BF) for size in sizes]
    call = ordered_call(split_kernel, (same, moved), [whole] * 2, [whole] * 5, out_shape, earlier, vmem=32)
    return call(same, moved, *earlier)


def from_far(begun):
    return [swap_fsdp(begun[3], 2), swap_fsdp(begun[4], 4)] if len(begun) == 5 else begun


def mix_kernel(to_x, to_y, by_x, by_y, out_x, out_y):
    half = by_x.shape[0]
    out_x[:half] = to_x[:half]
    out_x[half:] = (to_x[half:].astype(F32) + by_y[...].astype(F32)).astype(BF)
    out_y[:half] = (to_y[:half].astype(F32) + by_x[...].astype(F32)).astype(BF)
    out_y[half:] = to_y[half:]


def mix_sum(earlier, begun, moved):
    if len(begun) != 5:
        return begun
    own, to_x, to_y = begun[:3]
    whole = pl.BlockSpec(memory_space=pltpu.VMEM)
    out_shape = [jax.ShapeDtypeStruct(to_x.shape, BF)] * 2
    operands = (to_x, to_y, *moved)
    call = ordered_call(mix_kernel, operands, [whole] * 4, [whole] * 2, out_shape, earlier, vmem=32)
    return [own] + list(call(*operands, *earlier))


def from_near(sent):
    return [sent[0], swap_fsdp(sent[1], 2), swap_fsdp(sent[2], 4)] if len(sent) == 3 else sent


def sum_kernel(*refs):
    total = refs[0][...].astype(F32)
    for part in refs[1:-1]:
        total = total + part[...].astype(F32)
    refs[-1][...] = total.astype(BF)


def sum_low(earlier, parts):
    whole = pl.BlockSpec(memory_space=pltpu.VMEM)
    out_shape = jax.ShapeDtypeStruct(parts[0].shape, BF)
    call = ordered_call(sum_kernel, tuple(parts), [whole] * len(parts), whole, out_shape, earlier, vmem=32)
    return call(*parts, *earlier)


def sum_parts(parts):
    total = parts[0].astype(F32)
    for part in parts[1:]:
        total = total + part.astype(F32)
    return total


def to_middle(values):
    return lax.ppermute(values, "sp", [(0, 1), (3, 2)])


def across_middle(values):
    return lax.ppermute(values, "sp", [(1, 2), (2, 1)])


def to_ends(values):
    return lax.ppermute(values, "sp", [(1, 0), (2, 3)])


def pick_sum(total, moved):
    place = lax.axis_index("sp")
    return jnp.where((place == 1) | (place == 2), total, moved)


def join_kernel(middle, *refs, hidden_width, widths):
    out = refs[-1]
    chunks = [refs[2 * n : 2 * n + 2] for n in range(len(widths))]
    total = out.shape[1]

    def fill(number):
        for owner in range(total // hidden_width):
            column = owner * hidden_width
            for chunk, wide in zip(chunks, widths):
                part = chunk[number][owner].astype(F32)
                first = column // LANES * LANES
                shift = column - first
                span = round_up(shift + wide, LANES)
                if span > part.shape[1]:
                    part = jnp.concatenate([part, jnp.zeros((part.shape[0], span - part.shape[1]), F32)], axis=1)
                if shift:
                    part = pltpu.roll(part, shift, 1)
                    lane = lax.broadcasted_iota(jnp.int32, (part.shape[0], LANES), 1)
                    head = jnp.where(lane >= shift, part[:, :LANES], out[:, first : first + LANES])
                    out[:, first : first + LANES] = head
                    if span > LANES:
                        out[:, first + LANES : first + span] = part[:, LANES:span]
                else:
                    out[:, first : first + span] = part[:, :span]
                column += wide

    @pl.when(middle[0] == 1)
    def _():
        fill(0)

    @pl.when(middle[0] == 0)
    def _():
        fill(1)


def join_columns(earlier, found, columns, hidden_width, widths):
    place = lax.axis_index("sp")
    middle = ((place == 1) | (place == 2)).astype(jnp.int32)[None]
    arrays = [part for chunk in found for part in chunk]
    count, total = arrays[0].shape[:2]
    rows = 16
    in_specs = [pl.BlockSpec(memory_space=pltpu.SMEM)]
    for wide, column in zip(widths, columns):
        block = pl.BlockSpec((count, rows, round_up(wide, LANES)), lambda block, column=column: (0, block, column))
        in_specs += [block, block]
    out_specs = pl.BlockSpec((rows, count * hidden_width), lambda block: (block, 0))
    out_shape = jax.ShapeDtypeStruct((total, count * hidden_width), F32)
    operands = (middle, *arrays)
    kernel = functools.partial(join_kernel, hidden_width=hidden_width, widths=widths)
    call = ordered_call(kernel, operands, in_specs, out_specs, out_shape, earlier, (total // rows,), vmem=32)
    return call(*operands, *earlier)


def activate_kernel(normed, grad, weights, down, hidden_out, grads_out, *, first):
    padded = weights.shape[1] // 2
    rows = normed[...]
    gate = product(rows, weights[:, :padded])
    up = product(rows, weights[:, padded:])
    hidden_grad = contract_last(grad[...], down[first : first + padded])
    sigma = 1.0 / (1.0 + jnp.exp(-gate))
    activated = gate * sigma
    hidden_out[...] = (activated * up).astype(BF)
    grads_out[:, :padded] = (hidden_grad * up * (sigma * (1.0 + gate * (1.0 - sigma)))).astype(BF)
    grads_out[:, padded:] = (hidden_grad * activated).astype(BF)


def activate(earlier, normed, grad, weights, down, first):
    total, width = normed.shape
    wide = weights.shape[1] // 2
    rows = 256
    by_rows = pl.BlockSpec((rows, width), lambda step: (step, 0))
    in_specs = [
        by_rows,
        by_rows,
        pl.BlockSpec(weights.shape, lambda step: (0, 0)),
        pl.BlockSpec(down.shape, lambda step: (0, 0)),
    ]
    out_specs = [pl.BlockSpec((rows, wide * n), lambda step: (step, 0)) for n in (1, 2)]
    out_shape = [jax.ShapeDtypeStruct((total, wide * n), BF) for n in (1, 2)]
    operands = (normed, grad, weights, down)
    kernel = functools.partial(activate_kernel, first=first)
    call = ordered_call(kernel, operands, in_specs, out_specs, out_shape, earlier, (total // rows,), vmem=56)
    return call(*operands, *earlier)


def back_kernel(order, grads_1, grads_2, weights_1, weights_2, out):
    total = contract_last(grads_1[...], weights_1[...]) + contract_last(grads_2[...], weights_2[...])
    out[...] = total.astype(BF)


def branch_kernel(order, hidden_1, hidden_2, down, out):
    first = hidden_1.shape[1]
    total = product(hidden_1[...], down[:first]) + product(hidden_2[...], down[first:])
    out[...] = total.astype(BF)


def row_products(earlier, kernel, lefts, rights, order, rows, width):
    blocks = order.shape[0]
    in_specs = [pl.BlockSpec((rows, part.shape[1]), lambda step, order_ref: (order_ref[step], 0)) for part in lefts]
    in_specs += [pl.BlockSpec(part.shape, lambda step, order_ref: (0, 0)) for part in rights]
    out_specs = pl.BlockSpec((rows, width), lambda step, order_ref: (step, 0))
    out_shape = jax.ShapeDtypeStruct((blocks * rows, width), BF)
    operands = (*lefts, *rights)
    call = ordered_call(kernel, operands, in_specs, out_specs, out_shape, earlier, (blocks,), scalars=1, vmem=56)
    return call(order, *operands, *earlier)


def per_device(
    tokens,
    cotangent,
    seq_lengths,
    block_order,
    w_query,
    w_key,
    w_value,
    b_query,
    b_key,
    b_value,
    w_output,
    gain_attn,
    gain_mlp,
    w_gate,
    w_up,
    w_down,
):
    local_rows, width = tokens.shape
    sp_count = lax.axis_size("sp")
    sp_index = lax.axis_index("sp")
    fsdp_count = lax.axis_size("fsdp")
    group_rows = local_rows * sp_count
    block_rows = local_rows // 2
    query_width = H * HD
    key_width = KVH * HD
    hidden_all = w_gate.shape[1]
    hidden_width = hidden_all // fsdp_count
    shard_rows = w_gate.shape[0]
    widths = chunk_widths(hidden_width)

    vector_parts = [b_query, b_key, b_value, gain_attn, gain_mlp]
    vector_sizes = [part.shape[0] for part in vector_parts]
    vector_size = sum(vector_sizes)
    kv_columns = 2 * key_width
    vector_rows = round_up(-(-vector_size // kv_columns), 16)
    vector_pad = jnp.zeros((vector_rows * kv_columns - vector_size,), BF)
    kv_shard = jnp.concatenate(
        [
            jnp.concatenate([w_key, w_value], axis=1),
            jnp.concatenate(vector_parts + [vector_pad]).reshape(vector_rows, kv_columns),
        ],
        axis=0,
    )
    fsdp_index = lax.axis_index("fsdp")
    own_index = fsdp_index[None]
    kv_all, kv_hops = gather_small(kv_shard, own_index)
    kv_all = kv_all.reshape(fsdp_count, -1, kv_columns)
    w_kv = kv_all[:, :shard_rows].reshape(width, kv_columns)
    vectors = kv_all[:, shard_rows:].reshape(fsdp_count, -1).astype(F32)
    edges = [sum(vector_sizes[:n]) for n in range(len(vector_sizes) + 1)]
    bias_q, bias_k, bias_v, gain_one, gain_two = (
        vectors[:, edges[n] : edges[n + 1]].reshape(-1) for n in range(len(vector_sizes))
    )
    w_q, q_hops, q_far = gather_rows(w_query, own_index, *kv_hops)
    w_o, o_hops, o_far = gather_rows(w_output, own_index, *q_hops)

    cuts = cut_gate_up(w_gate, w_up, hidden_width, widths)

    def exchange(cut):
        return lax.all_to_all(cut, "fsdp", split_axis=0, concat_axis=0, tiled=True).reshape(width, -1)

    weights_first = exchange(after(cuts[0], *o_hops))

    order_row = block_order[0]
    local_pos = stream_positions(order_row, sp_index * local_rows, local_rows, block_rows)
    group_pos = stream_positions(order_row, 0, group_rows, block_rows)
    query_pos, key_pos = local_pos[:, None], group_pos[None, :]
    valid_rows = (local_pos < seq_lengths[0]).astype(F32)[:, None]
    upstream = cotangent.astype(F32)

    inputs = tokens.astype(F32)
    scale_one = lax.rsqrt(jnp.mean(inputs * inputs, axis=-1, keepdims=True) + EPS)
    unit_one = inputs * scale_one
    normed_one = (unit_one * gain_one).astype(BF)
    cosine, signed_sine = rotary_tables(local_pos)
    kv_lin = product(normed_one, w_kv)
    key_lin = kv_lin[:, :key_width] + bias_k
    key_rot = [
        (part * cosine + swap_halves(part) * signed_sine).astype(BF)
        for part in (key_lin[:, n * HD : (n + 1) * HD] for n in range(KVH))
    ]
    keys_values = jnp.concatenate(key_rot + [(kv_lin[:, key_width:] + bias_v).astype(BF)], axis=1)
    keys_values = lax.all_gather(keys_values, "sp", axis=0, tiled=True)
    query_lin = product(normed_one, w_q) + bias_q
    query_rot, mixed = attend_forward(query_lin, keys_values, cosine, signed_sine, query_pos, key_pos)
    attn_branch = product(mixed, w_o)
    hidden_in = inputs + valid_rows * attn_branch
    scale_two = lax.rsqrt(jnp.mean(hidden_in * hidden_in, axis=-1, keepdims=True) + EPS)
    unit_two = hidden_in * scale_two
    mlp_grad, grad_hops, grad_far = gather_rows((valid_rows * upstream).astype(BF), own_index, *o_far, weights_first)
    normed_two, two_hops, two_far = gather_rows((unit_two * gain_two).astype(BF), own_index)

    def rows_exchange(half):
        return lax.all_to_all(half, "fsdp", split_axis=0, concat_axis=0, tiled=True)

    def weight_term(left, right):
        return contract_first(left, right).astype(BF)

    def by_rows(term):
        return term.reshape(fsdp_count, shard_rows, -1)

    def block_order(other):
        if fsdp_count != 8:
            return jnp.arange(fsdp_count, dtype=jnp.int32)
        return jnp.array(far_masks(other), jnp.int32) ^ fsdp_index

    first_wide, last_wide = (round_up(wide, LANES) for wide in widths)
    down = jnp.pad(w_down, ((0, first_wide + last_wide - hidden_width), (0, 0)))
    weights_last = exchange(after(cuts[1], *grad_far, *two_far))
    both_weights = [weights_first, weights_last]
    order_other, order_same = block_order(True), block_order(False)
    line = Line(seq_lengths[0] > 0)

    def weight_step(left, right, rows=True):
        def work():
            term = weight_term(left, right)
            return by_rows(term) if rows else term

        return line.step(work)

    def add(left, right, *arrived):
        return line.kernel(lambda earlier: add_low(earlier, left, right), *arrived)

    def split(same, moved, *arrived):
        return line.kernel(lambda earlier: split_sum(earlier, same, moved), *arrived)

    def mix(begun, moved, *arrived):
        return line.kernel(lambda earlier: mix_sum(earlier, begun, moved), *arrived)

    def row_step(kernel, lefts, rights, order, *arrived):
        return line.kernel(
            lambda earlier: row_products(earlier, kernel, lefts, rights, order, local_rows, width), *arrived
        )

    hidden_1, grads_1 = line.kernel(lambda earlier: activate(earlier, normed_two, mlp_grad, weights_first, down, 0))
    def both_step(left, right, wide):
        def work():
            term = weight_term(left, right)
            return by_rows(term[:, :wide]), by_rows(term[:, wide:])

        return line.step(work)

    gate_term_1, up_term_1 = both_step(normed_two, grads_1, first_wide)
    gate_1_in, up_1_in = to_middle(gate_term_1), to_middle(up_term_1)
    hidden_2, grads_2 = line.kernel(
        lambda earlier: activate(earlier, normed_two, mlp_grad, weights_last, down, first_wide)
    )
    gate_2, up_2 = grads_2[:, :last_wide], grads_2[:, last_wide:]
    grads = [grads_1, grads_2]
    gate_1_sum = add(gate_term_1, gate_1_in)
    gate_1_across = across_middle(gate_1_sum)
    back_other = row_step(back_kernel, grads, both_weights, order_other)
    back_moved = from_core(back_other)
    back_same = row_step(back_kernel, grads, both_weights, order_same)
    back_begun = split(back_same, back_moved)
    back_far = from_far(back_begun)
    up_1_sum = add(up_term_1, up_1_in)
    up_1_across = across_middle(up_1_sum)
    gate_1_total = rows_exchange(add(gate_1_sum, gate_1_across))
    down_1 = weight_step(hidden_1, mlp_grad, False)
    down_1_in = to_middle(down_1)
    back_sent = mix(back_begun, back_far)
    back_parts = from_near(back_sent)
    down_2 = weight_step(hidden_2, mlp_grad, False)
    up_1_total = add(up_1_sum, up_1_across, gate_1_total)
    gate_1_ends = to_ends(gate_1_total)
    up_1_total = rows_exchange(up_1_total)
    down_2_in = to_middle(down_2)
    branch = row_step(branch_kernel, [hidden_1, hidden_2], [down], jnp.arange(fsdp_count, dtype=jnp.int32))
    branch = lax.psum_scatter(branch, "fsdp", scatter_dimension=0, tiled=True)

    def norm_step():
        gain_grad, back = norm_backward(sum_parts(back_parts), unit_two, gain_two, scale_two)
        hidden_in_grad = upstream + back
        attn_grad = (valid_rows * hidden_in_grad).astype(BF)
        return gain_grad, hidden_in_grad, attn_grad, contract_last(attn_grad, w_o).astype(BF)

    gain_two_grad, hidden_in_grad, attn_grad, mixed_grad = line.step(norm_step)

    def attend_step(number, *arrived):
        query_grad, pair = line.kernel(
            lambda earlier: attend_backward(
                earlier, number, query_rot, mixed_grad, keys_values, cosine, signed_sine, query_pos, key_pos
            ),
            *arrived,
        )
        return query_grad, pair.reshape(sp_count, local_rows, 2 * HD)

    def pair_exchange(pair):
        return lax.all_to_all(pair, "sp", split_axis=0, concat_axis=0, tiled=True)

    down_1_sum = add(down_1, down_1_in, up_1_total, gate_1_ends)
    down_1_across = across_middle(down_1_sum)
    up_1_ends = to_ends(up_1_total)
    query_grad_0, pair_0 = attend_step(0)

    def scatter_weight(term):
        return lax.psum_scatter(term, "fsdp", scatter_dimension=0, tiled=True)

    down_2_sum = add(down_2, down_2_in)
    down_2_across = across_middle(down_2_sum)
    gate_term_2 = weight_step(normed_two, gate_2)
    gate_2_in = to_middle(gate_term_2)
    down_1_total = add(down_1_sum, down_1_across, up_1_ends)
    down_1_ends = to_ends(down_1_total)
    query_grad_1, pair_1 = attend_step(1)
    pairs = pair_exchange(jnp.concatenate([pair_0, pair_1], axis=2))

    def kv_part(pair):
        pair_total = jnp.sum(pair.astype(F32), axis=0)
        part = pair_total[:, :HD]
        return (part * cosine - swap_halves(part) * signed_sine).astype(BF), pair_total[:, HD:].astype(BF)

    def query_step():
        query_lin_grad = jnp.concatenate([query_grad_0, query_grad_1], axis=1)
        sums = jnp.sum(query_lin_grad.astype(F32), axis=0)
        return weight_term(normed_one, query_lin_grad), contract_last(query_lin_grad, w_q), sums

    output_term = line.step(lambda: weight_term(mixed, attn_grad), branch)
    output_share = scatter_weight(output_term)
    query_term, normed_one_first, query_sums = line.step(query_step)
    query_share = scatter_weight(query_term)
    down_2_total = add(down_2_sum, down_2_across, down_1_ends)
    down_2_ends = to_ends(down_2_total)
    gate_2_sum = add(gate_term_2, gate_2_in)
    gate_2_across = across_middle(gate_2_sum)
    up_term_2 = weight_step(normed_two, up_2)
    up_2_in = to_middle(up_term_2)

    def kv_step():
        key_0, value_0 = kv_part(pairs[..., : 2 * HD])
        key_1, value_1 = kv_part(pairs[..., 2 * HD :])
        kv_lin_grad = jnp.concatenate([key_0, key_1, value_0, value_1], axis=1)
        normed_one_grad = normed_one_first + contract_last(kv_lin_grad, w_kv)
        gain_grad, back = norm_backward(normed_one_grad, unit_one, gain_one, scale_one)
        sums = jnp.sum(kv_lin_grad.astype(F32), axis=0)
        return weight_term(normed_one, kv_lin_grad), gain_grad, hidden_in_grad + back, sums

    kv_term, gain_one_grad, input_grad, kv_sums = line.step(kv_step)

    def last_rows(vector):
        return vector.reshape(fsdp_count, -1)

    extra_rows = 32

    marks = line.marks

    def pack_step():
        mlp_branch = branch.astype(F32)
        result = hidden_in + valid_rows * mlp_branch
        stat_parts = jnp.stack(
            [
                jnp.sum(valid_rows * result * result),
                jnp.sum(valid_rows * attn_branch * attn_branch),
                jnp.sum(valid_rows * mlp_branch * mlp_branch),
                jnp.sum(valid_rows),
            ]
        )
        vector_sums = jnp.concatenate(
            [
                last_rows(query_sums),
                last_rows(kv_sums[:key_width]),
                last_rows(kv_sums[key_width:]),
                last_rows(gain_one_grad),
                last_rows(gain_two_grad),
                jnp.broadcast_to(stat_parts[None, :], (fsdp_count, 4)),
                jnp.broadcast_to(jnp.concatenate(marks)[None, :].astype(F32), (fsdp_count, len(marks))),
            ],
            axis=1,
        ).astype(BF)
        extra = jnp.pad(vector_sums, ((0, 0), (0, extra_rows * kv_columns - vector_sums.shape[1])))
        packed = jnp.concatenate(
            [
                kv_term.reshape(fsdp_count, shard_rows, kv_columns),
                extra.reshape(fsdp_count, extra_rows, kv_columns),
            ],
            axis=1,
        )
        return packed.reshape(-1, kv_columns), result.astype(BF)

    packed, layer_out = line.step(pack_step)
    kv_share = scatter_weight(packed)
    gate_2_total = rows_exchange(add(gate_2_sum, gate_2_across, down_2_ends))
    up_2_sum = add(up_term_2, up_2_in)
    up_2_across = across_middle(up_2_sum)
    output_in = to_middle(output_share)

    def down_step():
        rows = [pick_sum(down_1_total, down_1_ends)[: widths[0]], pick_sum(down_2_total, down_2_ends)[: widths[1]]]
        return jnp.concatenate(rows, axis=0).astype(F32)

    grad_down = line.step(down_step, gate_2_total)
    gate_2_ends = to_ends(gate_2_total)
    output_sum = add(output_share, output_in)
    output_across = across_middle(output_sum)
    query_in = to_middle(query_share)
    up_2_total = rows_exchange(add(up_2_sum, up_2_across))
    kv_in = to_middle(kv_share)
    query_sum = add(query_share, query_in)
    query_across = across_middle(query_sum)
    output_total = add(output_sum, output_across)
    output_ends = to_ends(output_total)
    kv_sum = add(kv_share, kv_in, up_2_total)
    up_2_ends = to_ends(up_2_total)
    kv_across = across_middle(kv_sum)
    gate = (gate_1_total, gate_1_ends), (gate_2_total, gate_2_ends)
    up = (up_1_total, up_1_ends), (up_2_total, up_2_ends)
    query_total = add(query_sum, query_across)
    query_ends = to_ends(query_total)
    kv_total = add(kv_sum, kv_across)
    kv_ends = to_ends(kv_total)
    grad_gate = line.kernel(lambda earlier: join_columns(earlier, gate, (0, 0), hidden_width, widths))
    grad_up = line.kernel(lambda earlier: join_columns(earlier, up, (0, 0), hidden_width, widths))
    grad_output = pick_sum(output_total, output_ends).astype(F32)
    grad_query = pick_sum(query_total, query_ends).astype(F32)
    projections = pick_sum(kv_total, kv_ends).astype(F32)
    sums = projections[shard_rows:].reshape(-1)
    grad_b_query, grad_b_key, grad_b_value, grad_gain_one, grad_gain_two = (
        sums[edges[n] : edges[n + 1]] for n in range(len(vector_sizes))
    )
    stats = sums[edges[-1] : edges[-1] + 4]
    root_means = jnp.sqrt(stats[:3] / (stats[3] * width))

    return (
        layer_out,
        input_grad,
        grad_query,
        projections[:shard_rows, :key_width],
        projections[:shard_rows, key_width:],
        grad_b_query,
        grad_b_key,
        grad_b_value,
        grad_output,
        grad_gain_one,
        grad_gain_two,
        grad_gate,
        grad_up,
        grad_down,
        root_means,
    )


def solution(mesh):
    both, first = P(("fsdp", "sp"), None), P("fsdp", None)
    one = P("fsdp")
    in_specs = (both, both, one, first, first, first, first, one, one, one, first, one, one, first, first, first)
    out_specs = (both, both, first, first, first, one, one, one, first, one, one, first, first, first, P())
    return jax.shard_map(per_device, mesh=mesh, in_specs=in_specs, out_specs=out_specs, check_vma=False)
```

time: 1070 us -> 946 us (0.88)
  Pallas kernels: 52.1 us -> 268 us
  matrix products: 195 us -> 94.6 us
  waiting for transfers between devices: 330 us -> 270 us
  blocking collectives: 55.3 us -> 0 us
  local copies, waits for them, and re-layouts: 132 us -> 80.7 us
  other arithmetic: 106 us -> 60 us
  starting transfers between devices: 176 us -> 136 us
    pallas_call x1 -> x45, Pallas kernels: 32.7 us -> 248 us  [the longest x18 55.7 us: add_low(): return call(left, right, *earlier).reshape(shape)]
    ppermute x48 -> x27, starting transfers between devices: 142 us -> 70.5 us  [the longest x9 42.6 us: to_middle(): return lax.ppermute(values, 'sp', [(0, 1), (3, 2)])]
    dot_general x6 -> x3, matrix products: 76.2 us -> 13.3 us  [contract_last(): lax.dot_general(left, right, (((1,), (1,)), ((), ())), preferred_element_...]
    all_gather x3 -> x0, waiting for transfers between devices: 55.2 us -> none  [the longest x1 43.3 us: per_device(): w_o = lax.all_gather(w_output, 'fsdp', axis=0, tiled=True)]
    dot_general x6 -> x3, matrix products: 61.4 us -> 7.79 us  [product(): return jnp.dot(left, right, preferred_element_type=F32)]
    psum x1 -> x0, blocking collectives: 46.3 us -> none  [per_device(): lax.psum((jnp.sum(query_lin_grad.astype(F32), axis=0), jnp.sum(kv_lin_gra...]
    ppermute x20 -> x48, waiting for transfers between devices: 92.3 us -> 116 us  [swap_fsdp(): return lax.ppermute(values, 'fsdp', [(i, i ^ mask) for i in range(count)])]
    convert_element_type x25 -> x12, other arithmetic: 42.3 us -> 20 us  [the longest x1 6.16 us: norm_step(): attn_grad = (valid_rows * hidden_in_grad).astype(BF)]
  transfers between devices with their start and end apart: 78 -> 87, of which waited for: 31 -> 21; matrix products, arithmetic and copies ran while one was open for 27% -> 21% of each run, Pallas kernels for 2% -> 27%
where the time goes in v2:
time: 946 us; the launch traced here: 933 us
  waiting for transfers between devices  270 us (29%)
  Pallas kernels  268 us (28%)
  starting transfers between devices  136 us (14%)
  matrix products  94.6 us (10%)
  local copies, waits for them, and re-layouts  80.7 us (9%)
  other arithmetic  60 us (6%)
  between operations  16.7 us (2%)
    ppermute x9, waiting for transfers between devices, to_ends(): return lax.ppermute(values, 'sp', [(1, 0), (2, 3)])  125 us
    ppermute x48, waiting for transfers between devices, swap_fsdp(): return lax.ppermute(values, 'fsdp', [(i, i ^ mask) for i in range(count)])  116 us
    dot_general x8, matrix products, contract_first(): lax.dot_general(left, right, (((0,), (0,)), ((), ())), preferred_element_...  73.6 us
    pallas_call x18, Pallas kernels, add_low(): return call(left, right, *earlier).reshape(shape)  55.7 us
    pallas_call x3, Pallas kernels, row_products(): return call(order, *operands, *earlier)  52 us
    pallas_call x2, Pallas kernels, activate(): return call(*operands, *earlier)  51.9 us
    ppermute x9, starting transfers between devices, to_middle(): return lax.ppermute(values, 'sp', [(0, 1), (3, 2)])  42.6 us
    pallas_call x2, Pallas kernels, attend_backward(): return call(*operands, *earlier)  32.6 us
  transfers between devices with their start and end apart: 87, of which 21 were waited for; matrix products, arithmetic and copies ran while one was open for 21% of the time, Pallas kernels for 27%

profile of v2, /device:TPU:2, one launch (start us, length us, event | category | flops | bytes accessed | tf_op | source)
XLA Modules:
  0.0 933.3 jit_solution(12577384943005144971)
XLA Ops:
  45.5 19.3 %collective-permute-done.12.refs_6_ = bf16[96,1536]{1,0:T(8,128)(2,1)} collective-permute-done((bf16[96,1536]{1,0:T(8,128)(2,1)S(1)}, bf16[96,1536]{1,0:T(8,128)(2,1)}, u32[]{:S(2)}, u32[]{:S(2)}) %collective-permute-start.12) | collective-permute-done | bytes 294944 | tf_op jit(solution)/shard_map/ppermute | solution.py:229
  105.2 19.8 %shard_map.291 = (bf16[384,1536]{1,0:T(8,128)(2,1)S(1)}, bf16[384,1536]{1,0:T(8,128)(2,1)S(1)}) custom-call(f32[384,1536]{1,0:T(8,128)S(1)} %copy-done.30, bf16[1536,512]{1,0:T(8,128)(2,1)S(1)} %copy-done.23, bf16[1536,512]{1,0:T(8,128)(2,1)S(1)} %copy-done.23, f32[384,128]{1,0:T(8,128)} %get-tuple-element.1321.cosine.refs_4_, f32[384,128]{1,0:T(8,128)S(1)} %copy-done.56, ...), custom_call_target="tpu_custom_call" | custom-call | flops 3623878656 | bytes 6291456 | tf_op jit(solution)/shard_map/pallas_call | solution.py:95
  134.4 24.8 %collective-permute-done.28.refs_4_ = bf16[384,1536]{1,0:T(8,128)(2,1)} collective-permute-done((bf16[384,1536]{1,0:T(8,128)(2,1)S(1)}, bf16[384,1536]{1,0:T(8,128)(2,1)}, u32[]{:S(2)}, u32[]{:S(2)}) %collective-permute-start.28) | collective-permute-done | bytes 1179680 | tf_op jit(solution)/shard_map/ppermute | solution.py:229
  163.9 34.3 %collective-permute-done.30.refs_6_ = bf16[192,1536]{1,0:T(8,128)(2,1)S(1)} collective-permute-done((bf16[192,1536]{1,0:T(8,128)(2,1)S(1)}, bf16[192,1536]{1,0:T(8,128)(2,1)S(1)}, u32[]{:S(2)}, u32[]{:S(2)}) %collective-permute-start.30) | collective-permute-done | bytes 589856 | tf_op jit(solution)/shard_map/ppermute | solution.py:229
  250.8 22.6 %shard_map.296 = (bf16[3072,512]{1,0:T(8,128)(2,1)S(1)}, bf16[3072,1024]{1,0:T(8,128)(2,1)}) custom-call(bf16[3072,1536]{1,0:T(8,128)(2,1)} %shard_map.293.refs_0_, bf16[3072,1536]{1,0:T(8,128)(2,1)} %shard_map.295.refs_1_, bf16[1536,1024]{1,0:T(8,128)(2,1)} %bitcast.11.refs_2_.refs_3_, bf16[1152,1536]{1,0:T(8,128)(2,1)} %pad.8.refs_3_), custom_call_target="tpu_custom_call" | custom-call | flops 999999995904 | bytes 1024 | tf_op jit(solution)/shard_map/pallas_call | solution.py:553
  275.1 20.2 %conditional.46 = (pred[]{:T(512)}, bf16[8,192,512]{2,1,0:T(8,128)(2,1)}, bf16[8,192,512]{2,1,0:T(8,128)(2,1)}, bf16[1]{0:T(256)(128)(2,1)}, bf16[1536,512]{1,0:...) conditional(s32[]{:T(128)} %convert_element_type.288, pred[]{:T(512)} %gt.8, ...), branch_computations={%region_4.5_spmd.clone.clone, %region_5.6_spmd.clone.clone} | conditional | flops 9665249280 | bytes 31457332
  275.3 14.1 %convolution_convert_fusion.1 = bf16[1536,1024]{1,0:T(8,128)(2,1)S(1)} fusion(bf16[3072,1536]{1,0:T(8,128)(2,1)} %get-tuple-element.1207, bf16[3072,1024]{1,0:T(8,128)(2,1)} %get-tuple-element.1208), kind=kOutput, calls=%fused_computation.8 | convolution fusion | flops 9665249280 | bytes 18874368 | tf_op jit(solution)/shard_map/cond/branch_1_fun/dot_general | solution.py:59
  303.0 29.3 %shard_map.298 = (bf16[3072,640]{1,0:T(8,128)(2,1)}, bf16[3072,1280]{1,0:T(8,128)(2,1)}) custom-call(bf16[3072,1536]{1,0:T(8,128)(2,1)} %shard_map.293.refs_0_, bf16[3072,1536]{1,0:T(8,128)(2,1)} %shard_map.295.refs_1_, bf16[1536,1280]{1,0:T(8,128)(2,1)} %bitcast.13.refs_2_.refs_4_, bf16[1152,1536]{1,0:T(8,128)(2,1)} %pad.8.refs_3_, f32[8,128]{1,0:T(8,128)} %copy-done.35), custom_call_target="tpu_custom_call" | custom-call | flops 999999995904 | bytes 1024 | tf_op jit(solution)/shard_map/pallas_call | solution.py:553
  338.2 17.2 %shard_map.300.refs_5_ = bf16[1536,1536]{1,0:T(8,128)(2,1)} custom-call(s32[4]{0:T(128)} %broadcast_xor_fusion.refs_0_, bf16[3072,1024]{1,0:T(8,128)(2,1)} %get-tuple-element.805.refs_1_, bf16[3072,1280]{1,0:T(8,128)(2,1)} %get-tuple-element.816.refs_2_, bf16[1536,1024]{1,0:T(8,128)(2,1)} %bitcast.11.refs_2_.refs_3_, ...), custom_call_target="tpu_custom_call" | custom-call | flops 999999995904 | bytes 1024 | tf_op jit(solution)/shard_map/pallas_call | solution.py:575
  355.4 17.2 %shard_map.301.refs_0_.refs_2_ = bf16[1536,1536]{1,0:T(8,128)(2,1)} custom-call(s32[4]{0:T(128)} %multiply_xor_fusion.refs_0_, bf16[3072,1024]{1,0:T(8,128)(2,1)} %get-tuple-element.805.refs_1_, bf16[3072,1280]{1,0:T(8,128)(2,1)} %get-tuple-element.816.refs_2_, bf16[1536,1024]{1,0:T(8,128)(2,1)} %bitcast.11.refs_2_.refs_3_, ...), custom_call_target="tpu_custom_call" | custom-call | flops 999999995904 | bytes 1024 | tf_op jit(solution)/shard_map/pallas_call | solution.py:575
  384.5 12.6 %conditional.48 = (pred[]{:T(512)}, bf16[512,1536]{1,0:T(8,128)(2,1)}, bf16[1]{0:T(256)(128)(2,1)}) conditional(s32[]{:T(128)} %convert_element_type.367, pred[]{:T(512)} %get-tuple-element.1164, (bf16[3072,512]{1,0:T(8,128)(2,1)}, bf16[3072,1536]{1,0:T(8,128)(2,1)}, bf16[8,192,512]{2,1,0:T(8,128)(2,1)}, pred[]{:T(512)}) %tuple.541), branch_computations={%region_6.7_spmd.clone.clone, %region_7.8_spmd.clone.clone} | conditional | flops 4832624640 | bytes 14155804
  384.9 10.3 %convolution_convert_fusion.2 = bf16[512,1536]{1,0:T(8,128)(2,1)} fusion(bf16[3072,512]{1,0:T(8,128)(2,1)} %get-tuple-element.1220, bf16[3072,1536]{1,0:T(8,128)(2,1)} %get-tuple-element.1221), kind=kOutput, calls=%fused_computation.9 | convolution fusion | flops 4832624640 | bytes 14155776 | tf_op jit(solution)/shard_map/cond/branch_1_fun/dot_general | solution.py:59
  403.2 12.9 %conditional.49 = (pred[]{:T(512)}, bf16[640,1536]{1,0:T(8,128)(2,1)}, bf16[1]{0:T(256)(128)(2,1)}) conditional(s32[]{:T(128)} %convert_element_type.368, pred[]{:T(512)} %get-tuple-element.1169, (bf16[3072,640]{1,0:T(8,128)(2,1)}, bf16[3072,1536]{1,0:T(8,128)(2,1)}, bf16[384,1536]{1,0:T(8,128)(2,1)}, pred[]{:T(512)}) %tuple.523), branch_computations={%region_8.9_spmd.clone.clone, %region_9.10_spmd.clone.clone} | conditional | flops 6040780800 | bytes 15335452
  403.2 11.1 %convolution_convert_fusion.3 = bf16[640,1536]{1,0:T(8,128)(2,1)} fusion(bf16[3072,640]{1,0:T(8,128)(2,1)} %get-tuple-element.1230, bf16[3072,1536]{1,0:T(8,128)(2,1)} %get-tuple-element.1231), kind=kOutput, calls=%fused_computation.10 | convolution fusion | flops 6040780800 | bytes 15335424 | tf_op jit(solution)/shard_map/cond/branch_1_fun/dot_general | solution.py:59
  428.4 10.9 %collective-permute-done.47.refs_2_ = bf16[192,1536]{1,0:T(8,128)(2,1)} collective-permute-done((bf16[192,1536]{1,0:T(8,128)(2,1)}, bf16[192,1536]{1,0:T(8,128)(2,1)}, u32[]{:S(2)}, u32[]{:S(2)}) %collective-permute-start.47) | collective-permute-done | bytes 589856 | tf_op jit(solution)/shard_map/ppermute | solution.py:229
  455.1 17.6 %shard_map.309 = bf16[3072,1536]{1,0:T(8,128)(2,1)} custom-call(s32[8]{0:T(128)} %iota.40.refs_0_, bf16[3072,512]{1,0:T(8,128)(2,1)S(1)} %copy-done.94, bf16[3072,640]{1,0:T(8,128)(2,1)} %get-tuple-element.813.refs_2_, bf16[1152,1536]{1,0:T(8,128)(2,1)} %pad.8.refs_3_, bf16[8,192,512]{2,1,0:T(8,128)(2,1)} %bitcast.20.refs_4_), custom_call_target="tpu_custom_call" | custom-call | flops 999999995904 | bytes 1024 | tf_op jit(solution)/shard_map/pallas_call | solution.py:575
  479.3 21.5 %conditional.44 = (pred[]{:T(512)}, f32[1536]{0:T(1024)}, f32[384,1536]{1,0:T(8,128)}, bf16[384,1536]{1,0:T(8,128)(2,1)}, bf16[384,1536]{1,0:T(8,128)(2,1)}, /*index=5*/bf16[1]{0:T(256)(128)(2,1)}, s32[]{:T(128)}) conditional(s32[]{:T(128)} %convert_element_type.369, pred[]{:T(512)} %get-tuple-element.1174, ...), branch_computations={%region_10.11_spmd.clone, %region_11.14_spmd.clone} | conditional | flops 1825504512 | bytes 24846432
  507.0 16.3 %shard_map.312 = (bf16[384,768]{1,0:T(8,128)(2,1)S(1)}, bf16[1536,256]{1,0:T(8,128)(2,1)S(1)}) custom-call(bf16[384,1536]{1,0:T(8,128)(2,1)S(1)} %copy-done.32, bf16[384,1536]{1,0:T(8,128)(2,1)} %get-tuple-element.833.refs_1_, bf16[1536,512]{1,0:T(8,128)(2,1)S(1)} %copy-done.24, bf16[1536,512]{1,0:T(8,128)(2,1)S(1)} %copy-done.24, ...), custom_call_target="tpu_custom_call" | custom-call | flops 999999995904 | bytes 1024 | tf_op jit(solution)/shard_map/pallas_call | solution.py:181
  528.5 15.8 %conditional.50 = (pred[]{:T(512)}, bf16[8,192,640]{2,1,0:T(8,128)(2,1)}, bf16[1]{0:T(256)(128)(2,1)}, bf16[1536,640]{1,0:T(8,128)(2,1)S(1)}) conditional(s32[]{:T(128)} %get-tuple-element.1175, pred[]{:T(512)} %get-tuple-element.889, (bf16[3072,1280]{1,0:T(8,128)(2,1)}, bf16[3072,1536]{1,0:T(8,128)(2,1)}, ...), branch_computations={%region_14.15_spmd.clone.clone, %region_15.16_spmd.clone.clone} | conditional | flops 6040780800 | bytes 19267620
  528.5 12.4 %fusion.3 = bf16[1536,640]{1,0:T(8,128)(2,1)} fusion(bf16[3072,1536]{1,0:T(8,128)(2,1)} %get-tuple-element.1241, bf16[3072,1280]{1,0:T(8,128)(2,1)} %get-tuple-element.1242), kind=kOutput, calls=%fused_computation.13 | convolution fusion | flops 6040780800 | bytes 15335424 | tf_op jit(solution)/shard_map/cond/branch_1_fun/dot_general | solution.py:59
  554.6 26.8 %collective-permute-done.56.refs_3_.refs_2_ = bf16[8,192,512]{2,1,0:T(8,128)(2,1)} collective-permute-done((bf16[8,192,512]{2,1,0:T(8,128)(2,1)}, bf16[8,192,512]{2,1,0:T(8,128)(2,1)}, u32[]{:S(2)}, u32[]{:S(2)}) %collective-permute-start.56) | collective-permute-done | bytes 1572896 | tf_op jit(solution)/shard_map/ppermute | solution.py:463
  586.6 16.3 %shard_map.316 = (bf16[384,768]{1,0:T(8,128)(2,1)S(1)}, bf16[1536,256]{1,0:T(8,128)(2,1)S(1)}) custom-call(bf16[384,1536]{1,0:T(8,128)(2,1)S(1)} %copy-done.33, bf16[384,1536]{1,0:T(8,128)(2,1)} %get-tuple-element.833.refs_1_, bf16[1536,512]{1,0:T(8,128)(2,1)S(1)} %copy-done.25, bf16[1536,512]{1,0:T(8,128)(2,1)S(1)} %copy-done.25, ...), custom_call_target="tpu_custom_call" | custom-call | flops 999999995904 | bytes 1024 | tf_op jit(solution)/shard_map/pallas_call | solution.py:181
  618.3 20.2 %conditional.39 = (pred[]{:T(512)}, f32[384,1536]{1,0:T(8,128)S(1)}, bf16[1536]{0:T(1024)(128)(2,1)S(1)}, bf16[1]{0:T(256)(128)(2,1)}, s32[]{:T(128)}, /*index=5*/bf16[1536,1536]{1,0:T(8,128)(2,1)}) conditional(s32[]{:T(128)} %convert_element_type.373, pred[]{:T(512)} %get-tuple-element.1187, (bf16[384,768]{1,0:T(8,128)(2,1)}, ...), branch_computations={%region_19.20_spmd.clone, %region_20.22_spmd.clone} | conditional | flops 3627416064 | bytes 28314680
  647.8 16.1 %conditional.52 = (pred[]{:T(512)}, bf16[8,192,640]{2,1,0:T(8,128)(2,1)}, bf16[1]{0:T(256)(128)(2,1)}, bf16[1536,640]{1,0:T(8,128)(2,1)S(1)}) conditional(s32[]{:T(128)} %get-tuple-element.892, pred[]{:T(512)} %get-tuple-element.846, (bf16[3072,1280]{1,0:T(8,128)(2,1)}, bf16[3072,1536]{1,0:T(8,128)(2,1)}, ...), branch_computations={%region_22.23_spmd.clone.clone, %region_23.24_spmd.clone.clone} | conditional | flops 6040780800 | bytes 19267622
  648.2 12.4 %fusion.8 = bf16[1536,640]{1,0:T(8,128)(2,1)} fusion(bf16[3072,1536]{1,0:T(8,128)(2,1)} %get-tuple-element.1266, bf16[3072,1280]{1,0:T(8,128)(2,1)} %get-tuple-element.1267), kind=kOutput, calls=%fused_computation.17 | convolution fusion | flops 6040780800 | bytes 15335424 | tf_op jit(solution)/shard_map/cond/branch_1_fun/dot_general | solution.py:59
  676.1 13.6 %conditional.45 = (pred[]{:T(512)}, bf16[1536,512]{0,1:T(8,128)(2,1)}, bf16[1536]{0:T(1024)(128)(2,1)S(1)}, f32[384,1536]{1,0:T(8,128)}, bf16[512]{0:T(512)(128)(2,1)S(1)}, /*index=5*/bf16[1]{0:T(256)(128)(2,1)}, s32[]{:T(128)}) conditional(s32[]{:T(128)} %convert_element_type.374, pred[]{:T(512)} %get-tuple-element.1194, ...), branch_computations={%region_24.25_spmd.clone, %region_25.31_spmd.clone} | conditional | flops 1222015744 | bytes 31696476
  689.7 14.1 %conditional.53 = (bf16[1792,512]{1,0:T(8,128)(2,1)S(1)}, bf16[384,1536]{1,0:T(8,128)(2,1)}, pred[]{:T(512)}) conditional(s32[]{:T(128)} %get-tuple-element.1195, pred[]{:T(512)} %get-tuple-element.902, (bf16[1536,512]{0,1:T(8,128)(2,1)}, bf16[1536]{0:T(1024)(128)(2,1)S(1)}, bf16[512]{0:T(512)(128)(2,1)S(1)}, bf16[1536]{0:T(1024)(128)(2,1)S(1)}, ...), branch_computations={%region_31.32_spmd, %region_32.37_spmd} | conditional | flops 10749852 | bytes 14748150
  705.1 13.5 %collective-permute-done.63.refs_3_ = bf16[640,1536]{1,0:T(8,128)(2,1)} collective-permute-done((bf16[640,1536]{1,0:T(8,128)(2,1)}, bf16[640,1536]{1,0:T(8,128)(2,1)}, u32[]{:S(2)}, u32[]{:S(2)}) %collective-permute-start.63) | collective-permute-done | bytes 1966112 | tf_op jit(solution)/shard_map/ppermute | solution.py:463
  744.1 10.9 %collective-permute-done.65.refs_1_ = bf16[192,1536]{1,0:T(8,128)(2,1)} collective-permute-done((bf16[192,1536]{1,0:T(8,128)(2,1)}, bf16[192,1536]{1,0:T(8,128)(2,1)}, u32[]{:S(2)}, u32[]{:S(2)}) %collective-permute-start.65) | collective-permute-done | bytes 589856 | tf_op jit(solution)/shard_map/ppermute | solution.py:455
  776.3 11.3 %reduce-scatter.11.cloned.1.call-done.refs_0_ = bf16[224,512]{1,0:T(8,128)(2,1)} async-done(((bf16[1792,512]{1,0:T(8,128)(2,1)}), bf16[224,512]{1,0:T(8,128)(2,1)}) %reduce-scatter.11.cloned.1.call-update) | async-done | bytes 229392 | tf_op jit(solution)/shard_map/reduce_scatter | solution.py:776
  821.4 27.0 %collective-permute-done.73.refs_4_ = bf16[8,192,640]{2,1,0:T(8,128)(2,1)} collective-permute-done((bf16[8,192,640]{2,1,0:T(8,128)(2,1)}, bf16[8,192,640]{2,1,0:T(8,128)(2,1)}, u32[]{:S(2)}, u32[]{:S(2)}) %collective-permute-start.73) | collective-permute-done | bytes 1966112 | tf_op jit(solution)/shard_map/ppermute | solution.py:463
  858.4 48.1 %collective-permute-done.71 = bf16[224,512]{1,0:T(8,128)(2,1)} collective-permute-done((bf16[224,512]{1,0:T(8,128)(2,1)}, bf16[224,512]{1,0:T(8,128)(2,1)}, u32[]{:S(2)}, u32[]{:S(2)}) %collective-permute-start.71) | collective-permute-done | bytes 229408 | tf_op jit(solution)/shard_map/ppermute | solution.py:463
  (528 shorter events, 481.7 us)
Async XLA Ops:
  7.2 94.9 %all-gather.2.cloned.1.call-start = ((), (), s32[]{:S(2)}) async-start(), calls=%async_computation.11 | async-start | bytes 1966080 | tf_op jit(solution)/shard_map/all_gather | solution.py:661
  82.8 50.1 %all-to-all-start = ((bf16[8,192,1024]{2,1,0:T(8,128)(2,1)}), bf16[8,192,1024]{2,1,0:T(8,128)(2,1)}, u32[]{:S(2)}, u32[]{:S(2)}) async-start(bf16[8,192,1024]{2,1,0:T(8,128)(2,1)} %get-tuple-element.803), calls=%async_computation | async-start | bytes 6291456 | tf_op jit(solution)/shard_map/all_to_all | solution.py:638
  132.9 67.5 %collective-permute-start.35 = (bf16[384,1536]{1,0:T(8,128)(2,1)S(1)}, bf16[384,1536]{1,0:T(8,128)(2,1)S(1)}, u32[]{:S(2)}, u32[]{:S(2)}) collective-permute-start(bf16[384,1536]{1,0:T(8,128)(2,1)S(1)} %get-tuple-element.804.refs_0_), channel_id=1, source_target_pairs={{0,8},{4,12},{8,0},{12,4},{16,24},{20,28},{24,16},{28,20},{1,9},{5... | collective-permute-start | bytes 3538952 | tf_op jit(solution)/shard_map/ppermute | solution.py:229
  160.3 40.6 %collective-permute-start.37 = (bf16[384,1536]{1,0:T(8,128)(2,1)S(1)}, bf16[384,1536]{1,0:T(8,128)(2,1)}, u32[]{:S(2)}, u32[]{:S(2)}) collective-permute-start(bf16[384,1536]{1,0:T(8,128)(2,1)S(1)} %get-tuple-element.804.refs_0_), channel_id=1, source_target_pairs={{0,16},{4,20},{8,24},{12,28},{16,0},{20,4},{24,8},{28,12},{1,17},{... | collective-permute-start | bytes 3538952 | tf_op jit(solution)/shard_map/ppermute | solution.py:229
  163.9 38.3 %collective-permute-start.25 = (bf16[384,1536]{1,0:T(8,128)(2,1)S(1)}, bf16[384,1536]{1,0:T(8,128)(2,1)S(1)}, u32[]{:S(2)}, u32[]{:S(2)}) collective-permute-start(bf16[384,1536]{1,0:T(8,128)(2,1)S(1)} %get-tuple-element.1286.refs_0_), channel_id=1, source_target_pairs={{0,4},{4,0},{8,12},{12,8},{16,20},{20,16},{24,28},{28,24},{1,5},{5... | collective-permute-start | bytes 3538952 | tf_op jit(solution)/shard_map/ppermute | solution.py:229
  203.2 40.6 %collective-permute-start.34 = (bf16[384,1536]{1,0:T(8,128)(2,1)S(1)}, bf16[384,1536]{1,0:T(8,128)(2,1)}, u32[]{:S(2)}, u32[]{:S(2)}) collective-permute-start(bf16[384,1536]{1,0:T(8,128)(2,1)S(1)} %get-tuple-element.804.refs_0_), channel_id=1, source_target_pairs={{0,4},{4,0},{8,12},{12,8},{16,20},{20,16},{24,28},{28,24},{1,5},{5... | collective-permute-start | bytes 3538952 | tf_op jit(solution)/shard_map/ppermute | solution.py:229
  237.7 65.4 %all-to-all-start.1 = ((bf16[8,192,1280]{2,1,0:T(8,128)(2,1)}), bf16[8,192,1280]{2,1,0:T(8,128)(2,1)}, u32[]{:S(2)}, u32[]{:S(2)}) async-start(bf16[8,192,1280]{2,1,0:T(8,128)(2,1)} %get-tuple-element.812), calls=%async_computation.1 | async-start | bytes 7864320 | tf_op jit(solution)/shard_map/all_to_all | solution.py:638
  295.3 38.5 %collective-permute-start.43 = (bf16[8,192,512]{2,1,0:T(8,128)(2,1)}, bf16[8,192,512]{2,1,0:T(8,128)(2,1)}, u32[]{:S(2)}, u32[]{:S(2)}) collective-permute-start(bf16[8,192,512]{2,1,0:T(8,128)(2,1)} %get-tuple-element.810.refs_0_), channel_id=1, source_target_pairs={{0,1},{3,2},{4,5},{7,6},{8,9},{11,10},{12,13},{15,14},{16,17},{19,... | collective-permute-start | bytes 4718600 | tf_op jit(solution)/shard_map/ppermute | solution.py:455
  300.6 78.0 %collective-permute-start.45 = (bf16[8,192,512]{2,1,0:T(8,128)(2,1)}, bf16[8,192,512]{2,1,0:T(8,128)(2,1)}, u32[]{:S(2)}, u32[]{:S(2)}) collective-permute-start(bf16[8,192,512]{2,1,0:T(8,128)(2,1)} %get-tuple-element.815), channel_id=1, source_target_pairs={{0,1},{3,2},{4,5},{7,6},{8,9},{11,10},{12,13},{15,14},{16,17},{19,... | collective-permute-start | bytes 4718600 | tf_op jit(solution)/shard_map/ppermute | solution.py:455
  336.3 45.2 %collective-permute-start.44 = (bf16[8,192,512]{2,1,0:T(8,128)(2,1)}, bf16[8,192,512]{2,1,0:T(8,128)(2,1)}, u32[]{:S(2)}, u32[]{:S(2)}) collective-permute-start(bf16[8,192,512]{2,1,0:T(8,128)(2,1)} %bitcast.14.refs_5_), channel_id=1, source_target_pairs={{1,2},{2,1},{5,6},{6,5},{9,10},{10,9},{13,14},{14,13},{17,18},{18,... | collective-permute-start | bytes 4718600 | tf_op jit(solution)/shard_map/ppermute | solution.py:459
  397.1 48.4 %collective-permute-start.51 = (bf16[8,192,512]{2,1,0:T(8,128)(2,1)}, bf16[8,192,512]{2,1,0:T(8,128)(2,1)}, u32[]{:S(2)}, u32[]{:S(2)}) collective-permute-start(bf16[8,192,512]{2,1,0:T(8,128)(2,1)} %bitcast.17.refs_2_), channel_id=1, source_target_pairs={{1,2},{2,1},{5,6},{6,5},{9,10},{10,9},{13,14},{14,13},{17,18},{18,... | collective-permute-start | bytes 4718600 | tf_op jit(solution)/shard_map/ppermute | solution.py:459
  398.9 46.5 %all-to-all-start.2 = ((bf16[8,192,512]{2,1,0:T(8,128)(2,1)}), bf16[8,192,512]{2,1,0:T(8,128)(2,1)}, u32[]{:S(2)}, u32[]{:S(2)}) async-start(bf16[8,192,512]{2,1,0:T(8,128)(2,1)} %bitcast.108), calls=%async_computation.2 | async-start | bytes 3145728 | tf_op jit(solution)/shard_map/all_to_all | solution.py:672
  416.2 107.2 %collective-permute-start.52 = (bf16[640,1536]{1,0:T(8,128)(2,1)}, bf16[640,1536]{1,0:T(8,128)(2,1)}, u32[]{:S(2)}, u32[]{:S(2)}) collective-permute-start(bf16[640,1536]{1,0:T(8,128)(2,1)} %get-tuple-element.829.refs_0_), channel_id=1, source_target_pairs={{0,1},{3,2},{4,5},{7,6},{8,9},{11,10},{12,13},{15,14},{16,17},{19,... | collective-permute-start | bytes 5898248 | tf_op jit(solution)/shard_map/ppermute | solution.py:455
  425.9 74.8 %collective-permute-start.53 = (bf16[512,1536]{1,0:T(8,128)(2,1)}, bf16[512,1536]{1,0:T(8,128)(2,1)}, u32[]{:S(2)}, u32[]{:S(2)}) collective-permute-start(bf16[512,1536]{1,0:T(8,128)(2,1)} %get-tuple-element.826.refs_0_), channel_id=1, source_target_pairs={{0,1},{3,2},{4,5},{7,6},{8,9},{11,10},{12,13},{15,14},{16,17},{19,... | collective-permute-start | bytes 4718600 | tf_op jit(solution)/shard_map/ppermute | solution.py:455
  445.4 55.4 %collective-permute-start.54 = (bf16[8,192,512]{2,1,0:T(8,128)(2,1)}, bf16[8,192,512]{2,1,0:T(8,128)(2,1)}, u32[]{:S(2)}, u32[]{:S(2)}) collective-permute-start(bf16[8,192,512]{2,1,0:T(8,128)(2,1)} %all-to-all-done.2.refs_3_.refs_1_), channel_id=1, source_target_pairs={{1,0},{2,3},{5,4},{6,7},{9,8},{10,11},{13,12},{14,15},{17,16},{18,... | collective-permute-start | bytes 4718600 | tf_op jit(solution)/shard_map/ppermute | solution.py:463
  449.6 51.1 %all-to-all-start.3 = ((bf16[8,192,512]{2,1,0:T(8,128)(2,1)}), bf16[8,192,512]{2,1,0:T(8,128)(2,1)}, u32[]{:S(2)}, u32[]{:S(2)}) async-start(bf16[8,192,512]{2,1,0:T(8,128)(2,1)} %bitcast.20.refs_4_), calls=%async_computation.3 | async-start | bytes 3145728 | tf_op jit(solution)/shard_map/all_to_all | solution.py:672
  454.6 154.8 %reduce-scatter.5.cloned.1.call-start = ((), (), s32[]{:S(2)}) async-start(), calls=%async_computation.12 | async-start | bytes 10616832 | tf_op jit(solution)/shard_map/reduce_scatter | solution.py:748
  505.0 49.6 %collective-permute-start.55 = (bf16[512,1536]{1,0:T(8,128)(2,1)}, bf16[512,1536]{1,0:T(8,128)(2,1)}, u32[]{:S(2)}, u32[]{:S(2)}) collective-permute-start(bf16[512,1536]{1,0:T(8,128)(2,1)} %shard_map.311.refs_8_.refs_0_), channel_id=1, source_target_pairs={{1,2},{2,1},{5,6},{6,5},{9,10},{10,9},{13,14},{14,13},{17,18},{18,... | collective-permute-start | bytes 4718600 | tf_op jit(solution)/shard_map/ppermute | solution.py:459
  545.7 99.4 %collective-permute-start.57 = (bf16[8,192,640]{2,1,0:T(8,128)(2,1)}, bf16[8,192,640]{2,1,0:T(8,128)(2,1)}, u32[]{:S(2)}, u32[]{:S(2)}) collective-permute-start(bf16[8,192,640]{2,1,0:T(8,128)(2,1)} %get-tuple-element.840.refs_0_), channel_id=1, source_target_pairs={{0,1},{3,2},{4,5},{7,6},{8,9},{11,10},{12,13},{15,14},{16,17},{19,... | collective-permute-start | bytes 5898248 | tf_op jit(solution)/shard_map/ppermute | solution.py:455
  552.7 87.2 %collective-permute-start.58 = (bf16[640,1536]{1,0:T(8,128)(2,1)}, bf16[640,1536]{1,0:T(8,128)(2,1)}, u32[]{:S(2)}, u32[]{:S(2)}) collective-permute-start(bf16[640,1536]{1,0:T(8,128)(2,1)} %shard_map.313.refs_0_), channel_id=1, source_target_pairs={{1,2},{2,1},{5,6},{6,5},{9,10},{10,9},{13,14},{14,13},{17,18},{18,... | collective-permute-start | bytes 5898248 | tf_op jit(solution)/shard_map/ppermute | solution.py:459
  585.0 54.9 %collective-permute-start.59 = (bf16[512,1536]{1,0:T(8,128)(2,1)}, bf16[512,1536]{1,0:T(8,128)(2,1)}, u32[]{:S(2)}, u32[]{:S(2)}) collective-permute-start(bf16[512,1536]{1,0:T(8,128)(2,1)} %shard_map.315.refs_8_), channel_id=1, source_target_pairs={{1,0},{2,3},{5,4},{6,7},{9,8},{10,11},{13,12},{14,15},{17,16},{18,... | collective-permute-start | bytes 4718600 | tf_op jit(solution)/shard_map/ppermute | solution.py:463
  604.3 71.7 %all-to-all-start.4 = ((bf16[4,384,512]{2,1,0:T(8,128)(2,1)}), bf16[4,384,512]{2,1,0:T(8,128)(2,1)}, u32[]{:S(2)}, u32[]{:S(2)}) async-start(bf16[4,384,512]{2,1,0:T(8,128)(2,1)} %pad_maximum_fusion.4), calls=%async_computation.5 | async-start | bytes 3145728 | tf_op jit(solution)/shard_map/all_to_all | solution.py:768
  609.5 130.1 %reduce-scatter.9.cloned.1.call-start = ((), (), s32[]{:S(2)}) async-start(), calls=%async_computation.14 | async-start | bytes 5308416 | tf_op jit(solution)/shard_map/reduce_scatter | solution.py:776
  618.2 123.7 %reduce-scatter.7.cloned.1.call-start = ((), (), s32[]{:S(2)}) async-start(), calls=%async_computation.13 | async-start | bytes 5308416 | tf_op jit(solution)/shard_map/reduce_scatter | solution.py:776
  665.3 61.7 %collective-permute-start.61 = (bf16[8,192,640]{2,1,0:T(8,128)(2,1)}, bf16[8,192,640]{2,1,0:T(8,128)(2,1)}, u32[]{:S(2)}, u32[]{:S(2)}) collective-permute-start(bf16[8,192,640]{2,1,0:T(8,128)(2,1)} %get-tuple-element.855.refs_0_), channel_id=1, source_target_pairs={{0,1},{3,2},{4,5},{7,6},{8,9},{11,10},{12,13},{15,14},{16,17},{19,... | collective-permute-start | bytes 5898248 | tf_op jit(solution)/shard_map/ppermute | solution.py:455
  674.6 44.0 %collective-permute-start.63 = (bf16[640,1536]{1,0:T(8,128)(2,1)}, bf16[640,1536]{1,0:T(8,128)(2,1)}, u32[]{:S(2)}, u32[]{:S(2)}) collective-permute-start(bf16[640,1536]{1,0:T(8,128)(2,1)} %shard_map.319.refs_2_), channel_id=1, source_target_pairs={{1,0},{2,3},{5,4},{6,7},{9,8},{10,11},{13,12},{14,15},{17,16},{18,... | collective-permute-start | bytes 5898248 | tf_op jit(solution)/shard_map/ppermute | solution.py:463
  676.0 111.6 %reduce-scatter.11.cloned.1.call-start = ((), (), s32[]{:S(2)}) async-start(), calls=%async_computation.15 | async-start | bytes 2064384 | tf_op jit(solution)/shard_map/reduce_scatter | solution.py:776
  721.9 47.2 %all-to-all-start.6 = ((bf16[8,192,640]{2,1,0:T(8,128)(2,1)}), bf16[8,192,640]{2,1,0:T(8,128)(2,1)}, u32[]{:S(2)}, u32[]{:S(2)}) async-start(bf16[8,192,640]{2,1,0:T(8,128)(2,1)} %bitcast.27.refs_2_), calls=%async_computation.10 | async-start | bytes 3932160 | tf_op jit(solution)/shard_map/all_to_all | solution.py:672
  794.0 54.3 %collective-permute-start.73 = (bf16[8,192,640]{2,1,0:T(8,128)(2,1)}, bf16[8,192,640]{2,1,0:T(8,128)(2,1)}, u32[]{:S(2)}, u32[]{:S(2)}) collective-permute-start(bf16[8,192,640]{2,1,0:T(8,128)(2,1)} %all-to-all-done.6.refs_3_), channel_id=1, source_target_pairs={{1,0},{2,3},{5,4},{6,7},{9,8},{10,11},{13,12},{14,15},{17,16},{18,... | collective-permute-start | bytes 5898248 | tf_op jit(solution)/shard_map/ppermute | solution.py:463
  813.3 98.1 %collective-permute-start.69 = (bf16[192,1536]{1,0:T(8,128)(2,1)}, bf16[192,1536]{1,0:T(8,128)(2,1)}, u32[]{:S(2)}, u32[]{:S(2)}) collective-permute-start(bf16[192,1536]{1,0:T(8,128)(2,1)} %shard_map.331.refs_2_), channel_id=1, source_target_pairs={{1,0},{2,3},{5,4},{6,7},{9,8},{10,11},{13,12},{14,15},{17,16},{18,... | collective-permute-start | bytes 1769480 | tf_op jit(solution)/shard_map/ppermute | solution.py:463
  814.5 99.0 %collective-permute-start.74 = (bf16[8,192,640]{2,1,0:T(8,128)(2,1)}, bf16[8,192,640]{2,1,0:T(8,128)(2,1)}, u32[]{:S(2)}, u32[]{:S(2)}) collective-permute-start(bf16[8,192,640]{2,1,0:T(8,128)(2,1)} %all-to-all-done.5.refs_3_), channel_id=1, source_target_pairs={{1,0},{2,3},{5,4},{6,7},{9,8},{10,11},{13,12},{14,15},{17,16},{18,... | collective-permute-start | bytes 5898248 | tf_op jit(solution)/shard_map/ppermute | solution.py:463
  820.1 86.5 %collective-permute-start.71 = (bf16[224,512]{1,0:T(8,128)(2,1)}, bf16[224,512]{1,0:T(8,128)(2,1)}, u32[]{:S(2)}, u32[]{:S(2)}) collective-permute-start(bf16[224,512]{1,0:T(8,128)(2,1)} %shard_map.332.refs_5_), channel_id=1, source_target_pairs={{1,0},{2,3},{5,4},{6,7},{9,8},{10,11},{13,12},{14,15},{17,16},{18,... | collective-permute-start | bytes 688136 | tf_op jit(solution)/shard_map/ppermute | solution.py:463
  (151 other events, 1737.5 us)
Sparse Core Ops, SparseCore 0:
  42.0 37.3 all-gather.1
  472.9 78.7 reduce-scatter.4
  618.3 55.2 reduce-scatter.8
  677.9 60.0 reduce-scatter.6
  741.2 46.3 reduce-scatter.10

commit v3 on v2

--- a/solution.py
+++ b/solution.py
@@ -85,34 +85,28 @@
         mixed[:, columns] = product(probabilities, values[...]).astype(BF)
 
 
-def attend_forward(query_lin, keys_values, cosine, signed_sine, query_pos, key_pos):
+def attend_forward(earlier, query_lin, keys_values, cosine, signed_sine, query_pos, key_pos):
     rows, width = query_lin.shape
     count_all = keys_values.shape[0]
     per_kv = H // KVH // HEADS_STEP
     wide = HEADS_STEP * HD
     table = pl.BlockSpec((rows, HD), lambda step: (0, 0))
     by_head = pl.BlockSpec((rows, wide), lambda step: (0, step))
-    return pl.pallas_call(
-        attend_forward_kernel,
-        grid=(H // HEADS_STEP,),
-        in_specs=[
-            by_head,
-            pl.BlockSpec((count_all, HD), lambda step: (0, step // per_kv)),
-            pl.BlockSpec((count_all, HD), lambda step: (0, KVH + step // per_kv)),
-            table,
-            table,
-            pl.BlockSpec((rows, 1), lambda step: (0, 0)),
-            pl.BlockSpec((1, count_all), lambda step: (0, 0)),
-        ],
-        out_specs=[by_head, by_head],
-        out_shape=[jax.ShapeDtypeStruct((rows, width), BF)] * 2,
-        compiler_params=pltpu.CompilerParams(vmem_limit_bytes=48 * 1024 * 1024),
-        cost_estimate=pl.CostEstimate(
-            flops=4 * rows * count_all * width,
-            bytes_accessed=8 * rows * width + 2 * keys_values.size,
-            transcendentals=H * rows * count_all,
-        ),
-    )(query_lin, keys_values, keys_values, cosine, signed_sine, query_pos, key_pos)
+    in_specs = [
+        by_head,
+        pl.BlockSpec((count_all, HD), lambda step: (0, step // per_kv)),
+        pl.BlockSpec((count_all, HD), lambda step: (0, KVH + step // per_kv)),
+        table,
+        table,
+        pl.BlockSpec((rows, 1), lambda step: (0, 0)),
+        pl.BlockSpec((1, count_all), lambda step: (0, 0)),
+    ]
+    out_shape = [jax.ShapeDtypeStruct((rows, width), BF)] * 2
+    operands = (query_lin, keys_values, keys_values, cosine, signed_sine, query_pos, key_pos)
+    call = ordered_call(
+        attend_forward_kernel, operands, in_specs, [by_head, by_head], out_shape, earlier, (H // HEADS_STEP,), vmem=48
+    )
+    return call(*operands, *earlier)
 
 
 def attend_backward_kernel(
@@ -190,102 +184,38 @@
     return (value + step - 1) // step * step
 
 
-def cut_kernel(gate, up, *outputs, hidden_width, widths):
-    count = gate.shape[1] // hidden_width
-    for owner in range(count):
-        column = owner * hidden_width
-        for out, wide in zip(outputs, widths):
-            padded = round_up(wide, LANES)
-            first = column // LANES * LANES
-            shift = column - first
-            span = round_up(shift + wide, LANES)
-            for half, source in enumerate((gate, up)):
-                part = source[:, first : first + span].astype(F32)
-                if shift:
-                    part = pltpu.roll(part, span - shift, 1)
-                if span < padded:
-                    part = jnp.concatenate([part, jnp.zeros((part.shape[0], padded - span), F32)], axis=1)
-                part = part[:, :padded]
-                if wide < padded:
-                    lane = lax.broadcasted_iota(jnp.int32, part.shape, 1)
-                    part = jnp.where(lane < wide, part, 0.0)
-                out[owner, :, half * padded : (half + 1) * padded] = part.astype(BF)
-            column += wide
-
-
-def cut_gate_up(w_gate, w_up, hidden_width, widths):
+def cut_kernel(gate, up, out, *, hidden_width, offset, wide):
+    padded = round_up(wide, LANES)
+    for owner in range(gate.shape[1] // hidden_width):
+        column = owner * hidden_width + offset
+        first = column // LANES * LANES
+        shift = column - first
+        span = round_up(shift + wide, LANES)
+        for half, source in enumerate((gate, up)):
+            part = source[:, first : first + span].astype(F32)
+            if shift:
+                part = pltpu.roll(part, span - shift, 1)
+            if span < padded:
+                part = jnp.concatenate([part, jnp.zeros((part.shape[0], padded - span), F32)], axis=1)
+            part = part[:, :padded]
+            if wide < padded:
+                lane = lax.broadcasted_iota(jnp.int32, part.shape, 1)
+                part = jnp.where(lane < wide, part, 0.0)
+            out[owner, :, half * padded : (half + 1) * padded] = part.astype(BF)
+
+
+def cut_gate_up(earlier, w_gate, w_up, hidden_width, offset, wide):
     rows, total = w_gate.shape
-    count = total // hidden_width
-    return pl.pallas_call(
-        functools.partial(cut_kernel, hidden_width=hidden_width, widths=widths),
-        out_shape=[jax.ShapeDtypeStruct((count, rows, 2 * round_up(wide, LANES)), BF) for wide in widths],
-        compiler_params=pltpu.CompilerParams(vmem_limit_bytes=48 * 1024 * 1024),
-        cost_estimate=pl.CostEstimate(flops=4 * w_gate.size, bytes_accessed=8 * w_gate.size, transcendentals=0),
-    )(w_gate, w_up)
+    whole = pl.BlockSpec(memory_space=pltpu.VMEM)
+    out_shape = jax.ShapeDtypeStruct((total // hidden_width, rows, 2 * round_up(wide, LANES)), BF)
+    kernel = functools.partial(cut_kernel, hidden_width=hidden_width, offset=offset, wide=wide)
+    call = ordered_call(kernel, (w_gate, w_up), [whole] * 2, whole, out_shape, earlier, vmem=48)
+    return call(w_gate, w_up, *earlier)
 
 
 def swap_fsdp(values, mask):
     count = lax.axis_size("fsdp")
     return lax.ppermute(values, "fsdp", [(i, i ^ mask) for i in range(count)])
-
-
-def after(value, *others):
-    return lax.optimization_barrier((value,) + others)[0]
-
-
-def place_kernel(index, *refs, sizes):
-    count = len(sizes)
-    pieces, out, semaphores = refs[:count], refs[count], refs[count + 1]
-    copies = []
-    for number, (mask, first, size) in enumerate(sizes):
-        start = jnp.bitwise_xor(index[0], mask) * (out.shape[0] // 8) + first
-        target = out.at[pl.ds(pl.multiple_of(start, 16), size)]
-        copies.append(pltpu.make_async_copy(pieces[number], target, semaphores.at[number]))
-        copies[-1].start()
-    for copy in copies:
-        copy.wait()
-
-
-def place_parts(parts, index):
-    rows = sum(part.shape[0] for _, _, part in parts)
-    columns, dtype = parts[0][2].shape[1], parts[0][2].dtype
-    sizes = [(mask, first, part.shape[0]) for mask, first, part in parts]
-    anywhere = pl.BlockSpec(memory_space=pl.ANY)
-    return pl.pallas_call(
-        functools.partial(place_kernel, sizes=sizes),
-        in_specs=[pl.BlockSpec(memory_space=pltpu.SMEM)] + [anywhere] * len(parts),
-        out_specs=pl.BlockSpec(memory_space=pltpu.VMEM),
-        out_shape=jax.ShapeDtypeStruct((rows, columns), dtype),
-        scratch_shapes=[pltpu.SemaphoreType.DMA((len(parts),))],
-        compiler_params=pltpu.CompilerParams(vmem_limit_bytes=32 * 1024 * 1024),
-        cost_estimate=pl.CostEstimate(flops=0, bytes_accessed=4 * rows * columns, transcendentals=0),
-    )(index, *(part for _, _, part in parts))
-
-
-def gather_rows(rows, index, *earlier):
-    if lax.axis_size("fsdp") != 8:
-        return lax.all_gather(rows, "fsdp", axis=0, tiled=True), (rows,), (rows,)
-    size = rows.shape[0]
-    half = size // 2
-    rows = after(rows, *earlier)
-    from_x = swap_fsdp(rows, 2)
-    from_y = swap_fsdp(rows, 4)
-    far_first = swap_fsdp(from_y[:half], 2)
-    far_last = swap_fsdp(from_x[half:], 4)
-    parts = []
-    for mask, first, part in ((0, 0, rows), (2, 0, from_x), (4, 0, from_y), (6, 0, far_first), (6, half, far_last)):
-        parts.append((mask, first, part))
-        parts.append((mask ^ 1, first, swap_fsdp(part, 1)))
-    return place_parts(parts, index), (from_x, from_y), (far_first, far_last)
-
-
-def gather_small(rows, index):
-    if lax.axis_size("fsdp") != 8:
-        return lax.all_gather(rows, "fsdp", axis=0, tiled=True), (rows,)
-    found = [(mask, rows if mask == 0 else swap_fsdp(rows, mask)) for mask in (0, 2, 4, 6)]
-    parts = [(mask, 0, part) for mask, part in found]
-    parts += [(mask ^ 1, 0, swap_fsdp(part, 1)) for mask, part in found]
-    return place_parts(parts, index), tuple(part for _, part in found)
 
 
 COVER = 10**12
@@ -321,11 +251,89 @@
     return ordered_call(spacer_kernel, (), [], pl.BlockSpec(memory_space=pltpu.VMEM), out_shape, earlier)(*earlier)
 
 
+def place_kernel(index, *refs, sizes):
+    count = len(sizes)
+    pieces, out, semaphores = refs[:count], refs[count], refs[count + 1]
+    copies = []
+    for number, (mask, first, size) in enumerate(sizes):
+        start = jnp.bitwise_xor(index[0], mask) * (out.shape[0] // 8) + first
+        target = out.at[pl.ds(pl.multiple_of(start, 16), size)]
+        copies.append(pltpu.make_async_copy(pieces[number], target, semaphores.at[number]))
+        copies[-1].start()
+    for copy in copies:
+        copy.wait()
+
+
+def place_parts(earlier, parts, index):
+    if not isinstance(parts, list):
+        return parts
+    rows = sum(part.shape[0] for _, _, part in parts)
+    columns, dtype = parts[0][2].shape[1], parts[0][2].dtype
+    sizes = [(mask, first, part.shape[0]) for mask, first, part in parts]
+    in_specs = [pl.BlockSpec(memory_space=pltpu.SMEM)] + [pl.BlockSpec(memory_space=pl.ANY)] * len(parts)
+    out_specs = pl.BlockSpec(memory_space=pltpu.VMEM)
+    out_shape = jax.ShapeDtypeStruct((rows, columns), dtype)
+    operands = (index, *(part for _, _, part in parts))
+    scratch = [pltpu.SemaphoreType.DMA((len(parts),))]
+    kernel = functools.partial(place_kernel, sizes=sizes)
+    call = ordered_call(kernel, operands, in_specs, out_specs, out_shape, earlier, scratch=scratch, vmem=32)
+    return call(*operands, *earlier)
+
+
+def gather_rows(rows):
+    if lax.axis_size("fsdp") != 8:
+        return (rows,), lax.all_gather(rows, "fsdp", axis=0, tiled=True)
+    half = rows.shape[0] // 2
+    from_x = swap_fsdp(rows, 2)
+    from_y = swap_fsdp(rows, 4)
+    far_first = swap_fsdp(from_y[:half], 2)
+    far_last = swap_fsdp(from_x[half:], 4)
+    parts = []
+    for mask, first, part in ((0, 0, rows), (2, 0, from_x), (4, 0, from_y), (6, 0, far_first), (6, half, far_last)):
+        parts.append((mask, first, part))
+        parts.append((mask ^ 1, first, swap_fsdp(part, 1)))
+    return (from_x, from_y), parts
+
+
+def gather_small(rows):
+    if lax.axis_size("fsdp") != 8:
+        return lax.all_gather(rows, "fsdp", axis=0, tiled=True)
+    found = [(mask, rows if mask == 0 else swap_fsdp(rows, mask)) for mask in (0, 2, 4, 6)]
+    parts = [(mask, 0, part) for mask, part in found]
+    parts += [(mask ^ 1, 0, swap_fsdp(part, 1)) for mask, part in found]
+    return parts
+
+
+def hold_kernel(values, out):
+    out[...] = values[...]
+
+
+def hold(earlier, values):
+    whole = pl.BlockSpec(memory_space=pltpu.VMEM)
+    out_shape = jax.ShapeDtypeStruct(values.shape, values.dtype)
+    return ordered_call(hold_kernel, (values,), [whole], whole, out_shape, earlier)(values, *earlier)
+
+
+def mask_kernel(values, valid, out):
+    out[...] = (values[...].astype(F32) * valid[...]).astype(BF)
+
+
+def mask_rows(earlier, values, valid):
+    whole = pl.BlockSpec(memory_space=pltpu.VMEM)
+    out_shape = jax.ShapeDtypeStruct(values.shape, BF)
+    return ordered_call(mask_kernel, (values, valid), [whole] * 2, whole, out_shape, earlier)(values, valid, *earlier)
+
+
 class Line:
     def __init__(self, ready):
         self.ready = ready
         self.marks = []
         self.last = ()
+
+    def fence(self):
+        small = self.last[0]
+        small = small[(0,) * (small.ndim - 2)][:16, :LANES]
+        self.last = (swap_fsdp(small, 1),)
 
     def kernel(self, call, *arrived):
         found = call(self.last + arrived)
@@ -519,6 +527,36 @@
     kernel = functools.partial(join_kernel, hidden_width=hidden_width, widths=widths)
     call = ordered_call(kernel, operands, in_specs, out_specs, out_shape, earlier, (total // rows,), vmem=32)
     return call(*operands, *earlier)
+
+
+def stack_kernel(middle, *refs):
+    out, chunks = refs[-1], refs[:-1]
+
+    def fill(number):
+        first = 0
+        for n in range(len(chunks) // 2):
+            rows = min(chunks[2 * n].shape[0], out.shape[0] - first)
+            out[first : first + rows] = chunks[2 * n + number][:rows].astype(F32)
+            first += rows
+
+    @pl.when(middle[0] == 1)
+    def _():
+        fill(0)
+
+    @pl.when(middle[0] == 0)
+    def _():
+        fill(1)
+
+
+def stack_rows(earlier, found, rows):
+    place = lax.axis_index("sp")
+    middle = ((place == 1) | (place == 2)).astype(jnp.int32)[None]
+    arrays = [part for chunk in found for part in chunk]
+    whole = pl.BlockSpec(memory_space=pltpu.VMEM)
+    in_specs = [pl.BlockSpec(memory_space=pltpu.SMEM)] + [whole] * len(arrays)
+    out_shape = jax.ShapeDtypeStruct((rows, arrays[0].shape[1]), F32)
+    operands = (middle, *arrays)
+    return ordered_call(stack_kernel, operands, in_specs, whole, out_shape, earlier, vmem=40)(*operands, *earlier)
 
 
 def activate_kernel(normed, grad, weights, down, hidden_out, grads_out, *, first):
@@ -621,7 +659,20 @@
     )
     fsdp_index = lax.axis_index("fsdp")
     own_index = fsdp_index[None]
-    kv_all, kv_hops = gather_small(kv_shard, own_index)
+    line = Line(seq_lengths[0] > 0)
+
+    def exchange(cut):
+        return lax.all_to_all(cut, "fsdp", split_axis=0, concat_axis=0, tiled=True).reshape(width, -1)
+
+    def cut(first, wide, *arrived):
+        return line.kernel(lambda earlier: cut_gate_up(earlier, w_gate, w_up, hidden_width, first, wide), *arrived)
+
+    def place(parts, *arrived):
+        return line.kernel(lambda earlier: place_parts(earlier, parts, own_index), *arrived)
+
+    kv_parts = gather_small(kv_shard)
+    q_hops, q_parts = gather_rows(line.kernel(lambda earlier: hold(earlier, w_query), kv_shard))
+    kv_all = place(kv_parts)
     kv_all = kv_all.reshape(fsdp_count, -1, kv_columns)
     w_kv = kv_all[:, :shard_rows].reshape(width, kv_columns)
     vectors = kv_all[:, shard_rows:].reshape(fsdp_count, -1).astype(F32)
@@ -629,16 +680,6 @@
     bias_q, bias_k, bias_v, gain_one, gain_two = (
         vectors[:, edges[n] : edges[n + 1]].reshape(-1) for n in range(len(vector_sizes))
     )
-    w_q, q_hops, q_far = gather_rows(w_query, own_index, *kv_hops)
-    w_o, o_hops, o_far = gather_rows(w_output, own_index, *q_hops)
-
-    cuts = cut_gate_up(w_gate, w_up, hidden_width, widths)
-
-    def exchange(cut):
-        return lax.all_to_all(cut, "fsdp", split_axis=0, concat_axis=0, tiled=True).reshape(width, -1)
-
-    weights_first = exchange(after(cuts[0], *o_hops))
-
     order_row = block_order[0]
     local_pos = stream_positions(order_row, sp_index * local_rows, local_rows, block_rows)
     group_pos = stream_positions(order_row, 0, group_rows, block_rows)
@@ -659,14 +700,24 @@
     ]
     keys_values = jnp.concatenate(key_rot + [(kv_lin[:, key_width:] + bias_v).astype(BF)], axis=1)
     keys_values = lax.all_gather(keys_values, "sp", axis=0, tiled=True)
+    o_hops, o_parts = gather_rows(line.kernel(lambda earlier: hold(earlier, w_output), *q_hops))
+    w_q = place(q_parts)
     query_lin = product(normed_one, w_q) + bias_q
-    query_rot, mixed = attend_forward(query_lin, keys_values, cosine, signed_sine, query_pos, key_pos)
+    grad_rows = line.kernel(lambda earlier: mask_rows(earlier, cotangent, valid_rows), *o_hops)
+    grad_hops, grad_parts = gather_rows(grad_rows)
+    weights_first = exchange(cut(0, widths[0]))
+    query_rot, mixed = line.kernel(
+        lambda earlier: attend_forward(earlier, query_lin, keys_values, cosine, signed_sine, query_pos, key_pos)
+    )
+    w_o = place(o_parts)
     attn_branch = product(mixed, w_o)
     hidden_in = inputs + valid_rows * attn_branch
     scale_two = lax.rsqrt(jnp.mean(hidden_in * hidden_in, axis=-1, keepdims=True) + EPS)
     unit_two = hidden_in * scale_two
-    mlp_grad, grad_hops, grad_far = gather_rows((valid_rows * upstream).astype(BF), own_index, *o_far, weights_first)
-    normed_two, two_hops, two_far = gather_rows((unit_two * gain_two).astype(BF), own_index)
+    two_hops, two_parts = gather_rows((unit_two * gain_two).astype(BF))
+    mlp_grad = place(grad_parts, weights_first, *two_hops)
+    weights_last = exchange(cut(widths[0], widths[1]))
+    normed_two = place(two_parts)
 
     def rows_exchange(half):
         return lax.all_to_all(half, "fsdp", split_axis=0, concat_axis=0, tiled=True)
@@ -684,10 +735,8 @@
 
     first_wide, last_wide = (round_up(wide, LANES) for wide in widths)
     down = jnp.pad(w_down, ((0, first_wide + last_wide - hidden_width), (0, 0)))
-    weights_last = exchange(after(cuts[1], *grad_far, *two_far))
     both_weights = [weights_first, weights_last]
     order_other, order_same = block_order(True), block_order(False)
-    line = Line(seq_lengths[0] > 0)
 
     def weight_step(left, right, rows=True):
         def work():
@@ -779,10 +828,15 @@
     down_2_across = across_middle(down_2_sum)
     gate_term_2 = weight_step(normed_two, gate_2)
     gate_2_in = to_middle(gate_term_2)
-    down_1_total = add(down_1_sum, down_1_across, up_1_ends)
+    down_1_total = add(down_1_sum, down_1_across)
     down_1_ends = to_ends(down_1_total)
+    output_term = line.step(lambda: weight_term(mixed, attn_grad), branch)
+    output_share = scatter_weight(output_term)
     query_grad_1, pair_1 = attend_step(1)
     pairs = pair_exchange(jnp.concatenate([pair_0, pair_1], axis=2))
+    gate_2_sum = add(gate_term_2, gate_2_in)
+    gate_2_across = across_middle(gate_2_sum)
+    line.fence()
 
     def kv_part(pair):
         pair_total = jnp.sum(pair.astype(F32), axis=0)
@@ -794,16 +848,13 @@
         sums = jnp.sum(query_lin_grad.astype(F32), axis=0)
         return weight_term(normed_one, query_lin_grad), contract_last(query_lin_grad, w_q), sums
 
-    output_term = line.step(lambda: weight_term(mixed, attn_grad), branch)
-    output_share = scatter_weight(output_term)
     query_term, normed_one_first, query_sums = line.step(query_step)
     query_share = scatter_weight(query_term)
-    down_2_total = add(down_2_sum, down_2_across, down_1_ends)
-    down_2_ends = to_ends(down_2_total)
-    gate_2_sum = add(gate_term_2, gate_2_in)
-    gate_2_across = across_middle(gate_2_sum)
     up_term_2 = weight_step(normed_two, up_2)
     up_2_in = to_middle(up_term_2)
+    down_2_total = add(down_2_sum, down_2_across)
+    down_2_ends = to_ends(down_2_total)
+    gate_2_total = rows_exchange(add(gate_2_sum, gate_2_across, up_1_ends))
 
     def kv_step():
         key_0, value_0 = kv_part(pairs[..., : 2 * HD])
@@ -858,17 +909,13 @@
 
     packed, layer_out = line.step(pack_step)
     kv_share = scatter_weight(packed)
-    gate_2_total = rows_exchange(add(gate_2_sum, gate_2_across, down_2_ends))
-    up_2_sum = add(up_term_2, up_2_in)
+    up_2_sum = add(up_term_2, up_2_in, gate_2_total)
+    gate_2_ends = to_ends(gate_2_total)
     up_2_across = across_middle(up_2_sum)
     output_in = to_middle(output_share)
 
-    def down_step():
-        rows = [pick_sum(down_1_total, down_1_ends)[: widths[0]], pick_sum(down_2_total, down_2_ends)[: widths[1]]]
-        return jnp.concatenate(rows, axis=0).astype(F32)
-
-    grad_down = line.step(down_step, gate_2_total)
-    gate_2_ends = to_ends(gate_2_total)
+    down = (down_1_total, down_1_ends), (down_2_total, down_2_ends)
+    grad_down = line.kernel(lambda earlier: stack_rows(earlier, down, hidden_width))
     output_sum = add(output_share, output_in)
     output_across = across_middle(output_sum)
     query_in = to_middle(query_share)

time: 946 us -> 919 us (0.971)
  waiting for transfers between devices: 270 us -> 199 us
  starting transfers between devices: 136 us -> 177 us
  Pallas kernels: 268 us -> 280 us
  other arithmetic: 60 us -> 48 us
    ppermute x9, starting transfers between devices: 42.6 us -> 84.3 us  [to_middle(): return lax.ppermute(values, 'sp', [(0, 1), (3, 2)])]
    ppermute x9, waiting for transfers between devices: 125 us -> 84 us  [to_ends(): return lax.ppermute(values, 'sp', [(1, 0), (2, 3)])]
    ppermute x48 -> x49, waiting for transfers between devices: 116 us -> 98.1 us  [swap_fsdp(): return lax.ppermute(values, 'fsdp', [(i, i ^ mask) for i in range(count)])]
    pallas_call x7 -> x12, Pallas kernels: 49.3 us -> 60.6 us  [the longest x5 20.6 us: place_parts(): return call(*operands, *earlier)]
    reduce_scatter x3, waiting for transfers between devices: 11.3 us -> 0.02 us  [scatter_weight(): return lax.psum_scatter(term, 'fsdp', scatter_dimension=0, tiled=True)]
    unnamed x200 -> x177, local copies, waits for them, and re-layouts: 31.9 us -> 32.7 us
    ppermute x48 -> x49, starting transfers between devices: 28.5 us -> 28.6 us  [swap_fsdp(): return lax.ppermute(values, 'fsdp', [(i, i ^ mask) for i in range(count)])]
  transfers between devices with their start and end apart: 87 -> 88, of which waited for: 21 -> 26; matrix products, arithmetic and copies ran while one was open for 21% -> 20% of each run, Pallas kernels for 27% -> 29%
where the time goes in v3:
time: 919 us; the launch traced here: 907 us
  Pallas kernels  280 us (30%)
  waiting for transfers between devices  199 us (22%)
  starting transfers between devices  177 us (19%)
  matrix products  94.1 us (10%)
  local copies, waits for them, and re-layouts  83.9 us (9%)
  other arithmetic  48 us (5%)
  between operations  16.6 us (2%)
    ppermute x49, waiting for transfers between devices, swap_fsdp(): return lax.ppermute(values, 'fsdp', [(i, i ^ mask) for i in range(count)])  98.1 us
    ppermute x9, starting transfers between devices, to_middle(): return lax.ppermute(values, 'sp', [(0, 1), (3, 2)])  84.3 us
    ppermute x9, waiting for transfers between devices, to_ends(): return lax.ppermute(values, 'sp', [(1, 0), (2, 3)])  84 us
    dot_general x8, matrix products, contract_first(): lax.dot_general(left, right, (((0,), (0,)), ((), ())), preferred_element_...  73.5 us
    pallas_call x18, Pallas kernels, add_low(): return call(left, right, *earlier).reshape(shape)  55.8 us
    pallas_call x3, Pallas kernels, row_products(): return call(order, *operands, *earlier)  52 us
    pallas_call x2, Pallas kernels, activate(): return call(*operands, *earlier)  51.9 us
    pallas_call x2, Pallas kernels, attend_backward(): return call(*operands, *earlier)  32.9 us
  transfers between devices with their start and end apart: 88, of which 26 were waited for; matrix products, arithmetic and copies ran while one was open for 20% of the time, Pallas kernels for 29%

profile of v3, /device:TPU:2, one launch (start us, length us, event | category | flops | bytes accessed | tf_op | source)
XLA Modules:
  0.0 906.8 jit_solution(14584527565495416846)
XLA Ops:
  59.9 11.7 %collective-permute-done.16.refs_3_ = bf16[192,1536]{1,0:T(8,128)(2,1)} collective-permute-done((bf16[192,1536]{1,0:T(8,128)(2,1)}, bf16[192,1536]{1,0:T(8,128)(2,1)}, u32[]{:S(2)}, u32[]{:S(2)}) %collective-permute-start.16) | collective-permute-done | bytes 589856 | tf_op jit(solution)/shard_map/ppermute | solution.py:218
  108.5 10.1 %collective-permute-done.23.refs_9_ = bf16[96,1536]{1,0:T(8,128)(2,1)} collective-permute-done((bf16[96,1536]{1,0:T(8,128)(2,1)}, bf16[96,1536]{1,0:T(8,128)(2,1)}, u32[]{:S(2)}, u32[]{:S(2)}) %collective-permute-start.23) | collective-permute-done | bytes 294944 | tf_op jit(solution)/shard_map/ppermute | solution.py:218
  122.5 19.4 %shard_map.295 = (bf16[384,1536]{1,0:T(8,128)(2,1)S(1)}, bf16[384,1536]{1,0:T(8,128)(2,1)}) custom-call(f32[384,1536]{1,0:T(8,128)S(1)} %convolution_add_fusion.1.refs_0_, bf16[1536,512]{1,0:T(8,128)(2,1)S(1)} %copy-done.4, bf16[1536,512]{1,0:T(8,128)(2,1)S(1)} %copy-done.4, f32[384,128]{1,0:T(8,128)S(1)} %copy-done.47, f32[384,128]{1,0:T(8,128)S(1)} %copy-done.35, ...), custom_call_target="tpu_custom_call" | custom-call | flops 999999995904 | bytes 1024 | tf_op jit(solution)/shard_map/pallas_call | solution.py:109
  158.9 23.8 %collective-permute-done.26.refs_13_.refs_3_ = bf16[384,1536]{1,0:T(8,128)(2,1)} collective-permute-done((bf16[384,1536]{1,0:T(8,128)(2,1)}, bf16[384,1536]{1,0:T(8,128)(2,1)}, u32[]{:S(2)}, u32[]{:S(2)}) %collective-permute-start.26) | collective-permute-done | bytes 1179680 | tf_op jit(solution)/shard_map/ppermute | solution.py:218
  230.8 22.6 %shard_map.300 = (bf16[3072,512]{1,0:T(8,128)(2,1)S(1)}, bf16[3072,1024]{1,0:T(8,128)(2,1)}) custom-call(bf16[3072,1536]{1,0:T(8,128)(2,1)} %shard_map.299.refs_0_.refs_4_, bf16[3072,1536]{1,0:T(8,128)(2,1)} %shard_map.297.refs_2_.refs_1_, bf16[1536,1024]{1,0:T(8,128)(2,1)} %bitcast.13.refs_12_.refs_2_.refs_3_, bf16[1152,1536]{1,0:T(8,128)(2,1)} %pad.8.refs_3_, ...), custom_call_target="tpu_custom_call" | custom-call | flops 999999995904 | bytes 1024 | tf_op jit(solution)/shard_map/pallas_call | solution.py:591
  255.1 20.2 %conditional.42 = (pred[]{:T(512)}, bf16[8,192,512]{2,1,0:T(8,128)(2,1)}, bf16[8,192,512]{2,1,0:T(8,128)(2,1)}, bf16[1]{0:T(256)(128)(2,1)}, bf16[1536,512]{1,0:...) conditional(s32[]{:T(128)} %convert_element_type.269, pred[]{:T(512)} %gt.8, ...), branch_computations={%region_4.5_spmd.clone.clone, %region_5.6_spmd.clone.clone} | conditional | flops 9665249280 | bytes 31457332
  255.3 14.1 %convolution_convert_fusion.1 = bf16[1536,1024]{1,0:T(8,128)(2,1)S(1)} fusion(bf16[3072,1536]{1,0:T(8,128)(2,1)} %get-tuple-element.1090, bf16[3072,1024]{1,0:T(8,128)(2,1)} %get-tuple-element.1091), kind=kOutput, calls=%fused_computation.5 | convolution fusion | flops 9665249280 | bytes 18874368 | tf_op jit(solution)/shard_map/cond/branch_1_fun/dot_general | solution.py:59
  283.1 29.3 %shard_map.302 = (bf16[3072,640]{1,0:T(8,128)(2,1)}, bf16[3072,1280]{1,0:T(8,128)(2,1)}) custom-call(bf16[3072,1536]{1,0:T(8,128)(2,1)} %shard_map.299.refs_0_.refs_4_, bf16[3072,1536]{1,0:T(8,128)(2,1)} %shard_map.297.refs_2_.refs_1_, bf16[1536,1280]{1,0:T(8,128)(2,1)} %bitcast.15.refs_2_.refs_4_, bf16[1152,1536]{1,0:T(8,128)(2,1)} %pad.8.refs_3_, ...), custom_call_target="tpu_custom_call" | custom-call | flops 999999995904 | bytes 1024 | tf_op jit(solution)/shard_map/pallas_call | solution.py:591
  318.2 17.2 %shard_map.304.refs_5_ = bf16[1536,1536]{1,0:T(8,128)(2,1)} custom-call(s32[4]{0:T(128)} %broadcast_xor_fusion.refs_0_, bf16[3072,1024]{1,0:T(8,128)(2,1)} %get-tuple-element.730.refs_1_, bf16[3072,1280]{1,0:T(8,128)(2,1)} %get-tuple-element.739.refs_2_, bf16[1536,1024]{1,0:T(8,128)(2,1)} %bitcast.13.refs_12_.refs_2_.refs_3_, ...), custom_call_target="tpu_custom_call" | custom-call | flops 999999995904 | bytes 1024 | tf_op jit(solution)/shard_map/pallas_call | solution.py:613
  335.4 17.2 %shard_map.305.refs_0_.refs_2_ = bf16[1536,1536]{1,0:T(8,128)(2,1)} custom-call(s32[4]{0:T(128)} %multiply_xor_fusion.refs_0_, bf16[3072,1024]{1,0:T(8,128)(2,1)} %get-tuple-element.730.refs_1_, bf16[3072,1280]{1,0:T(8,128)(2,1)} %get-tuple-element.739.refs_2_, bf16[1536,1024]{1,0:T(8,128)(2,1)} %bitcast.13.refs_12_.refs_2_.refs_3_, ...), custom_call_target="tpu_custom_call" | custom-call | flops 999999995904 | bytes 1024 | tf_op jit(solution)/shard_map/pallas_call | solution.py:613
  364.5 12.6 %conditional.43 = (pred[]{:T(512)}, bf16[512,1536]{1,0:T(8,128)(2,1)}, bf16[1]{0:T(256)(128)(2,1)}) conditional(s32[]{:T(128)} %convert_element_type.337, pred[]{:T(512)} %get-tuple-element.1051, (bf16[3072,512]{1,0:T(8,128)(2,1)}, bf16[3072,1536]{1,0:T(8,128)(2,1)}, bf16[8,192,512]{2,1,0:T(8,128)(2,1)}, pred[]{:T(512)}) %tuple.495), branch_computations={%region_6.7_spmd.clone.clone, %region_7.8_spmd.clone.clone} | conditional | flops 4832624640 | bytes 14155804
  364.8 10.4 %convolution_convert_fusion.2 = bf16[512,1536]{1,0:T(8,128)(2,1)} fusion(bf16[3072,512]{1,0:T(8,128)(2,1)} %get-tuple-element.1103, bf16[3072,1536]{1,0:T(8,128)(2,1)} %get-tuple-element.1104), kind=kOutput, calls=%fused_computation.6 | convolution fusion | flops 4832624640 | bytes 14155776 | tf_op jit(solution)/shard_map/cond/branch_1_fun/dot_general | solution.py:59
  383.3 12.9 %conditional.44 = (pred[]{:T(512)}, bf16[640,1536]{1,0:T(8,128)(2,1)}, bf16[1]{0:T(256)(128)(2,1)}) conditional(s32[]{:T(128)} %convert_element_type.338, pred[]{:T(512)} %get-tuple-element.1056, (bf16[3072,640]{1,0:T(8,128)(2,1)}, bf16[3072,1536]{1,0:T(8,128)(2,1)}, bf16[384,1536]{1,0:T(8,128)(2,1)}, pred[]{:T(512)}) %tuple.475), branch_computations={%region_8.9_spmd.clone.clone, %region_9.10_spmd.clone.clone} | conditional | flops 6040780800 | bytes 15335452
  383.3 11.1 %convolution_convert_fusion.3 = bf16[640,1536]{1,0:T(8,128)(2,1)} fusion(bf16[3072,640]{1,0:T(8,128)(2,1)} %get-tuple-element.1113, bf16[3072,1536]{1,0:T(8,128)(2,1)} %get-tuple-element.1114), kind=kOutput, calls=%fused_computation.7 | convolution fusion | flops 6040780800 | bytes 15335424 | tf_op jit(solution)/shard_map/cond/branch_1_fun/dot_general | solution.py:59
  408.5 11.0 %collective-permute-done.47.refs_2_ = bf16[192,1536]{1,0:T(8,128)(2,1)} collective-permute-done((bf16[192,1536]{1,0:T(8,128)(2,1)}, bf16[192,1536]{1,0:T(8,128)(2,1)}, u32[]{:S(2)}, u32[]{:S(2)}) %collective-permute-start.47) | collective-permute-done | bytes 589856 | tf_op jit(solution)/shard_map/ppermute | solution.py:218
  435.3 17.6 %shard_map.313 = bf16[3072,1536]{1,0:T(8,128)(2,1)} custom-call(s32[8]{0:T(128)} %iota.40.refs_0_, bf16[3072,512]{1,0:T(8,128)(2,1)S(1)} %copy-done.78, bf16[3072,640]{1,0:T(8,128)(2,1)} %get-tuple-element.736.refs_2_, bf16[1152,1536]{1,0:T(8,128)(2,1)} %pad.8.refs_3_, bf16[8,192,512]{2,1,0:T(8,128)(2,1)} %bitcast.22.refs_4_), custom_call_target="tpu_custom_call" | custom-call | flops 999999995904 | bytes 1024 | tf_op jit(solution)/shard_map/pallas_call | solution.py:613
  458.8 18.5 %conditional.40 = (pred[]{:T(512)}, f32[1536]{0:T(1024)S(1)}, f32[384,1536]{1,0:T(8,128)}, bf16[384,1536]{1,0:T(8,128)(2,1)}, bf16[384,1536]{1,0:T(8,128)(2,1)}, /*index=5*/bf16[1]{0:T(256)(128)(2,1)}, s32[]{:T(128)}) conditional(s32[]{:T(128)} %convert_element_type.339, pred[]{:T(512)} %get-tuple-element.1061, ...), branch_computations={%region_10.11_spmd.clone, %region_11.14_spmd.clone} | conditional | flops 1825504512 | bytes 24821828
  484.8 16.4 %shard_map.316 = (bf16[384,768]{1,0:T(8,128)(2,1)S(1)}, bf16[1536,256]{1,0:T(8,128)(2,1)S(1)}) custom-call(bf16[384,1536]{1,0:T(8,128)(2,1)S(1)} %copy-done.16, bf16[384,1536]{1,0:T(8,128)(2,1)} %get-tuple-element.755.refs_1_, bf16[1536,512]{1,0:T(8,128)(2,1)S(1)} %copy-done.5, bf16[1536,512]{1,0:T(8,128)(2,1)S(1)} %copy-done.5, f32[384,128]{1,0:T(8,128)S(1)} %copy-done.48, ...), custom_call_target="tpu_custom_call" | custom-call | flops 999999995904 | bytes 1024 | tf_op jit(solution)/shard_map/pallas_call | solution.py:175
  506.3 15.7 %conditional.45 = (pred[]{:T(512)}, bf16[8,192,640]{2,1,0:T(8,128)(2,1)}, bf16[1]{0:T(256)(128)(2,1)}, bf16[1536,640]{1,0:T(8,128)(2,1)S(1)}) conditional(s32[]{:T(128)} %get-tuple-element.1062, pred[]{:T(512)} %get-tuple-element.808, (bf16[3072,1280]{1,0:T(8,128)(2,1)}, bf16[3072,1536]{1,0:T(8,128)(2,1)}, ...), branch_computations={%region_14.15_spmd.clone.clone, %region_15.16_spmd.clone.clone} | conditional | flops 6040780800 | bytes 19267620
  506.3 12.4 %fusion.3 = bf16[1536,640]{1,0:T(8,128)(2,1)} fusion(bf16[3072,1536]{1,0:T(8,128)(2,1)} %get-tuple-element.1124, bf16[3072,1280]{1,0:T(8,128)(2,1)} %get-tuple-element.1125), kind=kOutput, calls=%fused_computation.10 | convolution fusion | flops 6040780800 | bytes 15335424 | tf_op jit(solution)/shard_map/cond/branch_1_fun/dot_general | solution.py:59
  551.6 16.5 %shard_map.321 = (bf16[384,768]{1,0:T(8,128)(2,1)S(1)}, bf16[1536,256]{1,0:T(8,128)(2,1)S(1)}) custom-call(bf16[384,1536]{1,0:T(8,128)(2,1)S(1)} %copy-done.17, bf16[384,1536]{1,0:T(8,128)(2,1)} %get-tuple-element.755.refs_1_, bf16[1536,512]{1,0:T(8,128)(2,1)S(1)} %copy-done.6, bf16[1536,512]{1,0:T(8,128)(2,1)S(1)} %copy-done.6, f32[384,128]{1,0:T(8,128)S(1)} %copy-done.49, ...), custom_call_target="tpu_custom_call" | custom-call | flops 999999995904 | bytes 1024 | tf_op jit(solution)/shard_map/pallas_call | solution.py:175
  582.3 20.0 %conditional.35 = (pred[]{:T(512)}, f32[384,1536]{1,0:T(8,128)S(1)}, bf16[1536]{0:T(1024)(128)(2,1)S(1)}, bf16[1]{0:T(256)(128)(2,1)}, s32[]{:T(128)}, /*index=5*/bf16[1536,1536]{1,0:T(8,128)(2,1)}) conditional(s32[]{:T(128)} %convert_element_type.343, pred[]{:T(512)} %get-tuple-element.1074, (bf16[384,768]{1,0:T(8,128)(2,1)}, ...), branch_computations={%region_19.20_spmd.clone, %region_20.22_spmd.clone} | conditional | flops 3627416064 | bytes 28314680
  603.7 15.5 %conditional.48 = (pred[]{:T(512)}, bf16[8,192,640]{2,1,0:T(8,128)(2,1)}, bf16[1]{0:T(256)(128)(2,1)}, bf16[1536,640]{1,0:T(8,128)(2,1)S(1)}) conditional(s32[]{:T(128)} %get-tuple-element.811, pred[]{:T(512)} %get-tuple-element.769, (bf16[3072,1280]{1,0:T(8,128)(2,1)}, bf16[3072,1536]{1,0:T(8,128)(2,1)}, ...), branch_computations={%region_22.23_spmd.clone.clone, %region_23.24_spmd.clone.clone} | conditional | flops 6040780800 | bytes 19267620
  604.1 12.3 %fusion.8 = bf16[1536,640]{1,0:T(8,128)(2,1)} fusion(bf16[3072,1536]{1,0:T(8,128)(2,1)} %get-tuple-element.1149, bf16[3072,1280]{1,0:T(8,128)(2,1)} %get-tuple-element.1150), kind=kOutput, calls=%fused_computation.14 | convolution fusion | flops 6040780800 | bytes 15335424 | tf_op jit(solution)/shard_map/cond/branch_1_fun/dot_general | solution.py:59
  642.4 14.0 %conditional.41 = (bf16[1536,512]{0,1:T(8,128)(2,1)}, bf16[1536]{0:T(1024)(128)(2,1)S(1)}, f32[384,1536]{1,0:T(8,128)}, bf16[512]{0:T(512)(128)(2,1)S(1)}, bf16[1]{0:T(256)(128)(2,1)}, /*index=5*/s32[]{:T(128)}) conditional(s32[]{:T(128)} %convert_element_type.344, pred[]{:T(512)} %get-tuple-element.1081, (bf16[4,384,512]{2,1,0:T(8,128)(2,1)}, ...), branch_computations={%region_24.25_spmd, %region_25.31_spmd} | conditional | flops 1222015744 | bytes 31696468
  656.5 13.0 %conditional.39 = (bf16[1792,512]{1,0:T(8,128)(2,1)S(1)}, bf16[384,1536]{1,0:T(8,128)(2,1)}) conditional(s32[]{:T(128)} %get-tuple-element.1082, () %tuple.295, (bf16[1536,512]{0,1:T(8,128)(2,1)}, bf16[1536]{0:T(1024)(128)(2,1)S(1)}, bf16[512]{0:T(512)(128)(2,1)S(1)}, bf16[1536]{0:T(1024)(128)(2,1)S(1)}, f32[1536]{0:T(1024)S(1)}, ...), branch_computations={%region_31.32_spmd, %region_32.37_spmd} | conditional | flops 10749852 | bytes 14748142 | solution.py:355
  683.0 24.5 %collective-permute-start.64 = (bf16[192,1536]{1,0:T(8,128)(2,1)}, bf16[192,1536]{1,0:T(8,128)(2,1)}, u32[]{:S(2)}, u32[]{:S(2)}) collective-permute-start(bf16[192,1536]{1,0:T(8,128)(2,1)} %reduce-scatter.9.cloned.1.call-done.refs_0_), channel_id=1, source_target_pairs={{0,1},{3,2},{4,5},{7,6},{8,9},{11,10},{12,13},{15,14},{16,17},{19,... | collective-permute-start | bytes 1769480 | tf_op jit(solution)/shard_map/ppermute | solution.py:463
  743.5 25.7 %collective-permute-start.68 = (bf16[224,512]{1,0:T(8,128)(2,1)}, bf16[224,512]{1,0:T(8,128)(2,1)S(1)}, u32[]{:S(2)}, u32[]{:S(2)}) collective-permute-start(bf16[224,512]{1,0:T(8,128)(2,1)} %reduce-scatter.11.cloned.1.call-done.refs_0_), channel_id=1, source_target_pairs={{0,1},{3,2},{4,5},{7,6},{8,9},{11,10},{12,13},{15,14},{16,17},{19,... | collective-permute-start | bytes 688136 | tf_op jit(solution)/shard_map/ppermute | solution.py:463
  793.9 27.0 %collective-permute-done.74.refs_4_ = bf16[8,192,640]{2,1,0:T(8,128)(2,1)} collective-permute-done((bf16[8,192,640]{2,1,0:T(8,128)(2,1)}, bf16[8,192,640]{2,1,0:T(8,128)(2,1)}, u32[]{:S(2)}, u32[]{:S(2)}) %collective-permute-start.74) | collective-permute-done | bytes 1966112 | tf_op jit(solution)/shard_map/ppermute | solution.py:471
  820.8 10.1 %shard_map.337.refs_5_ = f32[192,8960]{1,0:T(8,128)} custom-call(s32[1]{0:T(128)} %bitcast.32.refs_0_, bf16[8,192,512]{2,1,0:T(8,128)(2,1)} %all-to-all-done.2.refs_3_.refs_1_, bf16[8,192,512]{2,1,0:T(8,128)(2,1)} %collective-permute-done.54.refs_4_.refs_2_, bf16[8,192,640]{2,1,0:T(8,128)(2,1)} %all-to-all-done.5.refs_3_, ...), custom_call_target="tpu_custom_call" | custom-call | flops 999999995904 | bytes 1024 | tf_op jit(solution)/shard_map/pallas_call | solution.py:529
  831.0 49.1 %collective-permute-done.72 = bf16[224,512]{1,0:T(8,128)(2,1)} collective-permute-done((bf16[224,512]{1,0:T(8,128)(2,1)}, bf16[224,512]{1,0:T(8,128)(2,1)}, u32[]{:S(2)}, u32[]{:S(2)}) %collective-permute-start.72) | collective-permute-done | bytes 229408 | tf_op jit(solution)/shard_map/ppermute | solution.py:471
  889.9 10.1 %shard_map.338 = f32[192,8960]{1,0:T(8,128)} custom-call(s32[1]{0:T(128)} %bitcast.32.refs_0_, bf16[8,192,512]{2,1,0:T(8,128)(2,1)} %all-to-all-done.3.refs_3_.refs_1_, bf16[8,192,512]{2,1,0:T(8,128)(2,1)} %collective-permute-done.60.refs_3_.refs_2_, bf16[8,192,640]{2,1,0:T(8,128)(2,1)} %all-to-all-done.6.refs_3_, ...), custom_call_target="tpu_custom_call" | custom-call | flops 999999995904 | bytes 1024 | tf_op jit(solution)/shard_map/pallas_call | solution.py:529
  (509 shorter events, 472.4 us)
Async XLA Ops:
  7.2 113.9 %all-gather.2.cloned.1.call-start = ((), (), s32[]{:S(2)}) async-start(), calls=%async_computation.11 | async-start | bytes 1966080 | tf_op jit(solution)/shard_map/all_gather | solution.py:702
  57.3 84.6 %collective-permute-start.18 = (bf16[192,1536]{1,0:T(8,128)(2,1)}, bf16[192,1536]{1,0:T(8,128)(2,1)}, u32[]{:S(2)}, u32[]{:S(2)}) collective-permute-start(bf16[192,1536]{1,0:T(8,128)(2,1)} %shard_map.291.refs_11_.refs_1_), channel_id=1, source_target_pairs={{0,4},{4,0},{8,12},{12,8},{16,20},{20,16},{24,28},{28,24},{1,5},{5... | collective-permute-start | bytes 1769480 | tf_op jit(solution)/shard_map/ppermute | solution.py:218
  72.9 45.6 %collective-permute-start.35 = (bf16[384,1536]{1,0:T(8,128)(2,1)}, bf16[384,1536]{1,0:T(8,128)(2,1)}, u32[]{:S(2)}, u32[]{:S(2)}) collective-permute-start(bf16[384,1536]{1,0:T(8,128)(2,1)} %shard_map.293.refs_2_.refs_1_), channel_id=1, source_target_pairs={{0,8},{4,12},{8,0},{12,4},{16,24},{20,28},{24,16},{28,20},{1,9},{5... | collective-permute-start | bytes 3538952 | tf_op jit(solution)/shard_map/ppermute | solution.py:218
  88.2 108.3 %all-to-all-start = ((bf16[8,192,1024]{2,1,0:T(8,128)(2,1)}), bf16[8,192,1024]{2,1,0:T(8,128)(2,1)}, u32[]{:S(2)}, u32[]{:S(2)}) async-start(bf16[8,192,1024]{2,1,0:T(8,128)(2,1)} %shard_map.294.refs_7_), calls=%async_computation | async-start | bytes 6291456 | tf_op jit(solution)/shard_map/all_to_all | solution.py:665
  216.0 67.1 %all-to-all-start.1 = ((bf16[8,192,1280]{2,1,0:T(8,128)(2,1)}), bf16[8,192,1280]{2,1,0:T(8,128)(2,1)}, u32[]{:S(2)}, u32[]{:S(2)}) async-start(bf16[8,192,1280]{2,1,0:T(8,128)(2,1)} %shard_map.298.refs_11_), calls=%async_computation.1 | async-start | bytes 7864320 | tf_op jit(solution)/shard_map/all_to_all | solution.py:665
  280.6 78.0 %collective-permute-start.45 = (bf16[8,192,512]{2,1,0:T(8,128)(2,1)}, bf16[8,192,512]{2,1,0:T(8,128)(2,1)}, u32[]{:S(2)}, u32[]{:S(2)}) collective-permute-start(bf16[8,192,512]{2,1,0:T(8,128)(2,1)} %get-tuple-element.738), channel_id=1, source_target_pairs={{0,1},{3,2},{4,5},{7,6},{8,9},{11,10},{12,13},{15,14},{16,17},{19,... | collective-permute-start | bytes 4718600 | tf_op jit(solution)/shard_map/ppermute | solution.py:463
  316.4 45.2 %collective-permute-start.44 = (bf16[8,192,512]{2,1,0:T(8,128)(2,1)}, bf16[8,192,512]{2,1,0:T(8,128)(2,1)}, u32[]{:S(2)}, u32[]{:S(2)}) collective-permute-start(bf16[8,192,512]{2,1,0:T(8,128)(2,1)} %bitcast.16.refs_5_), channel_id=1, source_target_pairs={{1,2},{2,1},{5,6},{6,5},{9,10},{10,9},{13,14},{14,13},{17,18},{18,... | collective-permute-start | bytes 4718600 | tf_op jit(solution)/shard_map/ppermute | solution.py:467
  377.1 48.5 %collective-permute-start.51 = (bf16[8,192,512]{2,1,0:T(8,128)(2,1)}, bf16[8,192,512]{2,1,0:T(8,128)(2,1)}, u32[]{:S(2)}, u32[]{:S(2)}) collective-permute-start(bf16[8,192,512]{2,1,0:T(8,128)(2,1)} %bitcast.19.refs_2_), channel_id=1, source_target_pairs={{1,2},{2,1},{5,6},{6,5},{9,10},{10,9},{13,14},{14,13},{17,18},{18,... | collective-permute-start | bytes 4718600 | tf_op jit(solution)/shard_map/ppermute | solution.py:467
  378.9 46.6 %all-to-all-start.2 = ((bf16[8,192,512]{2,1,0:T(8,128)(2,1)}), bf16[8,192,512]{2,1,0:T(8,128)(2,1)}, u32[]{:S(2)}, u32[]{:S(2)}) async-start(bf16[8,192,512]{2,1,0:T(8,128)(2,1)} %bitcast.110), calls=%async_computation.2 | async-start | bytes 3145728 | tf_op jit(solution)/shard_map/all_to_all | solution.py:723
  396.2 105.0 %collective-permute-start.52 = (bf16[640,1536]{1,0:T(8,128)(2,1)}, bf16[640,1536]{1,0:T(8,128)(2,1)}, u32[]{:S(2)}, u32[]{:S(2)}) collective-permute-start(bf16[640,1536]{1,0:T(8,128)(2,1)} %get-tuple-element.752.refs_0_), channel_id=1, source_target_pairs={{0,1},{3,2},{4,5},{7,6},{8,9},{11,10},{12,13},{15,14},{16,17},{19,... | collective-permute-start | bytes 5898248 | tf_op jit(solution)/shard_map/ppermute | solution.py:463
  406.0 73.2 %collective-permute-start.53 = (bf16[512,1536]{1,0:T(8,128)(2,1)}, bf16[512,1536]{1,0:T(8,128)(2,1)}, u32[]{:S(2)}, u32[]{:S(2)}) collective-permute-start(bf16[512,1536]{1,0:T(8,128)(2,1)} %get-tuple-element.749.refs_0_), channel_id=1, source_target_pairs={{0,1},{3,2},{4,5},{7,6},{8,9},{11,10},{12,13},{15,14},{16,17},{19,... | collective-permute-start | bytes 4718600 | tf_op jit(solution)/shard_map/ppermute | solution.py:463
  425.5 53.6 %collective-permute-start.54 = (bf16[8,192,512]{2,1,0:T(8,128)(2,1)}, bf16[8,192,512]{2,1,0:T(8,128)(2,1)}, u32[]{:S(2)}, u32[]{:S(2)}) collective-permute-start(bf16[8,192,512]{2,1,0:T(8,128)(2,1)} %all-to-all-done.2.refs_3_.refs_1_), channel_id=1, source_target_pairs={{1,0},{2,3},{5,4},{6,7},{9,8},{10,11},{13,12},{14,15},{17,16},{18,... | collective-permute-start | bytes 4718600 | tf_op jit(solution)/shard_map/ppermute | solution.py:471
  429.8 49.4 %all-to-all-start.3 = ((bf16[8,192,512]{2,1,0:T(8,128)(2,1)}), bf16[8,192,512]{2,1,0:T(8,128)(2,1)}, u32[]{:S(2)}, u32[]{:S(2)}) async-start(bf16[8,192,512]{2,1,0:T(8,128)(2,1)} %bitcast.22.refs_4_), calls=%async_computation.3 | async-start | bytes 3145728 | tf_op jit(solution)/shard_map/all_to_all | solution.py:723
  434.8 104.7 %reduce-scatter.5.cloned.1.call-start = ((), (), s32[]{:S(2)}) async-start(), calls=%async_computation.12 | async-start | bytes 10616832 | tf_op jit(solution)/shard_map/reduce_scatter | solution.py:797
  452.9 230.1 %reduce-scatter.9.cloned.1.call-start = ((), (), s32[]{:S(2)}) async-start(), calls=%async_computation.14 | async-start | bytes 5308416 | tf_op jit(solution)/shard_map/reduce_scatter | solution.py:825
  482.8 51.9 %collective-permute-start.55 = (bf16[512,1536]{1,0:T(8,128)(2,1)}, bf16[512,1536]{1,0:T(8,128)(2,1)}, u32[]{:S(2)}, u32[]{:S(2)}) collective-permute-start(bf16[512,1536]{1,0:T(8,128)(2,1)} %shard_map.315.refs_8_.refs_0_), channel_id=1, source_target_pairs={{1,2},{2,1},{5,6},{6,5},{9,10},{10,9},{13,14},{14,13},{17,18},{18,... | collective-permute-start | bytes 4718600 | tf_op jit(solution)/shard_map/ppermute | solution.py:467
  523.4 47.8 %collective-permute-start.56 = (bf16[8,192,640]{2,1,0:T(8,128)(2,1)}, bf16[8,192,640]{2,1,0:T(8,128)(2,1)}, u32[]{:S(2)}, u32[]{:S(2)}) collective-permute-start(bf16[8,192,640]{2,1,0:T(8,128)(2,1)} %get-tuple-element.762.refs_0_), channel_id=1, source_target_pairs={{0,1},{3,2},{4,5},{7,6},{8,9},{11,10},{12,13},{15,14},{16,17},{19,... | collective-permute-start | bytes 5898248 | tf_op jit(solution)/shard_map/ppermute | solution.py:463
  531.4 95.8 %collective-permute-start.59 = (bf16[640,1536]{1,0:T(8,128)(2,1)}, bf16[640,1536]{1,0:T(8,128)(2,1)}, u32[]{:S(2)}, u32[]{:S(2)}) collective-permute-start(bf16[640,1536]{1,0:T(8,128)(2,1)} %shard_map.317.refs_0_), channel_id=1, source_target_pairs={{1,2},{2,1},{5,6},{6,5},{9,10},{10,9},{13,14},{14,13},{17,18},{18,... | collective-permute-start | bytes 5898248 | tf_op jit(solution)/shard_map/ppermute | solution.py:467
  533.4 100.1 %collective-permute-start.60 = (bf16[8,192,512]{2,1,0:T(8,128)(2,1)}, bf16[8,192,512]{2,1,0:T(8,128)(2,1)}, u32[]{:S(2)}, u32[]{:S(2)}) collective-permute-start(bf16[8,192,512]{2,1,0:T(8,128)(2,1)} %all-to-all-done.3.refs_3_.refs_1_), channel_id=1, source_target_pairs={{1,0},{2,3},{5,4},{6,7},{9,8},{10,11},{13,12},{14,15},{17,16},{18,... | collective-permute-start | bytes 4718600 | tf_op jit(solution)/shard_map/ppermute | solution.py:471
  538.2 169.4 %collective-permute-start.65 = (bf16[512,1536]{1,0:T(8,128)(2,1)}, bf16[512,1536]{1,0:T(8,128)(2,1)}, u32[]{:S(2)}, u32[]{:S(2)}) collective-permute-start(bf16[512,1536]{1,0:T(8,128)(2,1)} %shard_map.319.refs_1_), channel_id=1, source_target_pairs={{1,0},{2,3},{5,4},{6,7},{9,8},{10,11},{13,12},{14,15},{17,16},{18,... | collective-permute-start | bytes 4718600 | tf_op jit(solution)/shard_map/ppermute | solution.py:471
  575.9 61.4 %all-to-all-start.4 = ((bf16[4,384,512]{2,1,0:T(8,128)(2,1)}), bf16[4,384,512]{2,1,0:T(8,128)(2,1)}, u32[]{:S(2)}, u32[]{:S(2)}) async-start(bf16[4,384,512]{2,1,0:T(8,128)(2,1)} %pad_maximum_fusion.4), calls=%async_computation.5 | async-start | bytes 3145728 | tf_op jit(solution)/shard_map/all_to_all | solution.py:817
  580.2 134.1 %reduce-scatter.7.cloned.1.call-start = ((), (), s32[]{:S(2)}) async-start(), calls=%async_computation.13 | async-start | bytes 5308416 | tf_op jit(solution)/shard_map/reduce_scatter | solution.py:825
  580.3 53.2 %collective-permute-start.58 = (bf16[8,192,640]{2,1,0:T(8,128)(2,1)}, bf16[8,192,640]{2,1,0:T(8,128)(2,1)}, u32[]{:S(2)}, u32[]{:S(2)}) collective-permute-start(bf16[8,192,640]{2,1,0:T(8,128)(2,1)} %bitcast.26), channel_id=1, source_target_pairs={{1,2},{2,1},{5,6},{6,5},{9,10},{10,9},{13,14},{14,13},{17,18},{18,... | collective-permute-start | bytes 5898248 | tf_op jit(solution)/shard_map/ppermute | solution.py:467
  620.6 50.2 %collective-permute-start.62 = (bf16[8,192,640]{2,1,0:T(8,128)(2,1)}, bf16[8,192,640]{2,1,0:T(8,128)(2,1)}, u32[]{:S(2)}, u32[]{:S(2)}) collective-permute-start(bf16[8,192,640]{2,1,0:T(8,128)(2,1)} %get-tuple-element.777.refs_0_), channel_id=1, source_target_pairs={{0,1},{3,2},{4,5},{7,6},{8,9},{11,10},{12,13},{15,14},{16,17},{19,... | collective-permute-start | bytes 5898248 | tf_op jit(solution)/shard_map/ppermute | solution.py:463
  632.1 75.4 %collective-permute-start.66 = (bf16[640,1536]{1,0:T(8,128)(2,1)}, bf16[640,1536]{1,0:T(8,128)(2,1)}, u32[]{:S(2)}, u32[]{:S(2)}) collective-permute-start(bf16[640,1536]{1,0:T(8,128)(2,1)} %shard_map.325.refs_2_.refs_3_), channel_id=1, source_target_pairs={{1,0},{2,3},{5,4},{6,7},{9,8},{10,11},{13,12},{14,15},{17,16},{18,... | collective-permute-start | bytes 5898248 | tf_op jit(solution)/shard_map/ppermute | solution.py:471
  642.3 101.2 %reduce-scatter.11.cloned.1.call-start = ((), (), s32[]{:S(2)}) async-start(), calls=%async_computation.15 | async-start | bytes 2064384 | tf_op jit(solution)/shard_map/reduce_scatter | solution.py:825
  681.0 46.5 %collective-permute-start.63 = (bf16[8,192,640]{2,1,0:T(8,128)(2,1)}, bf16[8,192,640]{2,1,0:T(8,128)(2,1)}, u32[]{:S(2)}, u32[]{:S(2)}) collective-permute-start(bf16[8,192,640]{2,1,0:T(8,128)(2,1)} %bitcast.30.refs_5_), channel_id=1, source_target_pairs={{1,2},{2,1},{5,6},{6,5},{9,10},{10,9},{13,14},{14,13},{17,18},{18,... | collective-permute-start | bytes 5898248 | tf_op jit(solution)/shard_map/ppermute | solution.py:467
  730.8 48.9 %all-to-all-start.6 = ((bf16[8,192,640]{2,1,0:T(8,128)(2,1)}), bf16[8,192,640]{2,1,0:T(8,128)(2,1)}, u32[]{:S(2)}, u32[]{:S(2)}) async-start(bf16[8,192,640]{2,1,0:T(8,128)(2,1)} %bitcast.33.refs_2_), calls=%async_computation.10 | async-start | bytes 3932160 | tf_op jit(solution)/shard_map/all_to_all | solution.py:723
  742.2 78.6 %collective-permute-start.74 = (bf16[8,192,640]{2,1,0:T(8,128)(2,1)}, bf16[8,192,640]{2,1,0:T(8,128)(2,1)}, u32[]{:S(2)}, u32[]{:S(2)}) collective-permute-start(bf16[8,192,640]{2,1,0:T(8,128)(2,1)} %all-to-all-done.5.refs_3_), channel_id=1, source_target_pairs={{1,0},{2,3},{5,4},{6,7},{9,8},{10,11},{13,12},{14,15},{17,16},{18,... | collective-permute-start | bytes 5898248 | tf_op jit(solution)/shard_map/ppermute | solution.py:471
  785.8 99.0 %collective-permute-start.70 = (bf16[192,1536]{1,0:T(8,128)(2,1)}, bf16[192,1536]{1,0:T(8,128)(2,1)}, u32[]{:S(2)}, u32[]{:S(2)}) collective-permute-start(bf16[192,1536]{1,0:T(8,128)(2,1)} %shard_map.335.refs_2_), channel_id=1, source_target_pairs={{1,0},{2,3},{5,4},{6,7},{9,8},{10,11},{13,12},{14,15},{17,16},{18,... | collective-permute-start | bytes 1769480 | tf_op jit(solution)/shard_map/ppermute | solution.py:471
  787.1 99.9 %collective-permute-start.75 = (bf16[8,192,640]{2,1,0:T(8,128)(2,1)}, bf16[8,192,640]{2,1,0:T(8,128)(2,1)}, u32[]{:S(2)}, u32[]{:S(2)}) collective-permute-start(bf16[8,192,640]{2,1,0:T(8,128)(2,1)} %all-to-all-done.6.refs_3_), channel_id=1, source_target_pairs={{1,0},{2,3},{5,4},{6,7},{9,8},{10,11},{13,12},{14,15},{17,16},{18,... | collective-permute-start | bytes 5898248 | tf_op jit(solution)/shard_map/ppermute | solution.py:471
  792.6 87.5 %collective-permute-start.72 = (bf16[224,512]{1,0:T(8,128)(2,1)}, bf16[224,512]{1,0:T(8,128)(2,1)}, u32[]{:S(2)}, u32[]{:S(2)}) collective-permute-start(bf16[224,512]{1,0:T(8,128)(2,1)} %shard_map.336.refs_5_), channel_id=1, source_target_pairs={{1,0},{2,3},{5,4},{6,7},{9,8},{10,11},{13,12},{14,15},{17,16},{18,... | collective-permute-start | bytes 688136 | tf_op jit(solution)/shard_map/ppermute | solution.py:471
  (141 other events, 1710.0 us)
Sparse Core Ops, SparseCore 0:
  48.3 37.9 all-gather.1
  453.0 78.7 reduce-scatter.4
  549.0 56.3 reduce-scatter.8
  627.3 66.0 reduce-scatter.6
  696.7 44.2 reduce-scatter.10

commit v4 on v3

--- a/solution.py
+++ b/solution.py
@@ -848,13 +848,15 @@
         sums = jnp.sum(query_lin_grad.astype(F32), axis=0)
         return weight_term(normed_one, query_lin_grad), contract_last(query_lin_grad, w_q), sums
 
+    up_term_2 = weight_step(normed_two, up_2)
+    up_2_in = to_middle(up_term_2)
     query_term, normed_one_first, query_sums = line.step(query_step)
     query_share = scatter_weight(query_term)
-    up_term_2 = weight_step(normed_two, up_2)
-    up_2_in = to_middle(up_term_2)
     down_2_total = add(down_2_sum, down_2_across)
     down_2_ends = to_ends(down_2_total)
-    gate_2_total = rows_exchange(add(gate_2_sum, gate_2_across, up_1_ends))
+
+    def held(values):
+        return line.kernel(lambda earlier: hold(earlier, values))
 
     def kv_step():
         key_0, value_0 = kv_part(pairs[..., : 2 * HD])
@@ -866,6 +868,10 @@
         return weight_term(normed_one, kv_lin_grad), gain_grad, hidden_in_grad + back, sums
 
     kv_term, gain_one_grad, input_grad, kv_sums = line.step(kv_step)
+
+    up_2_sum = add(up_term_2, up_2_in)
+    up_2_across = across_middle(up_2_sum)
+    gate_2_total = rows_exchange(add(gate_2_sum, gate_2_across, up_1_ends))
 
     def last_rows(vector):
         return vector.reshape(fsdp_count, -1)
@@ -909,36 +915,39 @@
 
     packed, layer_out = line.step(pack_step)
     kv_share = scatter_weight(packed)
-    up_2_sum = add(up_term_2, up_2_in, gate_2_total)
+    output_in = to_middle(output_share)
+    down = (down_1_total, down_1_ends), (down_2_total, down_2_ends)
+    grad_down = line.kernel(lambda earlier: stack_rows(earlier, down, hidden_width), gate_2_total)
     gate_2_ends = to_ends(gate_2_total)
-    up_2_across = across_middle(up_2_sum)
-    output_in = to_middle(output_share)
-
-    down = (down_1_total, down_1_ends), (down_2_total, down_2_ends)
-    grad_down = line.kernel(lambda earlier: stack_rows(earlier, down, hidden_width))
+    up_2_total = rows_exchange(add(up_2_sum, up_2_across))
     output_sum = add(output_share, output_in)
     output_across = across_middle(output_sum)
+    query_share = held(query_share)
     query_in = to_middle(query_share)
-    up_2_total = rows_exchange(add(up_2_sum, up_2_across))
-    kv_in = to_middle(kv_share)
+    output_total = add(output_sum, output_across)
+    output_ends = to_ends(output_total)
+    gate = (gate_1_total, gate_1_ends), (gate_2_total, gate_2_ends)
+    grad_gate = line.kernel(lambda earlier: join_columns(earlier, gate, (0, 0), hidden_width, widths))
     query_sum = add(query_share, query_in)
     query_across = across_middle(query_sum)
-    output_total = add(output_sum, output_across)
-    output_ends = to_ends(output_total)
-    kv_sum = add(kv_share, kv_in, up_2_total)
+
+    def picked(total, moved):
+        return line.kernel(lambda earlier: stack_rows(earlier, ((total, moved),), total.shape[0]))
+
+    grad_output = picked(output_total, output_ends)
+    kv_share = held(kv_share)
+    kv_in = to_middle(kv_share)
+    query_total = add(query_sum, query_across, up_2_total)
     up_2_ends = to_ends(up_2_total)
+    query_ends = to_ends(query_total)
+    kv_sum = add(kv_share, kv_in)
     kv_across = across_middle(kv_sum)
-    gate = (gate_1_total, gate_1_ends), (gate_2_total, gate_2_ends)
-    up = (up_1_total, up_1_ends), (up_2_total, up_2_ends)
-    query_total = add(query_sum, query_across)
-    query_ends = to_ends(query_total)
     kv_total = add(kv_sum, kv_across)
     kv_ends = to_ends(kv_total)
-    grad_gate = line.kernel(lambda earlier: join_columns(earlier, gate, (0, 0), hidden_width, widths))
+    grad_query = picked(query_total, query_ends)
+    up = (up_1_total, up_1_ends), (up_2_total, up_2_ends)
     grad_up = line.kernel(lambda earlier: join_columns(earlier, up, (0, 0), hidden_width, widths))
-    grad_output = pick_sum(output_total, output_ends).astype(F32)
-    grad_query = pick_sum(query_total, query_ends).astype(F32)
-    projections = pick_sum(kv_total, kv_ends).astype(F32)
+    projections = picked(kv_total, kv_ends)
     sums = projections[shard_rows:].reshape(-1)
     grad_b_query, grad_b_key, grad_b_value, grad_gain_one, grad_gain_two = (
         sums[edges[n] : edges[n + 1]] for n in range(len(vector_sizes))

time: 919 us -> 885 us (0.963)
  starting transfers between devices: 177 us -> 148 us
  waiting for transfers between devices: 199 us -> 185 us
    ppermute x9, starting transfers between devices: 84.3 us -> 56.8 us  [to_middle(): return lax.ppermute(values, 'sp', [(0, 1), (3, 2)])]
    ppermute x9, waiting for transfers between devices: 84 us -> 61.2 us  [to_ends(): return lax.ppermute(values, 'sp', [(1, 0), (2, 3)])]
    all_to_all x4, waiting for transfers between devices: 6.94 us -> 18.2 us  [rows_exchange(): return lax.all_to_all(half, 'fsdp', split_axis=0, concat_axis=0, tiled=True)]
    unnamed x177 -> x193, local copies, waits for them, and re-layouts: 32.7 us -> 40.6 us
  transfers between devices with their start and end apart: 88 -> 88, of which waited for: 26 -> 26; matrix products, arithmetic and copies ran while one was open for 20% -> 20% of each run, Pallas kernels for 29% -> 32%
where the time goes in v4:
time: 885 us; the launch traced here: 874 us
  Pallas kernels  286 us (32%)
  waiting for transfers between devices  185 us (21%)
  starting transfers between devices  148 us (17%)
  matrix products  94.4 us (11%)
  local copies, waits for them, and re-layouts  93 us (11%)
  other arithmetic  43.7 us (5%)
  between operations  16.6 us (2%)
    ppermute x49, waiting for transfers between devices, swap_fsdp(): return lax.ppermute(values, 'fsdp', [(i, i ^ mask) for i in range(count)])  98.1 us
    dot_general x8, matrix products, contract_first(): lax.dot_general(left, right, (((0,), (0,)), ((), ())), preferred_element_...  73.5 us
    ppermute x9, waiting for transfers between devices, to_ends(): return lax.ppermute(values, 'sp', [(1, 0), (2, 3)])  61.2 us
    ppermute x9, starting transfers between devices, to_middle(): return lax.ppermute(values, 'sp', [(0, 1), (3, 2)])  56.8 us
    pallas_call x18, Pallas kernels, add_low(): return call(left, right, *earlier).reshape(shape)  54.8 us
    pallas_call x3, Pallas kernels, row_products(): return call(order, *operands, *earlier)  52 us
    pallas_call x2, Pallas kernels, activate(): return call(*operands, *earlier)  51.9 us
    unnamed x193, local copies, waits for them, and re-layouts  40.6 us
  transfers between devices with their start and end apart: 88, of which 26 were waited for; matrix products, arithmetic and copies ran while one was open for 20% of the time, Pallas kernels for 32%

profile of v4, /device:TPU:2, one launch (start us, length us, event | category | flops | bytes accessed | tf_op | source)
XLA Modules:
  0.0 873.6 jit_solution(6110704355851198719)
XLA Ops:
  59.9 11.7 %collective-permute-done.16.refs_3_ = bf16[192,1536]{1,0:T(8,128)(2,1)} collective-permute-done((bf16[192,1536]{1,0:T(8,128)(2,1)}, bf16[192,1536]{1,0:T(8,128)(2,1)}, u32[]{:S(2)}, u32[]{:S(2)}) %collective-permute-start.16) | collective-permute-done | bytes 589856 | tf_op jit(solution)/shard_map/ppermute | solution.py:218
  94.5 9.4 %collective-permute-done.37.refs_5_ = bf16[384,1536]{1,0:T(8,128)(2,1)} collective-permute-done((bf16[384,1536]{1,0:T(8,128)(2,1)}, bf16[384,1536]{1,0:T(8,128)(2,1)}, u32[]{:S(2)}, u32[]{:S(2)}) %collective-permute-start.37) | collective-permute-done | bytes 1179680 | tf_op jit(solution)/shard_map/ppermute | solution.py:218
  108.5 10.1 %collective-permute-done.23.refs_9_ = bf16[96,1536]{1,0:T(8,128)(2,1)} collective-permute-done((bf16[96,1536]{1,0:T(8,128)(2,1)}, bf16[96,1536]{1,0:T(8,128)(2,1)}, u32[]{:S(2)}, u32[]{:S(2)}) %collective-permute-start.23) | collective-permute-done | bytes 294944 | tf_op jit(solution)/shard_map/ppermute | solution.py:218
  122.4 19.4 %shard_map.295 = (bf16[384,1536]{1,0:T(8,128)(2,1)S(1)}, bf16[384,1536]{1,0:T(8,128)(2,1)}) custom-call(f32[384,1536]{1,0:T(8,128)S(1)} %convolution_add_fusion.1.refs_0_, bf16[1536,512]{1,0:T(8,128)(2,1)S(1)} %copy-done.4, bf16[1536,512]{1,0:T(8,128)(2,1)S(1)} %copy-done.4, f32[384,128]{1,0:T(8,128)S(1)} %copy-done.51, f32[384,128]{1,0:T(8,128)S(1)} %copy-done.39, ...), custom_call_target="tpu_custom_call" | custom-call | flops 999999995904 | bytes 1024 | tf_op jit(solution)/shard_map/pallas_call | solution.py:109
  158.9 23.8 %collective-permute-done.26.refs_13_.refs_3_ = bf16[384,1536]{1,0:T(8,128)(2,1)} collective-permute-done((bf16[384,1536]{1,0:T(8,128)(2,1)}, bf16[384,1536]{1,0:T(8,128)(2,1)}, u32[]{:S(2)}, u32[]{:S(2)}) %collective-permute-start.26) | collective-permute-done | bytes 1179680 | tf_op jit(solution)/shard_map/ppermute | solution.py:218
  230.8 22.6 %shard_map.300 = (bf16[3072,512]{1,0:T(8,128)(2,1)S(1)}, bf16[3072,1024]{1,0:T(8,128)(2,1)}) custom-call(bf16[3072,1536]{1,0:T(8,128)(2,1)} %shard_map.299.refs_0_.refs_4_, bf16[3072,1536]{1,0:T(8,128)(2,1)} %shard_map.297.refs_2_.refs_1_, bf16[1536,1024]{1,0:T(8,128)(2,1)} %bitcast.13.refs_12_.refs_2_.refs_3_, bf16[1152,1536]{1,0:T(8,128)(2,1)} %pad.8.refs_3_, ...), custom_call_target="tpu_custom_call" | custom-call | flops 999999995904 | bytes 1024 | tf_op jit(solution)/shard_map/pallas_call | solution.py:591
  255.1 20.2 %conditional.42 = (pred[]{:T(512)}, bf16[8,192,512]{2,1,0:T(8,128)(2,1)}, bf16[8,192,512]{2,1,0:T(8,128)(2,1)}, bf16[1]{0:T(256)(128)(2,1)}, bf16[1536,512]{1,0:...) conditional(s32[]{:T(128)} %convert_element_type.263, pred[]{:T(512)} %gt.8, ...), branch_computations={%region_4.5_spmd.clone.clone, %region_5.6_spmd.clone.clone} | conditional | flops 9665249280 | bytes 31457332
  255.3 14.1 %convolution_convert_fusion.1 = bf16[1536,1024]{1,0:T(8,128)(2,1)S(1)} fusion(bf16[3072,1536]{1,0:T(8,128)(2,1)} %get-tuple-element.1090, bf16[3072,1024]{1,0:T(8,128)(2,1)} %get-tuple-element.1091), kind=kOutput, calls=%fused_computation.5 | convolution fusion | flops 9665249280 | bytes 18874368 | tf_op jit(solution)/shard_map/cond/branch_1_fun/dot_general | solution.py:59
  283.0 29.3 %shard_map.302 = (bf16[3072,640]{1,0:T(8,128)(2,1)}, bf16[3072,1280]{1,0:T(8,128)(2,1)}) custom-call(bf16[3072,1536]{1,0:T(8,128)(2,1)} %shard_map.299.refs_0_.refs_4_, bf16[3072,1536]{1,0:T(8,128)(2,1)} %shard_map.297.refs_2_.refs_1_, bf16[1536,1280]{1,0:T(8,128)(2,1)} %bitcast.15.refs_2_.refs_4_, bf16[1152,1536]{1,0:T(8,128)(2,1)} %pad.8.refs_3_, ...), custom_call_target="tpu_custom_call" | custom-call | flops 999999995904 | bytes 1024 | tf_op jit(solution)/shard_map/pallas_call | solution.py:591
  318.2 17.2 %shard_map.304.refs_5_ = bf16[1536,1536]{1,0:T(8,128)(2,1)} custom-call(s32[4]{0:T(128)} %broadcast_xor_fusion.refs_0_, bf16[3072,1024]{1,0:T(8,128)(2,1)} %get-tuple-element.730.refs_1_, bf16[3072,1280]{1,0:T(8,128)(2,1)} %get-tuple-element.739.refs_2_, bf16[1536,1024]{1,0:T(8,128)(2,1)} %bitcast.13.refs_12_.refs_2_.refs_3_, ...), custom_call_target="tpu_custom_call" | custom-call | flops 999999995904 | bytes 1024 | tf_op jit(solution)/shard_map/pallas_call | solution.py:613
  335.4 17.2 %shard_map.305.refs_0_.refs_2_ = bf16[1536,1536]{1,0:T(8,128)(2,1)} custom-call(s32[4]{0:T(128)} %multiply_xor_fusion.refs_0_, bf16[3072,1024]{1,0:T(8,128)(2,1)} %get-tuple-element.730.refs_1_, bf16[3072,1280]{1,0:T(8,128)(2,1)} %get-tuple-element.739.refs_2_, bf16[1536,1024]{1,0:T(8,128)(2,1)} %bitcast.13.refs_12_.refs_2_.refs_3_, ...), custom_call_target="tpu_custom_call" | custom-call | flops 999999995904 | bytes 1024 | tf_op jit(solution)/shard_map/pallas_call | solution.py:613
  364.5 12.5 %conditional.43 = (pred[]{:T(512)}, bf16[512,1536]{1,0:T(8,128)(2,1)}, bf16[1]{0:T(256)(128)(2,1)}) conditional(s32[]{:T(128)} %convert_element_type.328, pred[]{:T(512)} %get-tuple-element.1051, (bf16[3072,512]{1,0:T(8,128)(2,1)}, bf16[3072,1536]{1,0:T(8,128)(2,1)}, bf16[8,192,512]{2,1,0:T(8,128)(2,1)}, pred[]{:T(512)}) %tuple.496), branch_computations={%region_6.7_spmd.clone.clone, %region_7.8_spmd.clone.clone} | conditional | flops 4832624640 | bytes 14155804
  364.9 10.3 %convolution_convert_fusion.2 = bf16[512,1536]{1,0:T(8,128)(2,1)} fusion(bf16[3072,512]{1,0:T(8,128)(2,1)} %get-tuple-element.1103, bf16[3072,1536]{1,0:T(8,128)(2,1)} %get-tuple-element.1104), kind=kOutput, calls=%fused_computation.6 | convolution fusion | flops 4832624640 | bytes 14155776 | tf_op jit(solution)/shard_map/cond/branch_1_fun/dot_general | solution.py:59
  383.2 12.9 %conditional.44 = (pred[]{:T(512)}, bf16[640,1536]{1,0:T(8,128)(2,1)}, bf16[1]{0:T(256)(128)(2,1)}) conditional(s32[]{:T(128)} %convert_element_type.329, pred[]{:T(512)} %get-tuple-element.1056, (bf16[3072,640]{1,0:T(8,128)(2,1)}, bf16[3072,1536]{1,0:T(8,128)(2,1)}, bf16[384,1536]{1,0:T(8,128)(2,1)}, pred[]{:T(512)}) %tuple.475), branch_computations={%region_8.9_spmd.clone.clone, %region_9.10_spmd.clone.clone} | conditional | flops 6040780800 | bytes 15335452
  383.2 11.1 %convolution_convert_fusion.3 = bf16[640,1536]{1,0:T(8,128)(2,1)} fusion(bf16[3072,640]{1,0:T(8,128)(2,1)} %get-tuple-element.1113, bf16[3072,1536]{1,0:T(8,128)(2,1)} %get-tuple-element.1114), kind=kOutput, calls=%fused_computation.7 | convolution fusion | flops 6040780800 | bytes 15335424 | tf_op jit(solution)/shard_map/cond/branch_1_fun/dot_general | solution.py:59
  408.4 11.0 %collective-permute-done.47.refs_2_ = bf16[192,1536]{1,0:T(8,128)(2,1)} collective-permute-done((bf16[192,1536]{1,0:T(8,128)(2,1)}, bf16[192,1536]{1,0:T(8,128)(2,1)}, u32[]{:S(2)}, u32[]{:S(2)}) %collective-permute-start.47) | collective-permute-done | bytes 589856 | tf_op jit(solution)/shard_map/ppermute | solution.py:218
  435.2 17.5 %shard_map.313 = bf16[3072,1536]{1,0:T(8,128)(2,1)} custom-call(s32[8]{0:T(128)} %iota.40.refs_0_, bf16[3072,512]{1,0:T(8,128)(2,1)S(1)} %copy-done.86, bf16[3072,640]{1,0:T(8,128)(2,1)} %get-tuple-element.736.refs_2_, bf16[1152,1536]{1,0:T(8,128)(2,1)} %pad.8.refs_3_, bf16[8,192,512]{2,1,0:T(8,128)(2,1)} %bitcast.22.refs_4_), custom_call_target="tpu_custom_call" | custom-call | flops 999999995904 | bytes 1024 | tf_op jit(solution)/shard_map/pallas_call | solution.py:613
  458.8 18.6 %conditional.40 = (pred[]{:T(512)}, f32[1536]{0:T(1024)S(1)}, f32[384,1536]{1,0:T(8,128)}, bf16[384,1536]{1,0:T(8,128)(2,1)}, bf16[384,1536]{1,0:T(8,128)(2,1)}, /*index=5*/bf16[1]{0:T(256)(128)(2,1)}, s32[]{:T(128)}) conditional(s32[]{:T(128)} %convert_element_type.330, pred[]{:T(512)} %get-tuple-element.1061, ...), branch_computations={%region_10.11_spmd.clone, %region_11.14_spmd.clone} | conditional | flops 1825504512 | bytes 24821828
  484.7 16.3 %shard_map.316 = (bf16[384,768]{1,0:T(8,128)(2,1)S(1)}, bf16[1536,256]{1,0:T(8,128)(2,1)S(1)}) custom-call(bf16[384,1536]{1,0:T(8,128)(2,1)S(1)} %copy-done.19, bf16[384,1536]{1,0:T(8,128)(2,1)} %get-tuple-element.755.refs_1_, bf16[1536,512]{1,0:T(8,128)(2,1)S(1)} %copy-done.5, bf16[1536,512]{1,0:T(8,128)(2,1)S(1)} %copy-done.5, f32[384,128]{1,0:T(8,128)S(1)} %copy-done.52, ...), custom_call_target="tpu_custom_call" | custom-call | flops 999999995904 | bytes 1024 | tf_op jit(solution)/shard_map/pallas_call | solution.py:175
  506.2 15.8 %conditional.45 = (pred[]{:T(512)}, bf16[8,192,640]{2,1,0:T(8,128)(2,1)}, bf16[1]{0:T(256)(128)(2,1)}, bf16[1536,640]{1,0:T(8,128)(2,1)S(1)}) conditional(s32[]{:T(128)} %get-tuple-element.1062, pred[]{:T(512)} %get-tuple-element.808, (bf16[3072,1280]{1,0:T(8,128)(2,1)}, bf16[3072,1536]{1,0:T(8,128)(2,1)}, ...), branch_computations={%region_14.15_spmd.clone.clone, %region_15.16_spmd.clone.clone} | conditional | flops 6040780800 | bytes 19267620
  506.2 12.4 %fusion.3 = bf16[1536,640]{1,0:T(8,128)(2,1)} fusion(bf16[3072,1536]{1,0:T(8,128)(2,1)} %get-tuple-element.1124, bf16[3072,1280]{1,0:T(8,128)(2,1)} %get-tuple-element.1125), kind=kOutput, calls=%fused_computation.10 | convolution fusion | flops 6040780800 | bytes 15335424 | tf_op jit(solution)/shard_map/cond/branch_1_fun/dot_general | solution.py:59
  539.3 9.4 %conditional.46 = (pred[]{:T(512)}, bf16[1536,1536]{1,0:T(8,128)(2,1)}, bf16[1]{0:T(256)(128)(2,1)}, bf16[1]{0:T(256)(128)(2,1)}) conditional(s32[]{:T(128)} %convert_element_type.333, pred[]{:T(512)} %get-tuple-element.1068, (bf16[384,1536]{1,0:T(8,128)(2,1)S(1)}, bf16[384,1536]{1,0:T(8,128)(2,1)}, ...), branch_computations={%region_17.18_spmd.clone.clone, %region_18.19_spmd.clone.clone} | conditional | flops 1814298624 | bytes 7077928
  551.5 16.5 %shard_map.321 = (bf16[384,768]{1,0:T(8,128)(2,1)S(1)}, bf16[1536,256]{1,0:T(8,128)(2,1)S(1)}) custom-call(bf16[384,1536]{1,0:T(8,128)(2,1)S(1)} %copy-done.20, bf16[384,1536]{1,0:T(8,128)(2,1)} %get-tuple-element.755.refs_1_, bf16[1536,512]{1,0:T(8,128)(2,1)S(1)} %copy-done.6, bf16[1536,512]{1,0:T(8,128)(2,1)S(1)} %copy-done.6, f32[384,128]{1,0:T(8,128)S(1)} %copy-done.53, ...), custom_call_target="tpu_custom_call" | custom-call | flops 999999995904 | bytes 1024 | tf_op jit(solution)/shard_map/pallas_call | solution.py:175
  582.2 15.4 %conditional.48 = (pred[]{:T(512)}, bf16[8,192,640]{2,1,0:T(8,128)(2,1)}, bf16[1]{0:T(256)(128)(2,1)}, bf16[1536,640]{1,0:T(8,128)(2,1)S(1)}) conditional(s32[]{:T(128)} %convert_element_type.334, pred[]{:T(512)} %get-tuple-element.1074, (bf16[3072,1280]{1,0:T(8,128)(2,1)}, bf16[3072,1536]{1,0:T(8,128)(2,1)}, ...), branch_computations={%region_19.20_spmd.clone.clone, %region_20.21_spmd.clone.clone} | conditional | flops 6040780800 | bytes 19267622
  582.2 12.5 %fusion.8 = bf16[1536,640]{1,0:T(8,128)(2,1)} fusion(bf16[3072,1536]{1,0:T(8,128)(2,1)} %get-tuple-element.1149, bf16[3072,1280]{1,0:T(8,128)(2,1)} %get-tuple-element.1150), kind=kOutput, calls=%fused_computation.14 | convolution fusion | flops 6040780800 | bytes 15335424 | tf_op jit(solution)/shard_map/cond/branch_1_fun/dot_general | solution.py:59
  605.0 20.6 %conditional.36 = (pred[]{:T(512)}, f32[384,1536]{1,0:T(8,128)S(1)}, bf16[1536]{0:T(1024)(128)(2,1)S(1)}, bf16[1]{0:T(256)(128)(2,1)}, s32[]{:T(128)}, /*index=5*/bf16[1536,1536]{1,0:T(8,128)(2,1)}) conditional(s32[]{:T(128)} %convert_element_type.335, pred[]{:T(512)} %get-tuple-element.1080, (bf16[384,768]{1,0:T(8,128)(2,1)}, ...), branch_computations={%region_21.22_spmd.clone, %region_22.24_spmd.clone} | conditional | flops 3627416064 | bytes 28314680
  633.6 14.7 %conditional.41 = (bf16[1536,512]{0,1:T(8,128)(2,1)}, bf16[1536]{0:T(1024)(128)(2,1)S(1)}, f32[384,1536]{1,0:T(8,128)}, bf16[512]{0:T(512)(128)(2,1)S(1)}, bf16[1]{0:T(256)(128)(2,1)}, /*index=5*/s32[]{:T(128)}) conditional(s32[]{:T(128)} %get-tuple-element.812, pred[]{:T(512)} %get-tuple-element.772, (bf16[4,384,512]{2,1,0:T(8,128)(2,1)}, ...), branch_computations={%region_24.25_spmd, %region_25.31_spmd} | conditional | flops 1222015744 | bytes 31696468
  664.5 11.9 %conditional.39 = (bf16[1792,512]{1,0:T(8,128)(2,1)}, bf16[384,1536]{1,0:T(8,128)(2,1)}) conditional(s32[]{:T(128)} %get-tuple-element.1082, () %tuple.295, (bf16[1536,512]{0,1:T(8,128)(2,1)}, bf16[1536]{0:T(1024)(128)(2,1)S(1)}, bf16[512]{0:T(512)(128)(2,1)S(1)}, bf16[1536]{0:T(1024)(128)(2,1)S(1)}, f32[1536]{0:T(1024)S(1)}, ...), branch_computations={%region_31.32_spmd, %region_32.37_spmd} | conditional | flops 10749852 | bytes 14748142 | solution.py:355
  676.5 18.2 %all-to-all-done.5.refs_6_.refs_3_ = bf16[8,192,640]{2,1,0:T(8,128)(2,1)} async-done(((bf16[8,192,640]{2,1,0:T(8,128)(2,1)}), bf16[8,192,640]{2,1,0:T(8,128)(2,1)}, u32[]{:S(2)}, u32[]{:S(2)}) %all-to-all-start.5) | async-done | bytes 1966112 | tf_op jit(solution)/shard_map/all_to_all | solution.py:723
  744.1 10.1 %shard_map.335.refs_2_ = f32[192,8960]{1,0:T(8,128)} custom-call(s32[1]{0:T(128)} %bitcast.26.refs_0_, bf16[8,192,512]{2,1,0:T(8,128)(2,1)} %all-to-all-done.2.refs_3_.refs_1_, bf16[8,192,512]{2,1,0:T(8,128)(2,1)} %collective-permute-done.54.refs_4_.refs_2_, bf16[8,192,640]{2,1,0:T(8,128)(2,1)} %all-to-all-done.5.refs_6_.refs_3_, ...), custom_call_target="tpu_custom_call" | custom-call | flops 999999995904 | bytes 1024 | tf_op jit(solution)/shard_map/pallas_call | solution.py:529
  788.7 56.6 %collective-permute-done.71.refs_2_ = bf16[192,1536]{1,0:T(8,128)(2,1)} collective-permute-done((bf16[192,1536]{1,0:T(8,128)(2,1)}, bf16[192,1536]{1,0:T(8,128)(2,1)}, u32[]{:S(2)}, u32[]{:S(2)}) %collective-permute-start.71) | collective-permute-done | bytes 589856 | tf_op jit(solution)/shard_map/ppermute | solution.py:471
  848.9 10.1 %shard_map.343.refs_3_ = f32[192,8960]{1,0:T(8,128)} custom-call(s32[1]{0:T(128)} %bitcast.26.refs_0_, bf16[8,192,512]{2,1,0:T(8,128)(2,1)} %all-to-all-done.3.refs_3_.refs_1_, bf16[8,192,512]{2,1,0:T(8,128)(2,1)} %collective-permute-done.65.refs_3_.refs_2_, bf16[8,192,640]{2,1,0:T(8,128)(2,1)} %all-to-all-done.6.refs_3_, ...), custom_call_target="tpu_custom_call" | custom-call | flops 999999995904 | bytes 1024 | tf_op jit(solution)/shard_map/pallas_call | solution.py:529
  (529 shorter events, 472.0 us)
Async XLA Ops:
  7.2 113.8 %all-gather.2.cloned.1.call-start = ((), (), s32[]{:S(2)}) async-start(), calls=%async_computation.11 | async-start | bytes 1966080 | tf_op jit(solution)/shard_map/all_gather | solution.py:702
  57.3 84.6 %collective-permute-start.18 = (bf16[192,1536]{1,0:T(8,128)(2,1)}, bf16[192,1536]{1,0:T(8,128)(2,1)}, u32[]{:S(2)}, u32[]{:S(2)}) collective-permute-start(bf16[192,1536]{1,0:T(8,128)(2,1)} %shard_map.291.refs_11_.refs_1_), channel_id=1, source_target_pairs={{0,4},{4,0},{8,12},{12,8},{16,20},{20,16},{24,28},{28,24},{1,5},{5... | collective-permute-start | bytes 1769480 | tf_op jit(solution)/shard_map/ppermute | solution.py:218
  72.9 45.6 %collective-permute-start.35 = (bf16[384,1536]{1,0:T(8,128)(2,1)}, bf16[384,1536]{1,0:T(8,128)(2,1)}, u32[]{:S(2)}, u32[]{:S(2)}) collective-permute-start(bf16[384,1536]{1,0:T(8,128)(2,1)} %shard_map.293.refs_2_.refs_1_), channel_id=1, source_target_pairs={{0,8},{4,12},{8,0},{12,4},{16,24},{20,28},{24,16},{28,20},{1,9},{5... | collective-permute-start | bytes 3538952 | tf_op jit(solution)/shard_map/ppermute | solution.py:218
  88.2 108.3 %all-to-all-start = ((bf16[8,192,1024]{2,1,0:T(8,128)(2,1)}), bf16[8,192,1024]{2,1,0:T(8,128)(2,1)}, u32[]{:S(2)}, u32[]{:S(2)}) async-start(bf16[8,192,1024]{2,1,0:T(8,128)(2,1)} %shard_map.294.refs_7_), calls=%async_computation | async-start | bytes 6291456 | tf_op jit(solution)/shard_map/all_to_all | solution.py:665
  216.0 67.0 %all-to-all-start.1 = ((bf16[8,192,1280]{2,1,0:T(8,128)(2,1)}), bf16[8,192,1280]{2,1,0:T(8,128)(2,1)}, u32[]{:S(2)}, u32[]{:S(2)}) async-start(bf16[8,192,1280]{2,1,0:T(8,128)(2,1)} %shard_map.298.refs_11_), calls=%async_computation.1 | async-start | bytes 7864320 | tf_op jit(solution)/shard_map/all_to_all | solution.py:665
  280.5 78.1 %collective-permute-start.45 = (bf16[8,192,512]{2,1,0:T(8,128)(2,1)}, bf16[8,192,512]{2,1,0:T(8,128)(2,1)}, u32[]{:S(2)}, u32[]{:S(2)}) collective-permute-start(bf16[8,192,512]{2,1,0:T(8,128)(2,1)} %get-tuple-element.738), channel_id=1, source_target_pairs={{0,1},{3,2},{4,5},{7,6},{8,9},{11,10},{12,13},{15,14},{16,17},{19,... | collective-permute-start | bytes 4718600 | tf_op jit(solution)/shard_map/ppermute | solution.py:463
  316.3 45.2 %collective-permute-start.44 = (bf16[8,192,512]{2,1,0:T(8,128)(2,1)}, bf16[8,192,512]{2,1,0:T(8,128)(2,1)}, u32[]{:S(2)}, u32[]{:S(2)}) collective-permute-start(bf16[8,192,512]{2,1,0:T(8,128)(2,1)} %bitcast.16.refs_5_), channel_id=1, source_target_pairs={{1,2},{2,1},{5,6},{6,5},{9,10},{10,9},{13,14},{14,13},{17,18},{18,... | collective-permute-start | bytes 4718600 | tf_op jit(solution)/shard_map/ppermute | solution.py:467
  377.0 48.4 %collective-permute-start.51 = (bf16[8,192,512]{2,1,0:T(8,128)(2,1)}, bf16[8,192,512]{2,1,0:T(8,128)(2,1)}, u32[]{:S(2)}, u32[]{:S(2)}) collective-permute-start(bf16[8,192,512]{2,1,0:T(8,128)(2,1)} %bitcast.19.refs_2_), channel_id=1, source_target_pairs={{1,2},{2,1},{5,6},{6,5},{9,10},{10,9},{13,14},{14,13},{17,18},{18,... | collective-permute-start | bytes 4718600 | tf_op jit(solution)/shard_map/ppermute | solution.py:467
  378.8 46.6 %all-to-all-start.2 = ((bf16[8,192,512]{2,1,0:T(8,128)(2,1)}), bf16[8,192,512]{2,1,0:T(8,128)(2,1)}, u32[]{:S(2)}, u32[]{:S(2)}) async-start(bf16[8,192,512]{2,1,0:T(8,128)(2,1)} %bitcast.107), calls=%async_computation.2 | async-start | bytes 3145728 | tf_op jit(solution)/shard_map/all_to_all | solution.py:723
  396.1 104.9 %collective-permute-start.52 = (bf16[640,1536]{1,0:T(8,128)(2,1)}, bf16[640,1536]{1,0:T(8,128)(2,1)}, u32[]{:S(2)}, u32[]{:S(2)}) collective-permute-start(bf16[640,1536]{1,0:T(8,128)(2,1)} %get-tuple-element.752.refs_0_), channel_id=1, source_target_pairs={{0,1},{3,2},{4,5},{7,6},{8,9},{11,10},{12,13},{15,14},{16,17},{19,... | collective-permute-start | bytes 5898248 | tf_op jit(solution)/shard_map/ppermute | solution.py:463
  405.9 73.2 %collective-permute-start.53 = (bf16[512,1536]{1,0:T(8,128)(2,1)}, bf16[512,1536]{1,0:T(8,128)(2,1)}, u32[]{:S(2)}, u32[]{:S(2)}) collective-permute-start(bf16[512,1536]{1,0:T(8,128)(2,1)} %get-tuple-element.749.refs_0_), channel_id=1, source_target_pairs={{0,1},{3,2},{4,5},{7,6},{8,9},{11,10},{12,13},{15,14},{16,17},{19,... | collective-permute-start | bytes 4718600 | tf_op jit(solution)/shard_map/ppermute | solution.py:463
  425.5 53.7 %collective-permute-start.54 = (bf16[8,192,512]{2,1,0:T(8,128)(2,1)}, bf16[8,192,512]{2,1,0:T(8,128)(2,1)}, u32[]{:S(2)}, u32[]{:S(2)}) collective-permute-start(bf16[8,192,512]{2,1,0:T(8,128)(2,1)} %all-to-all-done.2.refs_3_.refs_1_), channel_id=1, source_target_pairs={{1,0},{2,3},{5,4},{6,7},{9,8},{10,11},{13,12},{14,15},{17,16},{18,... | collective-permute-start | bytes 4718600 | tf_op jit(solution)/shard_map/ppermute | solution.py:471
  429.7 49.4 %all-to-all-start.3 = ((bf16[8,192,512]{2,1,0:T(8,128)(2,1)}), bf16[8,192,512]{2,1,0:T(8,128)(2,1)}, u32[]{:S(2)}, u32[]{:S(2)}) async-start(bf16[8,192,512]{2,1,0:T(8,128)(2,1)} %bitcast.22.refs_4_), calls=%async_computation.3 | async-start | bytes 3145728 | tf_op jit(solution)/shard_map/all_to_all | solution.py:723
  434.7 104.6 %reduce-scatter.5.cloned.1.call-start = ((), (), s32[]{:S(2)}) async-start(), calls=%async_computation.12 | async-start | bytes 10616832 | tf_op jit(solution)/shard_map/reduce_scatter | solution.py:797
  452.8 249.6 %reduce-scatter.9.cloned.1.call-start = ((), (), s32[]{:S(2)}) async-start(), calls=%async_computation.14 | async-start | bytes 5308416 | tf_op jit(solution)/shard_map/reduce_scatter | solution.py:825
  482.7 51.8 %collective-permute-start.55 = (bf16[512,1536]{1,0:T(8,128)(2,1)}, bf16[512,1536]{1,0:T(8,128)(2,1)}, u32[]{:S(2)}, u32[]{:S(2)}) collective-permute-start(bf16[512,1536]{1,0:T(8,128)(2,1)} %shard_map.315.refs_8_.refs_0_), channel_id=1, source_target_pairs={{1,2},{2,1},{5,6},{6,5},{9,10},{10,9},{13,14},{14,13},{17,18},{18,... | collective-permute-start | bytes 4718600 | tf_op jit(solution)/shard_map/ppermute | solution.py:467
  523.2 47.9 %collective-permute-start.56 = (bf16[8,192,640]{2,1,0:T(8,128)(2,1)}, bf16[8,192,640]{2,1,0:T(8,128)(2,1)}, u32[]{:S(2)}, u32[]{:S(2)}) collective-permute-start(bf16[8,192,640]{2,1,0:T(8,128)(2,1)} %get-tuple-element.762.refs_0_), channel_id=1, source_target_pairs={{0,1},{3,2},{4,5},{7,6},{8,9},{11,10},{12,13},{15,14},{16,17},{19,... | collective-permute-start | bytes 5898248 | tf_op jit(solution)/shard_map/ppermute | solution.py:463
  531.3 95.8 %collective-permute-start.58 = (bf16[640,1536]{1,0:T(8,128)(2,1)}, bf16[640,1536]{1,0:T(8,128)(2,1)}, u32[]{:S(2)}, u32[]{:S(2)}) collective-permute-start(bf16[640,1536]{1,0:T(8,128)(2,1)} %shard_map.317.refs_0_), channel_id=1, source_target_pairs={{1,2},{2,1},{5,6},{6,5},{9,10},{10,9},{13,14},{14,13},{17,18},{18,... | collective-permute-start | bytes 5898248 | tf_op jit(solution)/shard_map/ppermute | solution.py:467
  533.2 123.1 %collective-permute-start.65 = (bf16[8,192,512]{2,1,0:T(8,128)(2,1)}, bf16[8,192,512]{2,1,0:T(8,128)(2,1)}, u32[]{:S(2)}, u32[]{:S(2)}) collective-permute-start(bf16[8,192,512]{2,1,0:T(8,128)(2,1)} %all-to-all-done.3.refs_3_.refs_1_), channel_id=1, source_target_pairs={{1,0},{2,3},{5,4},{6,7},{9,8},{10,11},{13,12},{14,15},{17,16},{18,... | collective-permute-start | bytes 4718600 | tf_op jit(solution)/shard_map/ppermute | solution.py:471
  538.0 157.9 %collective-permute-start.62 = (bf16[512,1536]{1,0:T(8,128)(2,1)}, bf16[512,1536]{1,0:T(8,128)(2,1)}, u32[]{:S(2)}, u32[]{:S(2)}) collective-permute-start(bf16[512,1536]{1,0:T(8,128)(2,1)} %shard_map.319.refs_1_), channel_id=1, source_target_pairs={{1,0},{2,3},{5,4},{6,7},{9,8},{10,11},{13,12},{14,15},{17,16},{18,... | collective-permute-start | bytes 4718600 | tf_op jit(solution)/shard_map/ppermute | solution.py:471
  575.8 57.7 %all-to-all-start.4 = ((bf16[4,384,512]{2,1,0:T(8,128)(2,1)}), bf16[4,384,512]{2,1,0:T(8,128)(2,1)}, u32[]{:S(2)}, u32[]{:S(2)}) async-start(bf16[4,384,512]{2,1,0:T(8,128)(2,1)} %pad_maximum_fusion.4), calls=%async_computation.5 | async-start | bytes 3145728 | tf_op jit(solution)/shard_map/all_to_all | solution.py:817
  580.2 146.9 %reduce-scatter.7.cloned.1.call-start = ((), (), s32[]{:S(2)}) async-start(), calls=%async_computation.13 | async-start | bytes 5308416 | tf_op jit(solution)/shard_map/reduce_scatter | solution.py:825
  580.2 76.1 %collective-permute-start.64 = (bf16[8,192,640]{2,1,0:T(8,128)(2,1)}, bf16[8,192,640]{2,1,0:T(8,128)(2,1)}, u32[]{:S(2)}, u32[]{:S(2)}) collective-permute-start(bf16[8,192,640]{2,1,0:T(8,128)(2,1)} %bitcast.30), channel_id=1, source_target_pairs={{1,2},{2,1},{5,6},{6,5},{9,10},{10,9},{13,14},{14,13},{17,18},{18,... | collective-permute-start | bytes 5898248 | tf_op jit(solution)/shard_map/ppermute | solution.py:467
  598.9 51.2 %collective-permute-start.60 = (bf16[8,192,640]{2,1,0:T(8,128)(2,1)}, bf16[8,192,640]{2,1,0:T(8,128)(2,1)}, u32[]{:S(2)}, u32[]{:S(2)}) collective-permute-start(bf16[8,192,640]{2,1,0:T(8,128)(2,1)} %get-tuple-element.770.refs_0_), channel_id=1, source_target_pairs={{0,1},{3,2},{4,5},{7,6},{8,9},{11,10},{12,13},{15,14},{16,17},{19,... | collective-permute-start | bytes 5898248 | tf_op jit(solution)/shard_map/ppermute | solution.py:463
  632.3 63.7 %collective-permute-start.63 = (bf16[640,1536]{1,0:T(8,128)(2,1)}, bf16[640,1536]{1,0:T(8,128)(2,1)}, u32[]{:S(2)}, u32[]{:S(2)}) collective-permute-start(bf16[640,1536]{1,0:T(8,128)(2,1)} %shard_map.325.refs_3_), channel_id=1, source_target_pairs={{1,0},{2,3},{5,4},{6,7},{9,8},{10,11},{13,12},{14,15},{17,16},{18,... | collective-permute-start | bytes 5898248 | tf_op jit(solution)/shard_map/ppermute | solution.py:471
  654.4 57.0 %collective-permute-start.61 = (bf16[8,192,640]{2,1,0:T(8,128)(2,1)}, bf16[8,192,640]{2,1,0:T(8,128)(2,1)}, u32[]{:S(2)}, u32[]{:S(2)}) collective-permute-start(bf16[8,192,640]{2,1,0:T(8,128)(2,1)} %bitcast.28.refs_2_), channel_id=1, source_target_pairs={{1,2},{2,1},{5,6},{6,5},{9,10},{10,9},{13,14},{14,13},{17,18},{18,... | collective-permute-start | bytes 5898248 | tf_op jit(solution)/shard_map/ppermute | solution.py:467
  664.5 98.7 %reduce-scatter.11.cloned.1.call-start = ((), (), s32[]{:S(2)}) async-start(), calls=%async_computation.15 | async-start | bytes 2064384 | tf_op jit(solution)/shard_map/reduce_scatter | solution.py:825
  694.6 49.4 %collective-permute-start.67 = (bf16[8,192,640]{2,1,0:T(8,128)(2,1)}, bf16[8,192,640]{2,1,0:T(8,128)(2,1)}, u32[]{:S(2)}, u32[]{:S(2)}) collective-permute-start(bf16[8,192,640]{2,1,0:T(8,128)(2,1)} %all-to-all-done.5.refs_6_.refs_3_), channel_id=1, source_target_pairs={{1,0},{2,3},{5,4},{6,7},{9,8},{10,11},{13,12},{14,15},{17,16},{18,... | collective-permute-start | bytes 5898248 | tf_op jit(solution)/shard_map/ppermute | solution.py:471
  717.6 57.8 %all-to-all-start.6 = ((bf16[8,192,640]{2,1,0:T(8,128)(2,1)}), bf16[8,192,640]{2,1,0:T(8,128)(2,1)}, u32[]{:S(2)}, u32[]{:S(2)}) async-start(bf16[8,192,640]{2,1,0:T(8,128)(2,1)} %bitcast.33.refs_2_), calls=%async_computation.10 | async-start | bytes 3932160 | tf_op jit(solution)/shard_map/all_to_all | solution.py:723
  782.3 65.3 %collective-permute-start.75 = (bf16[8,192,640]{2,1,0:T(8,128)(2,1)}, bf16[8,192,640]{2,1,0:T(8,128)(2,1)}, u32[]{:S(2)}, u32[]{:S(2)}) collective-permute-start(bf16[8,192,640]{2,1,0:T(8,128)(2,1)} %all-to-all-done.6.refs_3_), channel_id=1, source_target_pairs={{1,0},{2,3},{5,4},{6,7},{9,8},{10,11},{13,12},{14,15},{17,16},{18,... | collective-permute-start | bytes 5898248 | tf_op jit(solution)/shard_map/ppermute | solution.py:471
  783.6 61.7 %collective-permute-start.71 = (bf16[192,1536]{1,0:T(8,128)(2,1)}, bf16[192,1536]{1,0:T(8,128)(2,1)}, u32[]{:S(2)}, u32[]{:S(2)}) collective-permute-start(bf16[192,1536]{1,0:T(8,128)(2,1)} %shard_map.339.refs_2_.refs_1_), channel_id=1, source_target_pairs={{1,0},{2,3},{5,4},{6,7},{9,8},{10,11},{13,12},{14,15},{17,16},{18,... | collective-permute-start | bytes 1769480 | tf_op jit(solution)/shard_map/ppermute | solution.py:471
  787.4 71.6 %collective-permute-start.74 = (bf16[224,512]{1,0:T(8,128)(2,1)}, bf16[224,512]{1,0:T(8,128)(2,1)}, u32[]{:S(2)}, u32[]{:S(2)}) collective-permute-start(bf16[224,512]{1,0:T(8,128)(2,1)} %shard_map.341.refs_3_.refs_1_), channel_id=1, source_target_pairs={{1,0},{2,3},{5,4},{6,7},{9,8},{10,11},{13,12},{14,15},{17,16},{18,... | collective-permute-start | bytes 688136 | tf_op jit(solution)/shard_map/ppermute | solution.py:471
  (149 other events, 1602.9 us)
Sparse Core Ops, SparseCore 0:
  48.3 37.9 all-gather.1
  452.9 78.7 reduce-scatter.4
  548.9 56.2 reduce-scatter.8
  627.2 65.1 reduce-scatter.6
  695.6 52.4 reduce-scatter.10

commit v5 on v4

--- a/solution.py
+++ b/solution.py
@@ -916,12 +916,12 @@
     packed, layer_out = line.step(pack_step)
     kv_share = scatter_weight(packed)
     output_in = to_middle(output_share)
+    output_sum = add(output_share, output_in)
+    output_across = across_middle(output_sum)
     down = (down_1_total, down_1_ends), (down_2_total, down_2_ends)
     grad_down = line.kernel(lambda earlier: stack_rows(earlier, down, hidden_width), gate_2_total)
     gate_2_ends = to_ends(gate_2_total)
     up_2_total = rows_exchange(add(up_2_sum, up_2_across))
-    output_sum = add(output_share, output_in)
-    output_across = across_middle(output_sum)
     query_share = held(query_share)
     query_in = to_middle(query_share)
     output_total = add(output_sum, output_across)

time: 885 us -> 879 us (level)
  transfers between devices with their start and end apart: 88 -> 88, of which waited for: 26 -> 27; matrix products, arithmetic and copies ran while one was open for 20% -> 20% of each run, Pallas kernels for 32% -> 32%
where the time goes in v5:
time: 879 us; the launch traced here: 868 us
  Pallas kernels  286 us (33%)
  waiting for transfers between devices  182 us (21%)
  starting transfers between devices  144 us (16%)
  matrix products  94.4 us (11%)
  local copies, waits for them, and re-layouts  93.3 us (11%)
  other arithmetic  43.7 us (5%)
  between operations  16.6 us (2%)
    ppermute x49, waiting for transfers between devices, swap_fsdp(): return lax.ppermute(values, 'fsdp', [(i, i ^ mask) for i in range(count)])  98.1 us
    dot_general x8, matrix products, contract_first(): lax.dot_general(left, right, (((0,), (0,)), ((), ())), preferred_element_...  73.5 us
    ppermute x9, waiting for transfers between devices, to_ends(): return lax.ppermute(values, 'sp', [(1, 0), (2, 3)])  65.8 us
    pallas_call x18, Pallas kernels, add_low(): return call(left, right, *earlier).reshape(shape)  54.8 us
    ppermute x9, starting transfers between devices, to_middle(): return lax.ppermute(values, 'sp', [(0, 1), (3, 2)])  53.7 us
    pallas_call x3, Pallas kernels, row_products(): return call(order, *operands, *earlier)  52 us
    pallas_call x2, Pallas kernels, activate(): return call(*operands, *earlier)  51.9 us
    unnamed x193, local copies, waits for them, and re-layouts  40.9 us
  transfers between devices with their start and end apart: 88, of which 27 were waited for; matrix products, arithmetic and copies ran while one was open for 20% of the time, Pallas kernels for 32%

profile of v5, /device:TPU:2, one launch (start us, length us, event | category | flops | bytes accessed | tf_op | source)
XLA Modules:
  0.0 867.9 jit_solution(6743457422976987656)
XLA Ops:
  59.9 11.7 %collective-permute-done.16.refs_3_ = bf16[192,1536]{1,0:T(8,128)(2,1)} collective-permute-done((bf16[192,1536]{1,0:T(8,128)(2,1)}, bf16[192,1536]{1,0:T(8,128)(2,1)}, u32[]{:S(2)}, u32[]{:S(2)}) %collective-permute-start.16) | collective-permute-done | bytes 589856 | tf_op jit(solution)/shard_map/ppermute | solution.py:218
  108.5 10.1 %collective-permute-done.23.refs_9_ = bf16[96,1536]{1,0:T(8,128)(2,1)} collective-permute-done((bf16[96,1536]{1,0:T(8,128)(2,1)}, bf16[96,1536]{1,0:T(8,128)(2,1)}, u32[]{:S(2)}, u32[]{:S(2)}) %collective-permute-start.23) | collective-permute-done | bytes 294944 | tf_op jit(solution)/shard_map/ppermute | solution.py:218
  122.4 19.4 %shard_map.295 = (bf16[384,1536]{1,0:T(8,128)(2,1)S(1)}, bf16[384,1536]{1,0:T(8,128)(2,1)}) custom-call(f32[384,1536]{1,0:T(8,128)S(1)} %convolution_add_fusion.1.refs_0_, bf16[1536,512]{1,0:T(8,128)(2,1)S(1)} %copy-done.4, bf16[1536,512]{1,0:T(8,128)(2,1)S(1)} %copy-done.4, f32[384,128]{1,0:T(8,128)S(1)} %copy-done.51, f32[384,128]{1,0:T(8,128)S(1)} %copy-done.39, ...), custom_call_target="tpu_custom_call" | custom-call | flops 999999995904 | bytes 1024 | tf_op jit(solution)/shard_map/pallas_call | solution.py:109
  158.9 23.8 %collective-permute-done.26.refs_13_.refs_3_ = bf16[384,1536]{1,0:T(8,128)(2,1)} collective-permute-done((bf16[384,1536]{1,0:T(8,128)(2,1)}, bf16[384,1536]{1,0:T(8,128)(2,1)}, u32[]{:S(2)}, u32[]{:S(2)}) %collective-permute-start.26) | collective-permute-done | bytes 1179680 | tf_op jit(solution)/shard_map/ppermute | solution.py:218
  230.8 22.6 %shard_map.300 = (bf16[3072,512]{1,0:T(8,128)(2,1)S(1)}, bf16[3072,1024]{1,0:T(8,128)(2,1)}) custom-call(bf16[3072,1536]{1,0:T(8,128)(2,1)} %shard_map.299.refs_0_.refs_4_, bf16[3072,1536]{1,0:T(8,128)(2,1)} %shard_map.297.refs_2_.refs_1_, bf16[1536,1024]{1,0:T(8,128)(2,1)} %bitcast.13.refs_12_.refs_2_.refs_3_, bf16[1152,1536]{1,0:T(8,128)(2,1)} %pad.8.refs_3_, ...), custom_call_target="tpu_custom_call" | custom-call | flops 999999995904 | bytes 1024 | tf_op jit(solution)/shard_map/pallas_call | solution.py:591
  255.1 20.2 %conditional.42 = (pred[]{:T(512)}, bf16[8,192,512]{2,1,0:T(8,128)(2,1)}, bf16[8,192,512]{2,1,0:T(8,128)(2,1)}, bf16[1]{0:T(256)(128)(2,1)}, bf16[1536,512]{1,0:...) conditional(s32[]{:T(128)} %convert_element_type.263, pred[]{:T(512)} %gt.8, ...), branch_computations={%region_4.5_spmd.clone.clone, %region_5.6_spmd.clone.clone} | conditional | flops 9665249280 | bytes 31457332
  255.3 14.1 %convolution_convert_fusion.1 = bf16[1536,1024]{1,0:T(8,128)(2,1)S(1)} fusion(bf16[3072,1536]{1,0:T(8,128)(2,1)} %get-tuple-element.1090, bf16[3072,1024]{1,0:T(8,128)(2,1)} %get-tuple-element.1091), kind=kOutput, calls=%fused_computation.5 | convolution fusion | flops 9665249280 | bytes 18874368 | tf_op jit(solution)/shard_map/cond/branch_1_fun/dot_general | solution.py:59
  283.0 29.3 %shard_map.302 = (bf16[3072,640]{1,0:T(8,128)(2,1)}, bf16[3072,1280]{1,0:T(8,128)(2,1)}) custom-call(bf16[3072,1536]{1,0:T(8,128)(2,1)} %shard_map.299.refs_0_.refs_4_, bf16[3072,1536]{1,0:T(8,128)(2,1)} %shard_map.297.refs_2_.refs_1_, bf16[1536,1280]{1,0:T(8,128)(2,1)} %bitcast.15.refs_2_.refs_4_, bf16[1152,1536]{1,0:T(8,128)(2,1)} %pad.8.refs_3_, ...), custom_call_target="tpu_custom_call" | custom-call | flops 999999995904 | bytes 1024 | tf_op jit(solution)/shard_map/pallas_call | solution.py:591
  318.2 17.2 %shard_map.304.refs_5_ = bf16[1536,1536]{1,0:T(8,128)(2,1)} custom-call(s32[4]{0:T(128)} %broadcast_xor_fusion.refs_0_, bf16[3072,1024]{1,0:T(8,128)(2,1)} %get-tuple-element.730.refs_1_, bf16[3072,1280]{1,0:T(8,128)(2,1)} %get-tuple-element.739.refs_2_, bf16[1536,1024]{1,0:T(8,128)(2,1)} %bitcast.13.refs_12_.refs_2_.refs_3_, ...), custom_call_target="tpu_custom_call" | custom-call | flops 999999995904 | bytes 1024 | tf_op jit(solution)/shard_map/pallas_call | solution.py:613
  335.4 17.2 %shard_map.305.refs_0_.refs_2_ = bf16[1536,1536]{1,0:T(8,128)(2,1)} custom-call(s32[4]{0:T(128)} %multiply_xor_fusion.refs_0_, bf16[3072,1024]{1,0:T(8,128)(2,1)} %get-tuple-element.730.refs_1_, bf16[3072,1280]{1,0:T(8,128)(2,1)} %get-tuple-element.739.refs_2_, bf16[1536,1024]{1,0:T(8,128)(2,1)} %bitcast.13.refs_12_.refs_2_.refs_3_, ...), custom_call_target="tpu_custom_call" | custom-call | flops 999999995904 | bytes 1024 | tf_op jit(solution)/shard_map/pallas_call | solution.py:613
  364.5 12.5 %conditional.43 = (pred[]{:T(512)}, bf16[512,1536]{1,0:T(8,128)(2,1)}, bf16[1]{0:T(256)(128)(2,1)}) conditional(s32[]{:T(128)} %convert_element_type.328, pred[]{:T(512)} %get-tuple-element.1051, (bf16[3072,512]{1,0:T(8,128)(2,1)}, bf16[3072,1536]{1,0:T(8,128)(2,1)}, bf16[8,192,512]{2,1,0:T(8,128)(2,1)}, pred[]{:T(512)}) %tuple.496), branch_computations={%region_6.7_spmd.clone.clone, %region_7.8_spmd.clone.clone} | conditional | flops 4832624640 | bytes 14155804
  364.9 10.3 %convolution_convert_fusion.2 = bf16[512,1536]{1,0:T(8,128)(2,1)} fusion(bf16[3072,512]{1,0:T(8,128)(2,1)} %get-tuple-element.1103, bf16[3072,1536]{1,0:T(8,128)(2,1)} %get-tuple-element.1104), kind=kOutput, calls=%fused_computation.6 | convolution fusion | flops 4832624640 | bytes 14155776 | tf_op jit(solution)/shard_map/cond/branch_1_fun/dot_general | solution.py:59
  383.2 12.9 %conditional.44 = (pred[]{:T(512)}, bf16[640,1536]{1,0:T(8,128)(2,1)}, bf16[1]{0:T(256)(128)(2,1)}) conditional(s32[]{:T(128)} %convert_element_type.329, pred[]{:T(512)} %get-tuple-element.1056, (bf16[3072,640]{1,0:T(8,128)(2,1)}, bf16[3072,1536]{1,0:T(8,128)(2,1)}, bf16[384,1536]{1,0:T(8,128)(2,1)}, pred[]{:T(512)}) %tuple.475), branch_computations={%region_8.9_spmd.clone.clone, %region_9.10_spmd.clone.clone} | conditional | flops 6040780800 | bytes 15335452
  383.2 11.1 %convolution_convert_fusion.3 = bf16[640,1536]{1,0:T(8,128)(2,1)} fusion(bf16[3072,640]{1,0:T(8,128)(2,1)} %get-tuple-element.1113, bf16[3072,1536]{1,0:T(8,128)(2,1)} %get-tuple-element.1114), kind=kOutput, calls=%fused_computation.7 | convolution fusion | flops 6040780800 | bytes 15335424 | tf_op jit(solution)/shard_map/cond/branch_1_fun/dot_general | solution.py:59
  408.4 11.0 %collective-permute-done.47.refs_2_ = bf16[192,1536]{1,0:T(8,128)(2,1)} collective-permute-done((bf16[192,1536]{1,0:T(8,128)(2,1)}, bf16[192,1536]{1,0:T(8,128)(2,1)}, u32[]{:S(2)}, u32[]{:S(2)}) %collective-permute-start.47) | collective-permute-done | bytes 589856 | tf_op jit(solution)/shard_map/ppermute | solution.py:218
  435.2 17.5 %shard_map.313 = bf16[3072,1536]{1,0:T(8,128)(2,1)} custom-call(s32[8]{0:T(128)} %iota.40.refs_0_, bf16[3072,512]{1,0:T(8,128)(2,1)S(1)} %copy-done.86, bf16[3072,640]{1,0:T(8,128)(2,1)} %get-tuple-element.736.refs_2_, bf16[1152,1536]{1,0:T(8,128)(2,1)} %pad.8.refs_3_, bf16[8,192,512]{2,1,0:T(8,128)(2,1)} %bitcast.22.refs_4_), custom_call_target="tpu_custom_call" | custom-call | flops 999999995904 | bytes 1024 | tf_op jit(solution)/shard_map/pallas_call | solution.py:613
  458.8 18.6 %conditional.40 = (pred[]{:T(512)}, f32[1536]{0:T(1024)S(1)}, f32[384,1536]{1,0:T(8,128)}, bf16[384,1536]{1,0:T(8,128)(2,1)}, bf16[384,1536]{1,0:T(8,128)(2,1)}, /*index=5*/bf16[1]{0:T(256)(128)(2,1)}, s32[]{:T(128)}) conditional(s32[]{:T(128)} %convert_element_type.330, pred[]{:T(512)} %get-tuple-element.1061, ...), branch_computations={%region_10.11_spmd.clone, %region_11.14_spmd.clone} | conditional | flops 1825504512 | bytes 24821828
  484.7 16.3 %shard_map.316 = (bf16[384,768]{1,0:T(8,128)(2,1)S(1)}, bf16[1536,256]{1,0:T(8,128)(2,1)S(1)}) custom-call(bf16[384,1536]{1,0:T(8,128)(2,1)S(1)} %copy-done.19, bf16[384,1536]{1,0:T(8,128)(2,1)} %get-tuple-element.755.refs_1_, bf16[1536,512]{1,0:T(8,128)(2,1)S(1)} %copy-done.5, bf16[1536,512]{1,0:T(8,128)(2,1)S(1)} %copy-done.5, f32[384,128]{1,0:T(8,128)S(1)} %copy-done.52, ...), custom_call_target="tpu_custom_call" | custom-call | flops 999999995904 | bytes 1024 | tf_op jit(solution)/shard_map/pallas_call | solution.py:175
  506.2 15.8 %conditional.45 = (pred[]{:T(512)}, bf16[8,192,640]{2,1,0:T(8,128)(2,1)}, bf16[1]{0:T(256)(128)(2,1)}, bf16[1536,640]{1,0:T(8,128)(2,1)S(1)}) conditional(s32[]{:T(128)} %get-tuple-element.1062, pred[]{:T(512)} %get-tuple-element.808, (bf16[3072,1280]{1,0:T(8,128)(2,1)}, bf16[3072,1536]{1,0:T(8,128)(2,1)}, ...), branch_computations={%region_14.15_spmd.clone.clone, %region_15.16_spmd.clone.clone} | conditional | flops 6040780800 | bytes 19267620
  506.2 12.4 %fusion.3 = bf16[1536,640]{1,0:T(8,128)(2,1)} fusion(bf16[3072,1536]{1,0:T(8,128)(2,1)} %get-tuple-element.1124, bf16[3072,1280]{1,0:T(8,128)(2,1)} %get-tuple-element.1125), kind=kOutput, calls=%fused_computation.10 | convolution fusion | flops 6040780800 | bytes 15335424 | tf_op jit(solution)/shard_map/cond/branch_1_fun/dot_general | solution.py:59
  551.5 16.5 %shard_map.321 = (bf16[384,768]{1,0:T(8,128)(2,1)S(1)}, bf16[1536,256]{1,0:T(8,128)(2,1)S(1)}) custom-call(bf16[384,1536]{1,0:T(8,128)(2,1)S(1)} %copy-done.20, bf16[384,1536]{1,0:T(8,128)(2,1)} %get-tuple-element.755.refs_1_, bf16[1536,512]{1,0:T(8,128)(2,1)S(1)} %copy-done.6, bf16[1536,512]{1,0:T(8,128)(2,1)S(1)} %copy-done.6, f32[384,128]{1,0:T(8,128)S(1)} %copy-done.53, ...), custom_call_target="tpu_custom_call" | custom-call | flops 999999995904 | bytes 1024 | tf_op jit(solution)/shard_map/pallas_call | solution.py:175
  582.2 15.4 %conditional.48 = (pred[]{:T(512)}, bf16[8,192,640]{2,1,0:T(8,128)(2,1)}, bf16[1]{0:T(256)(128)(2,1)}, bf16[1536,640]{1,0:T(8,128)(2,1)S(1)}) conditional(s32[]{:T(128)} %convert_element_type.334, pred[]{:T(512)} %get-tuple-element.1074, (bf16[3072,1280]{1,0:T(8,128)(2,1)}, bf16[3072,1536]{1,0:T(8,128)(2,1)}, ...), branch_computations={%region_19.20_spmd.clone.clone, %region_20.21_spmd.clone.clone} | conditional | flops 6040780800 | bytes 19267622
  582.2 12.5 %fusion.8 = bf16[1536,640]{1,0:T(8,128)(2,1)} fusion(bf16[3072,1536]{1,0:T(8,128)(2,1)} %get-tuple-element.1149, bf16[3072,1280]{1,0:T(8,128)(2,1)} %get-tuple-element.1150), kind=kOutput, calls=%fused_computation.14 | convolution fusion | flops 6040780800 | bytes 15335424 | tf_op jit(solution)/shard_map/cond/branch_1_fun/dot_general | solution.py:59
  605.0 20.6 %conditional.36 = (pred[]{:T(512)}, f32[384,1536]{1,0:T(8,128)S(1)}, bf16[1536]{0:T(1024)(128)(2,1)S(1)}, bf16[1]{0:T(256)(128)(2,1)}, s32[]{:T(128)}, /*index=5*/bf16[1536,1536]{1,0:T(8,128)(2,1)}) conditional(s32[]{:T(128)} %convert_element_type.335, pred[]{:T(512)} %get-tuple-element.1080, (bf16[384,768]{1,0:T(8,128)(2,1)}, ...), branch_computations={%region_21.22_spmd.clone, %region_22.24_spmd.clone} | conditional | flops 3627416064 | bytes 28314680
  633.6 14.7 %conditional.41 = (bf16[1536,512]{0,1:T(8,128)(2,1)}, bf16[1536]{0:T(1024)(128)(2,1)S(1)}, f32[384,1536]{1,0:T(8,128)}, bf16[512]{0:T(512)(128)(2,1)S(1)}, bf16[1]{0:T(256)(128)(2,1)}, /*index=5*/s32[]{:T(128)}) conditional(s32[]{:T(128)} %get-tuple-element.812, pred[]{:T(512)} %get-tuple-element.772, (bf16[4,384,512]{2,1,0:T(8,128)(2,1)}, ...), branch_computations={%region_24.25_spmd, %region_25.31_spmd} | conditional | flops 1222015744 | bytes 31696468
  664.5 11.9 %conditional.39 = (bf16[1792,512]{1,0:T(8,128)(2,1)}, bf16[384,1536]{1,0:T(8,128)(2,1)}) conditional(s32[]{:T(128)} %get-tuple-element.1082, () %tuple.295, (bf16[1536,512]{0,1:T(8,128)(2,1)}, bf16[1536]{0:T(1024)(128)(2,1)S(1)}, bf16[512]{0:T(512)(128)(2,1)S(1)}, bf16[1536]{0:T(1024)(128)(2,1)S(1)}, f32[1536]{0:T(1024)S(1)}, ...), branch_computations={%region_31.32_spmd, %region_32.37_spmd} | conditional | flops 10749852 | bytes 14748142 | solution.py:355
  684.0 10.6 %all-to-all-done.5.refs_6_.refs_3_ = bf16[8,192,640]{2,1,0:T(8,128)(2,1)} async-done(((bf16[8,192,640]{2,1,0:T(8,128)(2,1)}), bf16[8,192,640]{2,1,0:T(8,128)(2,1)}, u32[]{:S(2)}, u32[]{:S(2)}) %all-to-all-start.5) | async-done | bytes 1966112 | tf_op jit(solution)/shard_map/all_to_all | solution.py:723
  720.1 10.7 %collective-permute-start.66 = (bf16[192,1536]{1,0:T(8,128)(2,1)}, bf16[192,1536]{1,0:T(8,128)(2,1)}, u32[]{:S(2)}, u32[]{:S(2)}) collective-permute-start(bf16[192,1536]{1,0:T(8,128)(2,1)} %shard_map.333.refs_2_.refs_0_), channel_id=1, source_target_pairs={{0,1},{3,2},{4,5},{7,6},{8,9},{11,10},{12,13},{15,14},{16,17},{19,... | collective-permute-start | bytes 1769480 | tf_op jit(solution)/shard_map/ppermute | solution.py:463
  734.4 10.3 %collective-permute-done.67.refs_4_ = bf16[8,192,640]{2,1,0:T(8,128)(2,1)} collective-permute-done((bf16[8,192,640]{2,1,0:T(8,128)(2,1)}, bf16[8,192,640]{2,1,0:T(8,128)(2,1)}, u32[]{:S(2)}, u32[]{:S(2)}) %collective-permute-start.67) | collective-permute-done | bytes 1966112 | tf_op jit(solution)/shard_map/ppermute | solution.py:471
  744.6 10.1 %shard_map.335.refs_2_ = f32[192,8960]{1,0:T(8,128)} custom-call(s32[1]{0:T(128)} %bitcast.26.refs_0_, bf16[8,192,512]{2,1,0:T(8,128)(2,1)} %all-to-all-done.2.refs_3_.refs_1_, bf16[8,192,512]{2,1,0:T(8,128)(2,1)} %collective-permute-done.54.refs_4_.refs_2_, bf16[8,192,640]{2,1,0:T(8,128)(2,1)} %all-to-all-done.5.refs_6_.refs_3_, ...), custom_call_target="tpu_custom_call" | custom-call | flops 999999995904 | bytes 1024 | tf_op jit(solution)/shard_map/pallas_call | solution.py:529
  784.1 16.2 %collective-permute-done.71.refs_2_ = bf16[192,1536]{1,0:T(8,128)(2,1)} collective-permute-done((bf16[192,1536]{1,0:T(8,128)(2,1)}, bf16[192,1536]{1,0:T(8,128)(2,1)}, u32[]{:S(2)}, u32[]{:S(2)}) %collective-permute-start.71) | collective-permute-done | bytes 589856 | tf_op jit(solution)/shard_map/ppermute | solution.py:471
  802.7 39.3 %collective-permute-done.75.refs_4_ = bf16[8,192,640]{2,1,0:T(8,128)(2,1)} collective-permute-done((bf16[8,192,640]{2,1,0:T(8,128)(2,1)}, bf16[8,192,640]{2,1,0:T(8,128)(2,1)}, u32[]{:S(2)}, u32[]{:S(2)}) %collective-permute-start.75) | collective-permute-done | bytes 1966112 | tf_op jit(solution)/shard_map/ppermute | solution.py:471
  (529 shorter events, 482.7 us)
Async XLA Ops:
  7.2 113.8 %all-gather.2.cloned.1.call-start = ((), (), s32[]{:S(2)}) async-start(), calls=%async_computation.11 | async-start | bytes 1966080 | tf_op jit(solution)/shard_map/all_gather | solution.py:702
  57.3 84.6 %collective-permute-start.18 = (bf16[192,1536]{1,0:T(8,128)(2,1)}, bf16[192,1536]{1,0:T(8,128)(2,1)}, u32[]{:S(2)}, u32[]{:S(2)}) collective-permute-start(bf16[192,1536]{1,0:T(8,128)(2,1)} %shard_map.291.refs_11_.refs_1_), channel_id=1, source_target_pairs={{0,4},{4,0},{8,12},{12,8},{16,20},{20,16},{24,28},{28,24},{1,5},{5... | collective-permute-start | bytes 1769480 | tf_op jit(solution)/shard_map/ppermute | solution.py:218
  72.9 45.6 %collective-permute-start.35 = (bf16[384,1536]{1,0:T(8,128)(2,1)}, bf16[384,1536]{1,0:T(8,128)(2,1)}, u32[]{:S(2)}, u32[]{:S(2)}) collective-permute-start(bf16[384,1536]{1,0:T(8,128)(2,1)} %shard_map.293.refs_2_.refs_1_), channel_id=1, source_target_pairs={{0,8},{4,12},{8,0},{12,4},{16,24},{20,28},{24,16},{28,20},{1,9},{5... | collective-permute-start | bytes 3538952 | tf_op jit(solution)/shard_map/ppermute | solution.py:218
  79.8 38.8 %collective-permute-start.23 = (bf16[96,1536]{1,0:T(8,128)(2,1)}, bf16[96,1536]{1,0:T(8,128)(2,1)}, u32[]{:S(2)}, u32[]{:S(2)}) collective-permute-start(bf16[96,1536]{1,0:T(8,128)(2,1)} %slice.385), channel_id=1, source_target_pairs={{0,16},{4,20},{8,24},{12,28},{16,0},{20,4},{24,8},{28,12},{1,17},{... | collective-permute-start | bytes 884744 | tf_op jit(solution)/shard_map/ppermute | solution.py:218
  88.2 108.3 %all-to-all-start = ((bf16[8,192,1024]{2,1,0:T(8,128)(2,1)}), bf16[8,192,1024]{2,1,0:T(8,128)(2,1)}, u32[]{:S(2)}, u32[]{:S(2)}) async-start(bf16[8,192,1024]{2,1,0:T(8,128)(2,1)} %shard_map.294.refs_7_), calls=%async_computation | async-start | bytes 6291456 | tf_op jit(solution)/shard_map/all_to_all | solution.py:665
  216.0 67.0 %all-to-all-start.1 = ((bf16[8,192,1280]{2,1,0:T(8,128)(2,1)}), bf16[8,192,1280]{2,1,0:T(8,128)(2,1)}, u32[]{:S(2)}, u32[]{:S(2)}) async-start(bf16[8,192,1280]{2,1,0:T(8,128)(2,1)} %shard_map.298.refs_11_), calls=%async_computation.1 | async-start | bytes 7864320 | tf_op jit(solution)/shard_map/all_to_all | solution.py:665
  280.5 78.1 %collective-permute-start.45 = (bf16[8,192,512]{2,1,0:T(8,128)(2,1)}, bf16[8,192,512]{2,1,0:T(8,128)(2,1)}, u32[]{:S(2)}, u32[]{:S(2)}) collective-permute-start(bf16[8,192,512]{2,1,0:T(8,128)(2,1)} %get-tuple-element.738), channel_id=1, source_target_pairs={{0,1},{3,2},{4,5},{7,6},{8,9},{11,10},{12,13},{15,14},{16,17},{19,... | collective-permute-start | bytes 4718600 | tf_op jit(solution)/shard_map/ppermute | solution.py:463
  316.3 45.2 %collective-permute-start.44 = (bf16[8,192,512]{2,1,0:T(8,128)(2,1)}, bf16[8,192,512]{2,1,0:T(8,128)(2,1)}, u32[]{:S(2)}, u32[]{:S(2)}) collective-permute-start(bf16[8,192,512]{2,1,0:T(8,128)(2,1)} %bitcast.16.refs_5_), channel_id=1, source_target_pairs={{1,2},{2,1},{5,6},{6,5},{9,10},{10,9},{13,14},{14,13},{17,18},{18,... | collective-permute-start | bytes 4718600 | tf_op jit(solution)/shard_map/ppermute | solution.py:467
  377.0 48.4 %collective-permute-start.51 = (bf16[8,192,512]{2,1,0:T(8,128)(2,1)}, bf16[8,192,512]{2,1,0:T(8,128)(2,1)}, u32[]{:S(2)}, u32[]{:S(2)}) collective-permute-start(bf16[8,192,512]{2,1,0:T(8,128)(2,1)} %bitcast.19.refs_2_), channel_id=1, source_target_pairs={{1,2},{2,1},{5,6},{6,5},{9,10},{10,9},{13,14},{14,13},{17,18},{18,... | collective-permute-start | bytes 4718600 | tf_op jit(solution)/shard_map/ppermute | solution.py:467
  378.8 46.6 %all-to-all-start.2 = ((bf16[8,192,512]{2,1,0:T(8,128)(2,1)}), bf16[8,192,512]{2,1,0:T(8,128)(2,1)}, u32[]{:S(2)}, u32[]{:S(2)}) async-start(bf16[8,192,512]{2,1,0:T(8,128)(2,1)} %bitcast.107), calls=%async_computation.2 | async-start | bytes 3145728 | tf_op jit(solution)/shard_map/all_to_all | solution.py:723
  396.1 104.9 %collective-permute-start.52 = (bf16[640,1536]{1,0:T(8,128)(2,1)}, bf16[640,1536]{1,0:T(8,128)(2,1)}, u32[]{:S(2)}, u32[]{:S(2)}) collective-permute-start(bf16[640,1536]{1,0:T(8,128)(2,1)} %get-tuple-element.752.refs_0_), channel_id=1, source_target_pairs={{0,1},{3,2},{4,5},{7,6},{8,9},{11,10},{12,13},{15,14},{16,17},{19,... | collective-permute-start | bytes 5898248 | tf_op jit(solution)/shard_map/ppermute | solution.py:463
  405.9 73.2 %collective-permute-start.53 = (bf16[512,1536]{1,0:T(8,128)(2,1)}, bf16[512,1536]{1,0:T(8,128)(2,1)}, u32[]{:S(2)}, u32[]{:S(2)}) collective-permute-start(bf16[512,1536]{1,0:T(8,128)(2,1)} %get-tuple-element.749.refs_0_), channel_id=1, source_target_pairs={{0,1},{3,2},{4,5},{7,6},{8,9},{11,10},{12,13},{15,14},{16,17},{19,... | collective-permute-start | bytes 4718600 | tf_op jit(solution)/shard_map/ppermute | solution.py:463
  425.5 53.7 %collective-permute-start.54 = (bf16[8,192,512]{2,1,0:T(8,128)(2,1)}, bf16[8,192,512]{2,1,0:T(8,128)(2,1)}, u32[]{:S(2)}, u32[]{:S(2)}) collective-permute-start(bf16[8,192,512]{2,1,0:T(8,128)(2,1)} %all-to-all-done.2.refs_3_.refs_1_), channel_id=1, source_target_pairs={{1,0},{2,3},{5,4},{6,7},{9,8},{10,11},{13,12},{14,15},{17,16},{18,... | collective-permute-start | bytes 4718600 | tf_op jit(solution)/shard_map/ppermute | solution.py:471
  429.7 49.4 %all-to-all-start.3 = ((bf16[8,192,512]{2,1,0:T(8,128)(2,1)}), bf16[8,192,512]{2,1,0:T(8,128)(2,1)}, u32[]{:S(2)}, u32[]{:S(2)}) async-start(bf16[8,192,512]{2,1,0:T(8,128)(2,1)} %bitcast.22.refs_4_), calls=%async_computation.3 | async-start | bytes 3145728 | tf_op jit(solution)/shard_map/all_to_all | solution.py:723
  434.7 104.6 %reduce-scatter.5.cloned.1.call-start = ((), (), s32[]{:S(2)}) async-start(), calls=%async_computation.12 | async-start | bytes 10616832 | tf_op jit(solution)/shard_map/reduce_scatter | solution.py:797
  452.8 223.6 %reduce-scatter.9.cloned.1.call-start = ((), (), s32[]{:S(2)}) async-start(), calls=%async_computation.14 | async-start | bytes 5308416 | tf_op jit(solution)/shard_map/reduce_scatter | solution.py:825
  482.7 51.8 %collective-permute-start.55 = (bf16[512,1536]{1,0:T(8,128)(2,1)}, bf16[512,1536]{1,0:T(8,128)(2,1)}, u32[]{:S(2)}, u32[]{:S(2)}) collective-permute-start(bf16[512,1536]{1,0:T(8,128)(2,1)} %shard_map.315.refs_8_.refs_0_), channel_id=1, source_target_pairs={{1,2},{2,1},{5,6},{6,5},{9,10},{10,9},{13,14},{14,13},{17,18},{18,... | collective-permute-start | bytes 4718600 | tf_op jit(solution)/shard_map/ppermute | solution.py:467
  523.2 47.9 %collective-permute-start.56 = (bf16[8,192,640]{2,1,0:T(8,128)(2,1)}, bf16[8,192,640]{2,1,0:T(8,128)(2,1)}, u32[]{:S(2)}, u32[]{:S(2)}) collective-permute-start(bf16[8,192,640]{2,1,0:T(8,128)(2,1)} %get-tuple-element.762.refs_0_), channel_id=1, source_target_pairs={{0,1},{3,2},{4,5},{7,6},{8,9},{11,10},{12,13},{15,14},{16,17},{19,... | collective-permute-start | bytes 5898248 | tf_op jit(solution)/shard_map/ppermute | solution.py:463
  531.3 95.8 %collective-permute-start.58 = (bf16[640,1536]{1,0:T(8,128)(2,1)}, bf16[640,1536]{1,0:T(8,128)(2,1)}, u32[]{:S(2)}, u32[]{:S(2)}) collective-permute-start(bf16[640,1536]{1,0:T(8,128)(2,1)} %shard_map.317.refs_0_), channel_id=1, source_target_pairs={{1,2},{2,1},{5,6},{6,5},{9,10},{10,9},{13,14},{14,13},{17,18},{18,... | collective-permute-start | bytes 5898248 | tf_op jit(solution)/shard_map/ppermute | solution.py:467
  533.2 123.1 %collective-permute-start.65 = (bf16[8,192,512]{2,1,0:T(8,128)(2,1)}, bf16[8,192,512]{2,1,0:T(8,128)(2,1)}, u32[]{:S(2)}, u32[]{:S(2)}) collective-permute-start(bf16[8,192,512]{2,1,0:T(8,128)(2,1)} %all-to-all-done.3.refs_3_.refs_1_), channel_id=1, source_target_pairs={{1,0},{2,3},{5,4},{6,7},{9,8},{10,11},{13,12},{14,15},{17,16},{18,... | collective-permute-start | bytes 4718600 | tf_op jit(solution)/shard_map/ppermute | solution.py:471
  538.0 161.8 %collective-permute-start.61 = (bf16[512,1536]{1,0:T(8,128)(2,1)}, bf16[512,1536]{1,0:T(8,128)(2,1)}, u32[]{:S(2)}, u32[]{:S(2)}) collective-permute-start(bf16[512,1536]{1,0:T(8,128)(2,1)} %shard_map.319.refs_1_), channel_id=1, source_target_pairs={{1,0},{2,3},{5,4},{6,7},{9,8},{10,11},{13,12},{14,15},{17,16},{18,... | collective-permute-start | bytes 4718600 | tf_op jit(solution)/shard_map/ppermute | solution.py:471
  575.8 57.7 %all-to-all-start.4 = ((bf16[4,384,512]{2,1,0:T(8,128)(2,1)}), bf16[4,384,512]{2,1,0:T(8,128)(2,1)}, u32[]{:S(2)}, u32[]{:S(2)}) async-start(bf16[4,384,512]{2,1,0:T(8,128)(2,1)} %pad_maximum_fusion.4), calls=%async_computation.5 | async-start | bytes 3145728 | tf_op jit(solution)/shard_map/all_to_all | solution.py:817
  580.2 138.0 %reduce-scatter.7.cloned.1.call-start = ((), (), s32[]{:S(2)}) async-start(), calls=%async_computation.13 | async-start | bytes 5308416 | tf_op jit(solution)/shard_map/reduce_scatter | solution.py:825
  580.2 76.1 %collective-permute-start.64 = (bf16[8,192,640]{2,1,0:T(8,128)(2,1)}, bf16[8,192,640]{2,1,0:T(8,128)(2,1)}, u32[]{:S(2)}, u32[]{:S(2)}) collective-permute-start(bf16[8,192,640]{2,1,0:T(8,128)(2,1)} %bitcast.30), channel_id=1, source_target_pairs={{1,2},{2,1},{5,6},{6,5},{9,10},{10,9},{13,14},{14,13},{17,18},{18,... | collective-permute-start | bytes 5898248 | tf_op jit(solution)/shard_map/ppermute | solution.py:467
  598.9 51.2 %collective-permute-start.59 = (bf16[8,192,640]{2,1,0:T(8,128)(2,1)}, bf16[8,192,640]{2,1,0:T(8,128)(2,1)}, u32[]{:S(2)}, u32[]{:S(2)}) collective-permute-start(bf16[8,192,640]{2,1,0:T(8,128)(2,1)} %get-tuple-element.770.refs_0_), channel_id=1, source_target_pairs={{0,1},{3,2},{4,5},{7,6},{8,9},{11,10},{12,13},{15,14},{16,17},{19,... | collective-permute-start | bytes 5898248 | tf_op jit(solution)/shard_map/ppermute | solution.py:463
  632.3 67.6 %collective-permute-start.62 = (bf16[640,1536]{1,0:T(8,128)(2,1)}, bf16[640,1536]{1,0:T(8,128)(2,1)}, u32[]{:S(2)}, u32[]{:S(2)}) collective-permute-start(bf16[640,1536]{1,0:T(8,128)(2,1)} %shard_map.325.refs_3_), channel_id=1, source_target_pairs={{1,0},{2,3},{5,4},{6,7},{9,8},{10,11},{13,12},{14,15},{17,16},{18,... | collective-permute-start | bytes 5898248 | tf_op jit(solution)/shard_map/ppermute | solution.py:471
  654.4 52.0 %collective-permute-start.60 = (bf16[8,192,640]{2,1,0:T(8,128)(2,1)}, bf16[8,192,640]{2,1,0:T(8,128)(2,1)}, u32[]{:S(2)}, u32[]{:S(2)}) collective-permute-start(bf16[8,192,640]{2,1,0:T(8,128)(2,1)} %bitcast.28.refs_2_), channel_id=1, source_target_pairs={{1,2},{2,1},{5,6},{6,5},{9,10},{10,9},{13,14},{14,13},{17,18},{18,... | collective-permute-start | bytes 5898248 | tf_op jit(solution)/shard_map/ppermute | solution.py:467
  664.5 99.3 %reduce-scatter.11.cloned.1.call-start = ((), (), s32[]{:S(2)}) async-start(), calls=%async_computation.15 | async-start | bytes 2064384 | tf_op jit(solution)/shard_map/reduce_scatter | solution.py:825
  694.6 50.0 %collective-permute-start.67 = (bf16[8,192,640]{2,1,0:T(8,128)(2,1)}, bf16[8,192,640]{2,1,0:T(8,128)(2,1)}, u32[]{:S(2)}, u32[]{:S(2)}) collective-permute-start(bf16[8,192,640]{2,1,0:T(8,128)(2,1)} %all-to-all-done.5.refs_6_.refs_3_), channel_id=1, source_target_pairs={{1,0},{2,3},{5,4},{6,7},{9,8},{10,11},{13,12},{14,15},{17,16},{18,... | collective-permute-start | bytes 5898248 | tf_op jit(solution)/shard_map/ppermute | solution.py:471
  712.9 57.7 %all-to-all-start.6 = ((bf16[8,192,640]{2,1,0:T(8,128)(2,1)}), bf16[8,192,640]{2,1,0:T(8,128)(2,1)}, u32[]{:S(2)}, u32[]{:S(2)}) async-start(bf16[8,192,640]{2,1,0:T(8,128)(2,1)} %bitcast.33.refs_1_), calls=%async_computation.10 | async-start | bytes 3932160 | tf_op jit(solution)/shard_map/all_to_all | solution.py:723
  779.1 62.9 %collective-permute-start.75 = (bf16[8,192,640]{2,1,0:T(8,128)(2,1)}, bf16[8,192,640]{2,1,0:T(8,128)(2,1)}, u32[]{:S(2)}, u32[]{:S(2)}) collective-permute-start(bf16[8,192,640]{2,1,0:T(8,128)(2,1)} %all-to-all-done.6.refs_3_), channel_id=1, source_target_pairs={{1,0},{2,3},{5,4},{6,7},{9,8},{10,11},{13,12},{14,15},{17,16},{18,... | collective-permute-start | bytes 5898248 | tf_op jit(solution)/shard_map/ppermute | solution.py:471
  782.9 70.5 %collective-permute-start.74 = (bf16[224,512]{1,0:T(8,128)(2,1)}, bf16[224,512]{1,0:T(8,128)(2,1)}, u32[]{:S(2)}, u32[]{:S(2)}) collective-permute-start(bf16[224,512]{1,0:T(8,128)(2,1)} %shard_map.341.refs_3_.refs_1_), channel_id=1, source_target_pairs={{1,0},{2,3},{5,4},{6,7},{9,8},{10,11},{13,12},{14,15},{17,16},{18,... | collective-permute-start | bytes 688136 | tf_op jit(solution)/shard_map/ppermute | solution.py:471
  (149 other events, 1618.7 us)
Sparse Core Ops, SparseCore 0:
  48.3 37.9 all-gather.1
  452.9 78.7 reduce-scatter.4
  548.9 56.2 reduce-scatter.8
  627.2 65.1 reduce-scatter.6
  695.6 53.5 reduce-scatter.10
